TPU v7x, 32 devices: a whole 2x2x4 slice. The times are simulated.
32 devices in a mesh: branch: 2 (over core), pts: 16 (over z, y, x).
Axes of the slice: x: 2, y: 2, z: 4, core: 2. Of those that a mesh axis runs over, the one named last changes fastest.
Arguments:
- tokens: bfloat16 [32768, 128], P('pts'), may hold values from -6 to 6
- funcs: float32 [2, 3, 65536], P('branch', None, 'pts'), may hold values from -6 to 6
- item_counts: int32 [4], replicated, may hold values from 1 to 16384, 32768 in all
- func_counts: int32 [2, 4], P('branch'), may hold values from 1 to 32768, as said below
- gate_ints: int32 [32768, 4], P('pts'), may hold values from 2 to 8
- cotangent: float32 [32768, 128], P('pts'), may hold values from -6 to 6
- shared_master: float32 [297088], P('pts')
- shared_m: float32 [297088], P('pts'), may hold values from -7.964851 to 7.964851
- shared_v: float32 [297088], P('pts'), may hold values from 0.32768 to 1.31072
- branch_master: float32 [2, 49792], P('branch', 'pts')
- branch_m: float32 [2, 49792], P('branch', 'pts'), may hold values from -7.964851 to 7.964851
- branch_v: float32 [2, 49792], P('branch', 'pts'), may hold values from 0.32768 to 1.31072
Outputs:
- output: bfloat16 [32768, 128], P('pts')
- token_grad: float32 [32768, 128], P('pts')
- new_shared: float32 [297088], P('pts')
- new_shared_m: float32 [297088], P('pts')
- new_shared_v: float32 [297088], P('pts')
- new_branch: float32 [2, 49792], P('branch', 'pts')
- new_branch_m: float32 [2, 49792], P('branch', 'pts')
- new_branch_v: float32 [2, 49792], P('branch', 'pts')
Inputs may be any that keep to these rules, and one draw needn't show every extreme that they name: `func_counts`: row b sums to 65536 // (b + 1); sample slots past that sum are padding of no item; one item of function 0 holds exactly the largest count.
All inputs are finite; a program needn't handle non-finite values.
Results may differ from a plain program's by a relative error of at most 0.0085.
The roundings to bfloat16 on the way count: a program that leaves them out, or rounds other values in their place, can miss the bound.
Values may be sent and summed in bfloat16 or wider, within the bound.
No kernel may reach another device: no remote copies, remote signals or barrier semaphores. Data moves between devices by JAX's collectives and lax.ppermute only.
A program may use at most 128 MiB of HBM per device.

v0:
```python
import math

import jax
import jax.numpy as jnp
from jax import lax
from jax.sharding import PartitionSpec as P

D = 128
H = 8
HD = 16
FF = 256
E = 4
FIN = 3
STEP = 10


EPS_NORM = 1e-05
BETA_ONE = 0.9
BETA_TWO = 0.999
RATE_LEARN = 0.1
DECAY_RATE = 0.01
EPS_ADAM = 1e-08
precise = lax.Precision.HIGHEST


def shared_layout():
    return [(D,), (D,), (D, D), (D, D), (D,), (D,), (D,), (E, D, FF), (E, FF), (E, FF, D), (E, D)]


def branch_layout():
    return [(FIN, D), (D,), (D, D), (D,), (D, 2 * D)]


def unpack(vector, layout):
    pieces = []
    offset = 0
    for dims in layout:
        amount = math.prod(dims)
        pieces.append(vector[offset : offset + amount].reshape(dims))
        offset += amount
    return pieces


def pack_vector(pieces, length):
    flat = jnp.concatenate([piece.reshape(-1) for piece in pieces])
    return jnp.concatenate([flat, jnp.zeros((length - flat.shape[0],), jnp.float32)])


def product(left, right):
    return jnp.dot(left, right, preferred_element_type=jnp.float32)


def left_product(left, right):
    return lax.dot_general(
        left, right, (((0,), (0,)), ((), ())), preferred_element_type=jnp.float32
    )


def right_product(left, right):
    return lax.dot_general(
        left, right, (((1,), (1,)), ((), ())), preferred_element_type=jnp.float32
    )


def exact_product(left, right):
    return jnp.dot(left, right, precision=precise, preferred_element_type=jnp.float32)


def gelu_grad(inner, grad):
    return jax.vjp(jax.nn.gelu, inner)[1](grad)[0]


def column_sum(values):
    return jnp.sum(values.astype(jnp.float32), axis=0)


def norm_forward(values, norm_gain, norm_shift):
    centre = values - jnp.mean(values, axis=-1, keepdims=True)
    scale = lax.rsqrt(jnp.mean(centre * centre, axis=-1, keepdims=True) + EPS_NORM)
    unit = centre * scale
    return (unit * norm_gain + norm_shift, unit, scale)


def norm_backward(grad_normed, unit, scale, norm_gain):
    grad_unit = grad_normed * norm_gain
    return scale * (
        grad_unit
        - jnp.mean(grad_unit, axis=-1, keepdims=True)
        - unit * jnp.mean(grad_unit * unit, axis=-1, keepdims=True)
    )


def segment_table(counts, first, length):
    item_ends = jnp.cumsum(counts)
    item_starts = item_ends - counts
    position = first + jnp.arange(length, dtype=jnp.int32)[:, None]
    return ((position >= item_starts[None, :]) & (position < item_ends[None, :])).astype(
        jnp.float32
    )


def adam_step(master, moment_one, moment_two, grad):
    first = BETA_ONE * moment_one + (1.0 - BETA_ONE) * grad
    second = BETA_TWO * moment_two + (1.0 - BETA_TWO) * grad * grad
    first_hat = first / (1.0 - BETA_ONE**STEP)
    second_hat = second / (1.0 - BETA_TWO**STEP)
    fresh = master - RATE_LEARN * (
        first_hat / (jnp.sqrt(second_hat) + EPS_ADAM) + DECAY_RATE * master
    )
    return (fresh, first, second)


def tail_pass(attended, token_rows, gate_rows, grad_rows, params):
    output_w, output_b, gain_two, shift_two, expert_up, expert_up_b, expert_down, expert_down_b = (
        params
    )
    attended_low = attended.astype(jnp.bfloat16)
    residual = token_rows + product(attended_low, output_w) + output_b.astype(jnp.float32)
    normed, unit, scale = norm_forward(
        residual, gain_two.astype(jnp.float32), shift_two.astype(jnp.float32)
    )
    normed_low = normed.astype(jnp.bfloat16)
    mixture = jnp.zeros_like(residual)
    grad_normed = jnp.zeros_like(residual)
    up_grads, up_bias_grads, down_grads, down_bias_grads = ([], [], [], [])
    for expert_no in range(expert_up.shape[0]):
        inner = product(normed_low, expert_up[expert_no]) + expert_up_b[expert_no].astype(
            jnp.float32
        )
        active = jax.nn.gelu(inner).astype(jnp.bfloat16)
        result = product(active, expert_down[expert_no]) + expert_down_b[expert_no].astype(
            jnp.float32
        )
        weight_col = gate_rows[:, expert_no : expert_no + 1]
        mixture = mixture + weight_col * result
        grad_result = (weight_col * grad_rows).astype(jnp.bfloat16)
        down_grads.append(left_product(active, grad_result))
        down_bias_grads.append(column_sum(grad_result))
        grad_inner = gelu_grad(inner, right_product(grad_result, expert_down[expert_no])).astype(
            jnp.bfloat16
        )
        up_grads.append(left_product(normed_low, grad_inner))
        up_bias_grads.append(column_sum(grad_inner))
        grad_normed = grad_normed + right_product(grad_inner, expert_up[expert_no])
    output = (residual + mixture).astype(jnp.bfloat16)
    gain_grad = jnp.sum(grad_normed * unit, axis=0)
    shift_grad = jnp.sum(grad_normed, axis=0)
    grad_residual = grad_rows + norm_backward(
        grad_normed, unit, scale, gain_two.astype(jnp.float32)
    )
    grad_proj = grad_residual.astype(jnp.bfloat16)
    grads = [
        left_product(attended_low, grad_proj),
        column_sum(grad_proj),
        gain_grad,
        shift_grad,
        jnp.stack(up_grads),
        jnp.stack(up_bias_grads),
        jnp.stack(down_grads),
        jnp.stack(down_bias_grads),
    ]
    grad_attended = right_product(grad_proj, output_w)
    return (output, grad_residual, grad_attended, grads)


def body(
    tokens,
    funcs,
    item_counts,
    func_counts,
    gate_ints,
    cotangent,
    shared_master,
    shared_m,
    shared_v,
    branch_master,
    branch_m,
    branch_v,
):
    branch_count = lax.axis_size("branch")
    point_count = lax.axis_size("pts")
    point_at = lax.axis_index("pts")
    local_rows = tokens.shape[0]
    local_samples = funcs.shape[2]
    item_total = item_counts.shape[0]
    shared_full, branch_full = (
        lax.all_gather(shared_master.astype(jnp.bfloat16), "pts", axis=0, tiled=True),
        lax.all_gather(branch_master.reshape(-1).astype(jnp.bfloat16), "pts", axis=0, tiled=True),
    )
    (
        gain_one,
        shift_one,
        query_w,
        output_w,
        output_b,
        gain_two,
        shift_two,
        expert_up,
        expert_up_b,
        expert_down,
        expert_down_b,
    ) = unpack(shared_full, shared_layout())
    input_w, input_b, hidden_w, hidden_b, pair_w = unpack(branch_full, branch_layout())
    point_hot = segment_table(item_counts, point_at * local_rows, local_rows)
    sample_hot = segment_table(func_counts[0], point_at * local_samples, local_samples)
    samples = funcs[0]
    first_in = lax.dot_general(
        samples,
        input_w.astype(jnp.float32),
        (((0,), (0,)), ((), ())),
        precision=precise,
        preferred_element_type=jnp.float32,
    ) + input_b.astype(jnp.float32)
    first = jax.nn.gelu(first_in).astype(jnp.bfloat16)
    second_in = product(first, hidden_w) + hidden_b.astype(jnp.float32)
    second = jax.nn.gelu(second_in).astype(jnp.bfloat16)
    pair = product(second, pair_w)
    key_soft = jax.nn.softmax(pair[:, :D].reshape(-1, H, HD), axis=-1)
    keys = key_soft.astype(jnp.bfloat16)
    values = pair[:, D:].astype(jnp.bfloat16).reshape(-1, H, HD)
    hot_low = sample_hot.astype(jnp.bfloat16)
    weighted = hot_low[:, :, None, None] * keys[:, None]
    summary_part = jnp.einsum(
        "jiha,jhc->ihac", weighted, values, preferred_element_type=jnp.float32
    )
    totals_part = left_product(hot_low, keys.reshape(-1, D)).reshape(item_total, H, HD)
    summary, totals = lax.psum((summary_part, totals_part), "pts")
    token_f = tokens.astype(jnp.float32)
    normed, unit_one, scale_one = norm_forward(
        token_f, gain_one.astype(jnp.float32), shift_one.astype(jnp.float32)
    )
    normed_low = normed.astype(jnp.bfloat16)
    query = product(normed_low, query_w)
    query_soft = jax.nn.softmax(query.reshape(-1, H, HD), axis=-1)
    query_vals = query_soft.astype(jnp.bfloat16).astype(jnp.float32)
    spread_q = point_hot[:, :, None, None] * query_vals[:, None]
    numer = jnp.einsum("tiha,ihac->thc", spread_q, summary, precision=precise)
    denom = jnp.einsum("tiha,iha->th", spread_q, totals, precision=precise)
    own_att = (numer / denom[:, :, None]).reshape(local_rows, D)
    gate_vals = gate_ints.astype(jnp.float32)
    gates = gate_vals / jnp.sum(gate_vals, axis=1, keepdims=True)
    tail_params = (
        output_w,
        output_b,
        gain_two,
        shift_two,
        expert_up,
        expert_up_b,
        expert_down,
        expert_down_b,
    )
    attended = lax.psum(own_att, "branch") / branch_count
    output, grad_residual, grad_attended, tail_grads = tail_pass(
        attended, token_f, gates, cotangent, tail_params
    )
    query_scale = 1.0
    grad_own = grad_attended.reshape(-1, H, HD) / branch_count
    grad_numer = grad_own / denom[:, :, None]
    grad_denom = -jnp.sum(grad_own * numer, axis=-1) / (denom * denom)
    spread_g = point_hot[:, :, None, None] * grad_numer[:, None]
    totals_rows = jnp.einsum("ti,iha->tha", point_hot, totals, precision=precise)
    query_grad_part = (
        jnp.einsum("tihc,ihac->tha", spread_g, summary, precision=precise)
        + grad_denom[:, :, None] * totals_rows
    )
    summary_grad_part = jnp.einsum("tiha,thc->ihac", spread_q, grad_numer, precision=precise)
    totals_grad_part = jnp.einsum("tiha,th->iha", spread_q, grad_denom, precision=precise)
    summary_grad, totals_grad = lax.psum((summary_grad_part, totals_grad_part), "pts")
    grad_qs = lax.psum(query_grad_part.astype(jnp.bfloat16), "branch").astype(jnp.float32)
    grad_q = (
        (query_soft * (grad_qs - jnp.sum(grad_qs * query_soft, axis=-1, keepdims=True)))
        .reshape(-1, D)
        .astype(jnp.bfloat16)
    )
    query_w_grad = left_product(normed_low, grad_q)
    grad_normed_one = right_product(grad_q, query_w)
    gain_one_grad = jnp.sum(grad_normed_one * unit_one, axis=0)
    shift_one_grad = jnp.sum(grad_normed_one, axis=0)
    token_grad = grad_residual + norm_backward(
        grad_normed_one, unit_one, scale_one, gain_one.astype(jnp.float32)
    )
    sample_summary = exact_product(sample_hot, summary_grad.reshape(item_total, -1)).reshape(
        -1, H, HD, HD
    )
    sample_totals = exact_product(sample_hot, totals_grad.reshape(item_total, -1)).reshape(
        -1, H, HD
    )
    grad_keys = (
        jnp.einsum("jhac,jhc->jha", sample_summary, values.astype(jnp.float32), precision=precise)
        + sample_totals
    )
    grad_values = jnp.einsum(
        "jhac,jha->jhc", sample_summary, keys.astype(jnp.float32), precision=precise
    )
    grad_key_in = key_soft * (grad_keys - jnp.sum(grad_keys * key_soft, axis=-1, keepdims=True))
    grad_pair = jnp.concatenate(
        [grad_key_in.reshape(-1, D), grad_values.reshape(-1, D)], axis=1
    ).astype(jnp.bfloat16)
    pair_w_grad = left_product(second, grad_pair)
    grad_second_in = gelu_grad(second_in, right_product(grad_pair, pair_w)).astype(jnp.bfloat16)
    hidden_w_grad = left_product(first, grad_second_in)
    hidden_b_grad = column_sum(grad_second_in)
    grad_first_in = gelu_grad(first_in, right_product(grad_second_in, hidden_w))
    input_w_grad = jnp.dot(
        samples, grad_first_in, precision=precise, preferred_element_type=jnp.float32
    )
    input_b_grad = jnp.sum(grad_first_in, axis=0)
    shard_len = shared_master.shape[0]
    branch_len = branch_master.shape[1]
    head_grads = [
        gain_one_grad * query_scale,
        shift_one_grad * query_scale,
        query_w_grad * query_scale,
    ]
    shared_grad = pack_vector(head_grads + tail_grads, shard_len * point_count)
    branch_grad = pack_vector(
        [input_w_grad, input_b_grad, hidden_w_grad, hidden_b_grad, pair_w_grad],
        branch_len * point_count,
    )
    shared_sum, branch_sum = lax.psum((shared_grad, branch_grad), "pts")
    shared_part = lax.dynamic_slice_in_dim(shared_sum, point_at * shard_len, shard_len, 0)
    branch_part = lax.dynamic_slice_in_dim(branch_sum, point_at * branch_len, branch_len, 0)
    new_shared, new_shared_m, new_shared_v = adam_step(
        shared_master, shared_m, shared_v, shared_part
    )
    new_branch, new_branch_m, new_branch_v = adam_step(
        branch_master, branch_m, branch_v, branch_part.reshape(1, -1)
    )
    return (
        output,
        token_grad,
        new_shared,
        new_shared_m,
        new_shared_v,
        new_branch,
        new_branch_m,
        new_branch_v,
    )


def solution(mesh):
    in_specs = (
        P("pts", None),
        P("branch", None, "pts"),
        P(),
        P("branch", None),
        P("pts", None),
        P("pts", None),
        P("pts"),
        P("pts"),
        P("pts"),
        P("branch", "pts"),
        P("branch", "pts"),
        P("branch", "pts"),
    )
    out_specs = (
        P("pts", None),
        P("pts", None),
        P("pts"),
        P("pts"),
        P("pts"),
        P("branch", "pts"),
        P("branch", "pts"),
        P("branch", "pts"),
    )
    return jax.shard_map(body, mesh=mesh, in_specs=in_specs, out_specs=out_specs, check_vma=False)
```

profile of v0, /device:TPU:0, one launch (start us, length us, event | category | flops | bytes accessed | tf_op | source)
XLA Modules:
  0.0 622.6 jit_solution(18083307079090274006)
XLA Ops:
  9.0 1.2 dynamic-slice
  14.7 1.2 copy.46
  17.2 1.9 convert_reduce_fusion.6
  19.8 107.0 %all-reduce.17.cloned.1.call-done = (bf16[297088]{0:T(1024)(128)(2,1)}, bf16[49792]{0:T(1024)(128)(2,1)}) async-done(((bf16[297088]{0:T(1024)(128)(2,1)}, bf16[49792]{0:T(1024)(128)(2,1)}), (bf16[297088]{0:T(1024)(128)(2,1)}, bf16[49792]{0:T(1024)(128)(2,1)})) %all-reduce.17.cloned.1.call-update) | async-done | bytes 693776
  130.9 1.3 copy-done.8
  133.2 1.9 bitcast_convert_fusion
  136.0 2.1 fusion.185
  138.7 1.4 slice_convert_fusion.1
  140.1 1.5 fusion.187
  141.6 1.3 fusion.148
  143.7 6.2 fusion.115
  149.9 78.7 %all-reduce.3 = (f32[4,8,16,16]{2,3,0,1:T(8,128)S(1)}, f32[4,8,16]{2,0,1:T(4,128)S(1)}) all-reduce(f32[4,8,16,16]{2,3,0,1:T(8,128)S(1)} %fusion.115, f32[4,8,16]{2,0,1:T(4,128)S(1)} %fusion.148), channel_id=1, replica_groups=mesh['branch'=2,'pts'=16] {'pts'}, use_global_device_ids=true, to_apply=%region_3.4 | all-reduce | flops 8704 | bytes 69632 | tf_op jit(solution)/shard_map/psum | solution.py:227
  228.7 2.3 convert_convert_fusion
  231.0 2.4 fusion.8
  234.0 5.8 broadcast_divide_fusion.1
  240.3 15.5 %all-reduce.11.cloned.1.call-done = f32[2048,128]{0,1:T(8,128)} async-done(((f32[2048,128]{0,1:T(8,128)}), f32[2048,128]{0,1:T(8,128)}) %all-reduce.11.cloned.1.call-update) | async-done | bytes 1048592 | tf_op jit(solution)/shard_map/psum | solution.py:252
  255.8 1.6 fusion.192
  258.3 2.2 convert_reduce_fusion.4
  262.0 3.1 convert_reduce_fusion.1
  265.1 1.5 convolution_bitcast_fusion.3
  267.7 3.2 convert_reduce_fusion.2
  270.8 1.5 convolution_bitcast_fusion.4
  273.4 3.2 convert_reduce_fusion.3
  276.6 1.9 convolution_bitcast_fusion.5
  278.5 1.5 convolution_bitcast_fusion.6
  283.9 1.2 multiply_reduce_fusion.3
  287.4 3.2 fusion.23
  290.6 14.8 %fusion.112 = f32[4,8,16,16]{2,3,0,1:T(8,128)S(1)} fusion(f32[2048,8,16]{0,2,1:T(8,128)S(1)} %copy-done.22, f32[2048,4]{0,1:T(4,128)S(1)} %copy-done.35, f32[2048,8,16]{0,2,1:T(8,128)S(1)} %get-tuple-element.60), kind=kOutput, calls=%fused_computation.163 | convolution fusion | flops 202375168 | bytes 2162688 | tf_op jit(solution)/shard_map/tiha,thc->ihac/dot_general | solution.py:266
  306.8 16.1 %fusion.4 = f32[8,1,4,16]{3,1,2,0:T(1,128)S(1)} fusion(f32[2048,8,16]{0,2,1:T(8,128)} %copy-done.21, f32[2048,4]{0,1:T(4,128)} %copy-done.34, f32[2048,8,1,1]{0,1,2,3:T(8,128)} %bitcast.314), kind=kOutput, calls=%fused_computation.6 | convolution fusion | flops 13631488 | bytes 1148928 | tf_op jit(solution)/shard_map/tiha,th->iha/dot_general | solution.py:267
  323.7 80.5 %all-reduce.2 = (f32[8,16,16,4]{2,3,1,0:T(4,128)S(1)}, f32[8,16,4]{1,2,0:T(4,128)}) all-reduce(f32[8,16,16,4]{2,3,1,0:T(4,128)S(1)} %copy.68, f32[8,16,4]{1,2,0:T(4,128)} %copy.69), channel_id=1, replica_groups=mesh['branch'=2,'pts'=16] {'pts'}, use_global_device_ids=true, to_apply=%region_35.36 | all-reduce | flops 8704 | bytes 69632 | tf_op jit(solution)/shard_map/psum | solution.py:268
  404.1 19.8 %multiply_reduce_fusion = (bf16[4096,8,16]{0,2,1:T(8,128)(2,1)S(1)}, f32[4096,8,16,16]{0,3,2,1:T(8,128)}) fusion(f32[4096,8,16]{0,2,1:T(8,128)} %get-tuple-element.47, f32[8,16,16,4]{2,3,1,0:T(4,128)S(1)} %get-tuple-element.31, s32[4]{0:T(128)} %bitcast.332, s32[4]{0:T(128)} %copy-done.85, s32[4096]{0:T(1024)S(1)} %iota_add_fusion), kind=kOutput, calls=%fused_computation.4 | convolution fusion | flops 418955264 | bytes 36749344 | tf_op jit(solution)/shard_map/dot_general | solution.py:66
  424.0 14.2 %multiply_reduce_fusion.1 = f32[4096,8,16]{0,2,1:T(8,128)S(1)} fusion(f32[4096,8,16,16]{0,3,2,1:T(8,128)} %get-tuple-element.112, f32[4096,8,16]{0,2,1:T(8,128)S(1)} %copy-done.4), kind=kLoop, calls=%fused_computation.5 | loop fusion | flops 16252928 | bytes 37748736 | tf_op jit(solution)/shard_map/jhac,jhc->jha/dot_general | solution.py:289
  438.3 1.1 convolution_add_fusion
  442.1 2.3 convert_reduce_fusion
  444.4 3.0 fusion.194
  447.4 1.5 convolution_bitcast_fusion
  448.9 1.6 fusion.118
  450.6 2.8 fusion.40
  453.6 1.5 fusion.42
  455.6 1.1 copy-done.17
  456.7 1.7 convolution_bitcast_fusion.11
  460.7 2.8 fusion.39
  463.5 6.8 %all-reduce.13.cloned.1.call-done = bf16[2048,8,16]{0,2,1:T(8,128)(2,1)} async-done(((bf16[2048,8,16]{0,2,1:T(8,128)(2,1)}), bf16[2048,8,16]{0,2,1:T(8,128)(2,1)}) %all-reduce.13.cloned.1.call-update) | async-done | bytes 524304 | tf_op jit(solution)/shard_map/psum | solution.py:269
  470.2 2.2 fusion.43
  472.4 2.1 fusion.193
  474.9 2.5 copy.65
  477.5 1.9 fusion.125
  479.4 1.3 constant_dynamic-update-slice_fusion
  480.7 1.3 constant_dynamic-update-slice_fusion.11
  482.0 1.5 constant_dynamic-update-slice_fusion.10
  483.5 1.5 constant_dynamic-update-slice_fusion.9
  485.0 1.3 constant_dynamic-update-slice_fusion.8
  486.3 1.3 constant_dynamic-update-slice_fusion.7
  487.6 1.3 constant_dynamic-update-slice_fusion.6
  488.9 1.9 constant_dynamic-update-slice_fusion.5
  490.8 1.3 constant_dynamic-update-slice_fusion.4
  492.1 1.9 constant_dynamic-update-slice_fusion.3
  494.0 1.3 constant_dynamic-update-slice_fusion.2
  495.4 3.0 fusion.37
  498.4 1.9 fusion.41
  501.3 1.9 fusion.124
  503.2 1.3 copy.75
  504.5 107.9 %all-reduce.15.cloned.1.call-done = (f32[297088]{0:T(1024)}, f32[49792]{0:T(1024)}) async-done(((f32[297088]{0:T(1024)}, f32[49792]{0:T(1024)}), (f32[297088]{0:T(1024)}, f32[49792]{0:T(1024)})) %all-reduce.15.cloned.1.call-update) | async-done | bytes 1387536 | tf_op jit(solution)/shard_map/psum | solution.py:320
  613.2 1.7 multiply_subtract_fusion
  (328 shorter events, 35.7 us)
Async XLA Ops:
  7.2 9.1 %copy-start.113 = (s32[4]{0:T(128)S(1)}, s32[4]{0:T(128)}, u32[]{:S(2)}) copy-start(s32[4]{0:T(128)} %param.14) | copy-start | bytes 52
  7.2 9.3 %copy-start.48 = (s32[2048,4]{0,1:T(4,128)S(1)}, s32[2048,4]{0,1:T(4,128)}, u32[]{:S(2)}) copy-start(s32[2048,4]{0,1:T(4,128)} %param.16) | copy-start | bytes 98308
  7.2 9.4 %copy-start.23 = (f32[2048,128]{1,0:T(8,128)S(1)}, f32[2048,128]{1,0:T(8,128)}, u32[]{:S(2)}) copy-start(f32[2048,128]{1,0:T(8,128)} %param.17) | copy-start | bytes 3145732
  7.2 119.7 %all-reduce.17.cloned.1.call-start = ((), (), s32[]{:S(2)}) async-start(), calls=%async_computation.3 | async-start | bytes 1392640
  13.2 242.6 %all-reduce.11.cloned.1.call-start = ((), (), s32[]{:S(2)}) async-start(), calls=%async_computation | async-start | bytes 2097152 | tf_op jit(solution)/shard_map/psum | solution.py:252
  14.1 5.0 copy-start.82
  14.7 4.4 copy-start.85
  16.1 212.6 %copy-start.46 = (f32[2048]{0:T(1024)}, f32[2048]{0:T(1024)S(1)}, u32[]{:S(2)}) copy-start(f32[2048]{0:T(1024)S(1)} %broadcast_multiply_fusion.5) | copy-start | bytes 24580
  16.3 212.4 %copy-start.56 = (f32[2048]{0:T(1024)}, f32[2048]{0:T(1024)S(1)}, u32[]{:S(2)}) copy-start(f32[2048]{0:T(1024)S(1)} %add_rsqrt_fusion.1) | copy-start | bytes 24580
  17.0 112.5 %copy-start.2 = (f32[2048,128]{0,1:T(8,128)}, f32[2048,128]{0,1:T(8,128)S(1)}, u32[]{:S(2)}) copy-start(f32[2048,128]{0,1:T(8,128)S(1)} %copy.62) | copy-start | bytes 3145732
  17.0 111.5 %copy-start.31 = (f32[1,3,4096]{2,0,1:T(1,128)S(1)}, f32[1,3,4096]{2,0,1:T(1,128)}, u32[]{:S(2)}) copy-start(f32[1,3,4096]{2,0,1:T(1,128)} %param.13) | copy-start | bytes 147460
  17.1 216.8 %copy-start.34 = (f32[2048,4]{0,1:T(4,128)}, f32[2048,4]{0,1:T(4,128)S(1)}, u32[]{:S(2)}) copy-start(f32[2048,4]{0,1:T(4,128)S(1)} %fusion.172) | copy-start | bytes 98308
  133.2 5.0 copy-start
  138.2 3.4 copy-start.83
  138.2 3.4 copy-start.86
  138.2 5.5 copy-start.74
  143.7 85.0 %copy-start.75 = (bf16[128,128]{1,0:T(8,128)(2,1)S(1)}, bf16[128,128]{1,0:T(8,128)(2,1)}, u32[]{:S(2)}) copy-start(bf16[128,128]{1,0:T(8,128)(2,1)} %copy.48) | copy-start | bytes 98308
  228.6 5.3 copy-start.39
  231.0 8.8 %copy-start.21 = (f32[2048,8,16]{0,2,1:T(8,128)}, f32[2048,8,16]{0,2,1:T(8,128)S(1)}, u32[]{:S(2)}) copy-start(f32[2048,8,16]{0,2,1:T(8,128)S(1)} %get-tuple-element.94) | copy-start | bytes 3145732
  233.4 6.4 %copy-start.60 = (f32[8,1,2048,1]{2,0,1,3:T(8,128)}, f32[8,1,2048,1]{2,0,1,3:T(8,128)S(1)}, u32[]{:S(2)}) copy-start(f32[8,1,2048,1]{2,0,1,3:T(8,128)S(1)} %copy.132) | copy-start | bytes 196612
  234.0 6.1 copy-start.36
  239.7 16.1 %copy-start.96 = (f32[128]{0:T(128)S(1)}, f32[128]{0:T(128)}, u32[]{:S(2)}) copy-start(f32[128]{0:T(128)} %get-tuple-element.83) | copy-start | bytes 1540
  239.7 230.5 %all-reduce.13.cloned.1.call-start = ((), (), s32[]{:S(2)}) async-start(), calls=%async_computation.1 | async-start | bytes 1048576 | tf_op jit(solution)/shard_map/psum | solution.py:269
  240.1 17.4 %copy-start.88 = (f32[128]{0:T(128)S(1)}, f32[128]{0:T(128)}, u32[]{:S(2)}) copy-start(f32[128]{0:T(128)} %get-tuple-element.82) | copy-start | bytes 1540
  240.1 17.4 %copy-start.95 = (f32[128]{0:T(128)S(1)}, f32[128]{0:T(128)}, u32[]{:S(2)}) copy-start(f32[128]{0:T(128)} %get-tuple-element.81) | copy-start | bytes 1540
  258.3 20.2 %copy-start.15 = (f32[2048,256]{1,0:T(8,128)}, f32[2048,256]{1,0:T(8,128)S(1)}, u32[]{:S(2)}) copy-start(f32[2048,256]{1,0:T(8,128)S(1)} %convolution_add_fusion.6) | copy-start | bytes 6291460
  261.7 3.4 copy-start.10
  267.1 3.7 copy-start.12
  272.8 3.7 copy-start.13
  286.9 3.7 copy-start.22
  287.4 18.1 %copy-start.43 = (f32[8,1,2048,1]{2,1,3,0:T(1,128)S(1)}, f32[8,1,2048,1]{2,1,3,0:T(1,128)}, u32[]{:S(2)}) copy-start(f32[8,1,2048,1]{2,1,3,0:T(1,128)} %copy-done.42) | copy-start | bytes 196612
  404.1 19.9 %copy-start.4 = (f32[4096,8,16]{0,2,1:T(8,128)S(1)}, f32[4096,8,16]{0,2,1:T(8,128)}, u32[]{:S(2)}) copy-start(f32[4096,8,16]{0,2,1:T(8,128)} %get-tuple-element.45) | copy-start | bytes 6291460
  424.0 14.3 %copy-start.79 = (f32[8,16,4]{1,2,0:T(4,128)S(1)}, f32[8,16,4]{1,2,0:T(4,128)}, u32[]{:S(2)}) copy-start(f32[8,16,4]{1,2,0:T(4,128)} %get-tuple-element.32) | copy-start | bytes 6148
  424.0 14.2 %copy-start.84 = (s32[4,1]{0,1:T(1,128)S(1)}, s32[4,1]{0,1:T(1,128)}, u32[]{:S(2)}) copy-start(s32[4,1]{0,1:T(1,128)} %copy-done.82) | copy-start | bytes 52
  424.0 14.2 %copy-start.87 = (s32[4]{0:T(128)S(1)}, s32[4]{0:T(128)}, u32[]{:S(2)}) copy-start(s32[4]{0:T(128)} %copy-done.85) | copy-start | bytes 52
  455.0 157.4 %all-reduce.15.cloned.1.call-start = ((), (), s32[]{:S(2)}) async-start(), calls=%async_computation.2 | async-start | bytes 2785280 | tf_op jit(solution)/shard_map/psum | solution.py:320
  455.1 3.3 copy-start.49
  455.1 3.4 copy-start.44
  455.2 3.4 copy-start.62
  455.2 4.2 copy-start.50
  455.2 4.1 copy-start.51
  455.2 4.1 copy-start.52
  455.2 4.1 copy-start.53
  455.5 4.7 copy-start.6
  463.5 11.1 %copy-start.47 = (f32[2048]{0:T(1024)S(1)}, f32[2048]{0:T(1024)}, u32[]{:S(2)}) copy-start(f32[2048]{0:T(1024)} %copy-done.46) | copy-start | bytes 24580
  463.5 11.1 %copy-start.57 = (f32[2048]{0:T(1024)S(1)}, f32[2048]{0:T(1024)}, u32[]{:S(2)}) copy-start(f32[2048]{0:T(1024)} %copy-done.56) | copy-start | bytes 24580
  463.5 11.1 %copy-start.90 = (f32[128]{0:T(128)S(1)}, f32[128]{0:T(128)}, u32[]{:S(2)}) copy-start(f32[128]{0:T(128)} %get-tuple-element.85) | copy-start | bytes 1540
  463.5 11.1 %copy-start.110 = (f32[128]{0:T(128)S(1)}, f32[128]{0:T(128)}, u32[]{:S(2)}) copy-start(f32[128]{0:T(128)} %get-tuple-element.84) | copy-start | bytes 1540
  474.9 10.1 %copy-start.107 = (f32[128]{0:T(128)S(1)}, f32[128]{0:T(128)}, u32[]{:S(2)}) copy-start(f32[128]{0:T(128)} %get-tuple-element.57) | copy-start | bytes 1540
  474.9 11.4 %copy-start.106 = (f32[128]{0:T(128)S(1)}, f32[128]{0:T(128)}, u32[]{:S(2)}) copy-start(f32[128]{0:T(128)} %get-tuple-element.24) | copy-start | bytes 1540
  474.9 12.7 %copy-start.105 = (f32[128]{0:T(128)S(1)}, f32[128]{0:T(128)}, u32[]{:S(2)}) copy-start(f32[128]{0:T(128)} %get-tuple-element.30) | copy-start | bytes 1540
  477.5 14.6 %copy-start.20 = (f32[4,256,128]{2,1,0:T(8,128)S(1)}, f32[4,256,128]{2,1,0:T(8,128)}, u32[]{:S(2)}) copy-start(f32[4,256,128]{2,1,0:T(8,128)} %pad_maximum_fusion.8) | copy-start | bytes 1572868
  477.5 16.5 %copy-start.97 = (f32[128]{0:T(128)S(1)}, f32[128]{0:T(128)}, u32[]{:S(2)}) copy-start(f32[128]{0:T(128)} %get-tuple-element.55) | copy-start | bytes 1540
  477.5 16.5 %copy-start.98 = (f32[128]{0:T(128)S(1)}, f32[128]{0:T(128)}, u32[]{:S(2)}) copy-start(f32[128]{0:T(128)} %get-tuple-element.61) | copy-start | bytes 1540
  477.5 16.5 %copy-start.99 = (f32[128]{0:T(128)S(1)}, f32[128]{0:T(128)}, u32[]{:S(2)}) copy-start(f32[128]{0:T(128)} %get-tuple-element.63) | copy-start | bytes 1540
  477.5 16.5 %copy-start.100 = (f32[128]{0:T(128)S(1)}, f32[128]{0:T(128)}, u32[]{:S(2)}) copy-start(f32[128]{0:T(128)} %get-tuple-element.65) | copy-start | bytes 1540
  479.4 16.0 %copy-start.67 = (f32[2048,1]{0,1:T(1,128)S(1)}, f32[2048,1]{0,1:T(1,128)}, u32[]{:S(2)}) copy-start(f32[2048,1]{0,1:T(1,128)} %copy-done.66) | copy-start | bytes 24580
  479.4 16.0 %copy-start.109 = (f32[128]{0:T(128)S(1)}, f32[128]{0:T(128)}, u32[]{:S(2)}) copy-start(f32[128]{0:T(128)} %get-tuple-element.78) | copy-start | bytes 1540
  501.3 112.0 %copy-start.33 = (f32[18568]{0:T(1024)S(1)}, f32[18568]{0:T(1024)}, u32[]{:S(2)}) copy-start(f32[18568]{0:T(1024)} %param.18) | copy-start | bytes 222820
  501.3 112.0 %copy-start.54 = (f32[18568]{0:T(1024)S(1)}, f32[18568]{0:T(1024)}, u32[]{:S(2)}) copy-start(f32[18568]{0:T(1024)} %param.19) | copy-start | bytes 222820
  501.3 112.0 %copy-start.55 = (f32[18568]{0:T(1024)S(1)}, f32[18568]{0:T(1024)}, u32[]{:S(2)}) copy-start(f32[18568]{0:T(1024)} %param.20) | copy-start | bytes 222820
  503.2 111.8 %copy-start.63 = (f32[1,3112]{1,0:T(1,128)S(1)}, f32[1,3112]{1,0:T(1,128)}, u32[]{:S(2)}) copy-start(f32[1,3112]{1,0:T(1,128)} %param.21) | copy-start | bytes 37348
  503.2 111.8 %copy-start.80 = (f32[1,3112]{1,0:T(1,128)S(1)}, f32[1,3112]{1,0:T(1,128)}, u32[]{:S(2)}) copy-start(f32[1,3112]{1,0:T(1,128)} %param.22) | copy-start | bytes 37348
  503.2 111.8 %copy-start.81 = (f32[1,3112]{1,0:T(1,128)S(1)}, f32[1,3112]{1,0:T(1,128)}, u32[]{:S(2)}) copy-start(f32[1,3112]{1,0:T(1,128)} %param.23) | copy-start | bytes 37348
  (56 other events, 100.7 us)
Sparse Core Ops, SparseCore 0:
  14.0 112.7 all-reduce.16
  239.9 15.8 all-reduce.10
  455.2 15.0 all-reduce.12
  495.5 116.9 all-reduce.14
where the time goes:
time: 633 us; the launch traced here: 623 us
  waiting for transfers between devices  237 us (37%)
  blocking collectives  159 us (25%)
  matrix products  129 us (20%)
  other arithmetic  41.8 us (7%)
  local copies, waits for them, and re-layouts  38.1 us (6%)
  between operations  17.1 us (3%)
    psum x1, waiting for transfers between devices, body(): shared_sum, branch_sum = lax.psum((shared_grad, branch_grad), 'pts')  108 us
    unnamed x5, waiting for transfers between devices  107 us
    psum x1, blocking collectives, body(): lax.psum((summary_grad_part, totals_grad_part), 'pts')  80.5 us
    psum x1, blocking collectives, body(): summary, totals = lax.psum((summary_part, totals_part), 'pts')  78.7 us
    unnamed x259, local copies, waits for them, and re-layouts  31.2 us
    dot_general x12, matrix products, right_product(): lax.dot_general(left, right, (((1,), (1,)), ((), ())), preferred_element_...  22.1 us
    dot_general x2, matrix products, exact_product(): jnp.dot(left, right, precision=precise, preferred_element_type=jnp.float32)  20.9 us
    dot_general x1, matrix products, body(): jnp.einsum('tiha,th->iha', spread_q, grad_denom, precision=precise)  16.1 us
  transfers between devices with their start and end apart: 4, of which 4 were waited for; matrix products, arithmetic and copies ran while one was open for 3% of the time, Pallas kernels for 0%

commit v1 on v0

v1 whole, which is shorter than its diff:
```python
import functools
import math

import jax
import jax.numpy as jnp
from jax import lax
from jax.experimental import pallas as pl
from jax.experimental.pallas import tpu as pltpu
from jax.sharding import PartitionSpec as P

D = 128
H = 8
HD = 16
FF = 256
E = 4
FIN = 3
STEP = 10

EPS_NORM = 1e-05
BETA_ONE = 0.9
BETA_TWO = 0.999
RATE_LEARN = 0.1
DECAY_RATE = 0.01
EPS_ADAM = 1e-08

LANES = 128
VMEM_LIMIT = 56 * 1024 * 1024
SAMPLE_TILE = 512
TOKEN_TILE = 512

F32 = jnp.float32
BF16 = jnp.bfloat16

ROW_GAIN_ONE = 0
ROW_SHIFT_ONE = 1
ROW_QUERY = 2
ROW_OUT = ROW_QUERY + D
ROW_OUT_B = ROW_OUT + D
ROW_GAIN_TWO = ROW_OUT_B + 1
ROW_SHIFT_TWO = ROW_GAIN_TWO + 1
ROW_UP = ROW_SHIFT_TWO + 1
ROW_UP_B = ROW_UP + E * D * 2
ROW_DOWN = ROW_UP_B + E * 2
ROW_DOWN_B = ROW_DOWN + E * FF
SHARED_ROWS = ROW_DOWN_B + E

ROW_IN = 0
ROW_IN_B = ROW_IN + FIN
ROW_HID = ROW_IN_B + 1
ROW_HID_B = ROW_HID + D
ROW_PAIR = ROW_HID_B + 1
BRANCH_ROWS = ROW_PAIR + 2 * D

COL_GAIN_ONE = 0
COL_SHIFT_ONE = 1
COL_OUT_B = 2
COL_GAIN_TWO = 3
COL_SHIFT_TWO = 4
COL_UP_B = 5
COL_DOWN_B = COL_UP_B + 2 * E

TANH_C = math.sqrt(2.0 / math.pi)
TANH_CUBE = 0.044715


def up_to(amount, unit):
    return -(-amount // unit) * unit


def adam_step(master, moment_one, moment_two, grad):
    first = BETA_ONE * moment_one + (1.0 - BETA_ONE) * grad
    second = BETA_TWO * moment_two + (1.0 - BETA_TWO) * grad * grad
    first_hat = first / (1.0 - BETA_ONE**STEP)
    second_hat = second / (1.0 - BETA_TWO**STEP)
    fresh = master - RATE_LEARN * (
        first_hat / (jnp.sqrt(second_hat) + EPS_ADAM) + DECAY_RATE * master
    )
    return (fresh, first, second)


def dot_nn(left, right):
    return jnp.dot(left, right, preferred_element_type=F32)


def dot_nt(left, right):
    return lax.dot_general(left, right, (((1,), (1,)), ((), ())), preferred_element_type=F32)


def head_sum(values):
    split = values.reshape(H, HD, values.shape[1])
    total = jnp.sum(split, axis=1, keepdims=True)
    return jnp.broadcast_to(total, split.shape).reshape(values.shape)


def head_softmax(values):
    split = values.reshape(H, HD, values.shape[1])
    top = jnp.max(split, axis=1, keepdims=True)
    raised = jnp.exp(split - top)
    total = jnp.sum(raised, axis=1, keepdims=True)
    return (raised * (1.0 / total)).reshape(values.shape)


def gelu_parts(inner):
    square = inner * inner
    bend = TANH_C + (TANH_C * TANH_CUBE) * square
    curve = jnp.tanh(inner * bend)
    gate = 0.5 + 0.5 * curve
    slope = (TANH_C) + (3.0 * TANH_C * TANH_CUBE) * square
    grad = gate + inner * (0.5 - 0.5 * curve * curve) * slope
    return inner * gate, grad


def wide(tile, length):
    if length == tile.shape[1]:
        return tile
    return jnp.concatenate([tile] * (length // tile.shape[1]), axis=1)


def column(matrix, index, length):
    return jnp.broadcast_to(matrix[:, index : index + 1], (matrix.shape[0], length))


def fold_lanes(values):
    total = values[:, :LANES]
    for start in range(LANES, values.shape[1], LANES):
        total = total + values[:, start : start + LANES]
    return total


def lane_total_row(values):
    return jnp.sum(jnp.transpose(values), axis=0, keepdims=True)


def head_mask():
    row = lax.broadcasted_iota(jnp.int32, (D, D), 0) // HD
    col = lax.broadcasted_iota(jnp.int32, (D, D), 1) // HD
    return (row == col).astype(F32)


def fold_heads(values, mask):
    return jnp.sum((values * mask).reshape(H, HD, D), axis=0)


def spread_heads(compact, mask):
    return jnp.concatenate([compact] * H, axis=0) * mask


def store_starts(counts, starts, items):
    if items <= 8:
        total = jnp.int32(0)
        for item in range(items):
            starts[item] = total
            total = total + counts(item)
        starts[items] = total
    else:
        def step(item, total):
            starts[item] = total
            return total + counts(item)

        starts[items] = lax.fori_loop(0, items, step, jnp.int32(0))


def item_span(starts, items, begin, end):
    def step(item, span):
        low, high = span
        return (
            low + (starts[item + 1] <= begin).astype(jnp.int32),
            high + (starts[item] < end).astype(jnp.int32),
        )

    span = (jnp.int32(0), jnp.int32(0))
    if items <= 8:
        for item in range(items):
            span = step(item, span)
        return span
    return lax.fori_loop(0, items, step, span)


def item_row(starts, item, begin, length):
    position = begin + lax.broadcasted_iota(jnp.int32, (1, length), 1)
    return ((position >= starts[item]) & (position < starts[item + 1])).astype(F32)


def over_items(starts, items, begin, length, visit):
    low, high = item_span(starts, items, begin, begin + length)
    visit(jnp.minimum(low, items - 1), True)

    def step(item, carry):
        visit(item, False)
        return carry

    lax.fori_loop(low + 1, high, step, 0)


def put_shard(vec_ref, tmp_ref, number, shard, height):
    row, shift = divmod(number * shard, LANES)
    touched = (shift + shard - 1) // LANES + 1
    if shift == 0:
        vec_ref[row : row + touched, :] = tmp_ref[8 : 8 + touched, :]
        return
    if number == 0:
        tmp_ref[7:8, :] = jnp.zeros((1, LANES), F32)
    else:
        tmp_ref[7:8, :] = vec_ref[row : row + 1, :]
    lane = lax.broadcasted_iota(jnp.int32, (touched, LANES), 1)
    vec_ref[row : row + touched, :] = jnp.where(
        lane >= shift, tmp_ref[8 : 8 + touched, :], tmp_ref[7 : 7 + touched, :]
    )


def turned(block, amount):
    amount = amount % LANES
    return block if amount == 0 else pltpu.roll(block, amount, 1)


def take_shard(vec_ref, number, shard, height):
    row, shift = divmod(number * shard, LANES)
    here = vec_ref[row : row + height, :]
    if shift == 0:
        return here
    after = vec_ref[row + 1 : row + 1 + height, :]
    lane = lax.broadcasted_iota(jnp.int32, (height, LANES), 1)
    return turned(jnp.where(lane >= shift, here, after), LANES - shift)


def sample_forward_kernel(
    plan,
    scal_ref,
    count_ref,
    recv_ref,
    func_ref,
    msg_ref,
    keys_ref,
    vals_ref,
    first_ref,
    second_ref,
    slope_one_ref,
    slope_two_ref,
    hid_ref,
    pair_ref,
    vec_ref,
    tmp_ref,
    col_ref,
    hid_t_ref,
    pair_t_ref,
    acc_ref,
    starts,
):
    tile, items, parts, shard, height, slots = plan
    step = pl.program_id(0)

    @pl.when(step == 0)
    def _():
        store_starts(lambda item: count_ref[0, item], starts, items)
        acc_ref[...] = jnp.zeros(acc_ref.shape, F32)
        for number in range(parts):
            shift = (number * shard) % LANES
            tmp_ref[8 : 8 + height, :] = turned(recv_ref[number].astype(F32), shift)
            put_shard(vec_ref, tmp_ref, number, shard, height)
        for slot, row in enumerate((0, 1, 2, ROW_IN_B, ROW_HID_B)):
            col_ref[slot] = jnp.transpose(
                jnp.broadcast_to(vec_ref[row : row + 1, :], (D, D))
            )
        hid = vec_ref[ROW_HID : ROW_HID + D, :]
        hid_ref[...] = hid.astype(BF16)
        hid_t_ref[...] = jnp.transpose(hid).astype(BF16)
        for part in range(2):
            piece = vec_ref[pl.ds(ROW_PAIR + part, D, stride=2), :]
            pair_ref[:, part * D : (part + 1) * D] = piece.astype(BF16)
            pair_t_ref[part * D : (part + 1) * D, :] = jnp.transpose(piece).astype(BF16)

    funcs = func_ref[0]
    first_in = wide(col_ref[3], tile)
    for part in range(FIN):
        first_in = first_in + wide(col_ref[part], tile) * funcs[part : part + 1, :]
    first, slope_one = gelu_parts(first_in)
    first = first.astype(BF16)
    first_ref[...] = first
    slope_one_ref[...] = slope_one.astype(slope_one_ref.dtype)
    second_in = dot_nn(hid_t_ref[...], first) + wide(col_ref[4], tile)
    second, slope_two = gelu_parts(second_in)
    second = second.astype(BF16)
    second_ref[...] = second
    slope_two_ref[...] = slope_two.astype(slope_two_ref.dtype)
    pair = dot_nn(pair_t_ref[...], second)
    keys = head_softmax(pair[:D])
    keys_ref[...] = keys.astype(BF16)
    vals = pair[D:].astype(BF16)
    vals_ref[...] = vals
    vals_ones = jnp.concatenate([vals, jnp.ones((16, tile), BF16)], axis=0)
    begin = scal_ref[1] * slots + step * tile

    def visit(item, _):
        masked = (keys * item_row(starts, item, begin, tile)).astype(BF16)
        acc_ref[item] += dot_nt(vals_ones, masked)

    over_items(starts, items, begin, tile, visit)

    @pl.when(step == pl.num_programs(0) - 1)
    def _():
        mask = head_mask()
        msg_ref[items * HD :, :] = jnp.zeros((msg_ref.shape[0] - items * HD, LANES), F32)
        for item in range(items):
            msg_ref[item * HD : (item + 1) * HD, :] = fold_heads(acc_ref[item, :D, :], mask)
            msg_ref[items * HD + item : items * HD + item + 1, :] = acc_ref[item, D : D + 1, :]


def weight_kernel(
    plan,
    scal_ref,
    own_ref,
    other_ref,
    query_ref,
    query_t_ref,
    out_ref,
    out_t_ref,
    up_ref,
    up_t_ref,
    down_ref,
    down_t_ref,
    cols_ref,
    vec_ref,
    tmp_ref,
):
    parts, shard, half, offset = plan
    core = scal_ref[0]
    own_at = pl.multiple_of(8 + core * half, 8)
    other_at = pl.multiple_of(8 + (1 - core) * half, 8)
    for number in range(parts):
        shift = (number * shard) % LANES
        tmp_ref[pl.ds(own_at, half), :] = turned(
            own_ref[number, offset : offset + half, :].astype(F32), shift
        )
        tmp_ref[pl.ds(other_at, half), :] = turned(
            other_ref[number, offset : offset + half, :].astype(F32), shift
        )
        put_shard(vec_ref, tmp_ref, number, shard, 2 * half)
    query = vec_ref[ROW_QUERY : ROW_QUERY + D, :]
    query_ref[...] = query.astype(BF16)
    query_t_ref[...] = jnp.transpose(query).astype(BF16)
    out = vec_ref[ROW_OUT : ROW_OUT + D, :]
    out_ref[...] = out.astype(BF16)
    out_t_ref[...] = jnp.transpose(out).astype(BF16)
    for expert in range(E):
        for part in range(2):
            up = vec_ref[pl.ds(ROW_UP + expert * 2 * D + part, D, stride=2), :]
            up_ref[expert, :, part * D : (part + 1) * D] = up.astype(BF16)
            up_t_ref[expert, part * D : (part + 1) * D, :] = jnp.transpose(up).astype(BF16)
            row = ROW_DOWN + expert * FF + part * D
            down = vec_ref[row : row + D, :]
            down_ref[expert, part * D : (part + 1) * D, :] = down.astype(BF16)
            down_t_ref[expert, :, part * D : (part + 1) * D] = jnp.transpose(down).astype(BF16)
    tmp_ref[0:D, :] = jnp.zeros((D, LANES), F32)
    rows = [ROW_GAIN_ONE, ROW_SHIFT_ONE, ROW_OUT_B, ROW_GAIN_TWO, ROW_SHIFT_TWO]
    rows += [ROW_UP_B + number for number in range(2 * E)]
    rows += [ROW_DOWN_B + number for number in range(E)]
    for slot, row in enumerate(rows):
        tmp_ref[slot : slot + 1, :] = vec_ref[row : row + 1, :]
    cols_ref[...] = jnp.transpose(tmp_ref[0:D, :])


def norm_unit(values):
    centre = values - jnp.sum(values, axis=0, keepdims=True) * (1.0 / D)
    spread = jnp.sum(centre * centre, axis=0, keepdims=True) * (1.0 / D)
    scale = lax.rsqrt(spread + EPS_NORM)
    return centre * scale, scale


def norm_back(grad_unit, unit, scale):
    mean_one = jnp.sum(grad_unit, axis=0, keepdims=True) * (1.0 / D)
    mean_two = jnp.sum(grad_unit * unit, axis=0, keepdims=True) * (1.0 / D)
    return scale * (grad_unit - mean_one - unit * mean_two)


def query_kernel(
    scal_ref,
    token_ref,
    cot_ref,
    query_t_ref,
    cols_ref,
    token_t_ref,
    cot_t_ref,
    unit_ref,
    scale_ref,
    norm_ref,
    soft_ref,
):
    tokens = jnp.transpose(token_ref[...].astype(F32))
    length = tokens.shape[1]
    token_t_ref[...] = tokens.astype(BF16)
    cot_t_ref[...] = jnp.transpose(cot_ref[...])
    unit, scale = norm_unit(tokens)
    unit_ref[...] = unit
    scale_ref[...] = jnp.broadcast_to(scale, scale_ref.shape)
    cols = cols_ref[...]
    norm = (unit * column(cols, COL_GAIN_ONE, length) + column(cols, COL_SHIFT_ONE, length)).astype(
        BF16
    )
    norm_ref[...] = norm
    soft_ref[...] = head_softmax(dot_nn(query_t_ref[...], norm))


def token_kernel(
    plan,
    scal_ref,
    count_ref,
    own_ref,
    other_ref,
    gate_ref,
    token_t_ref,
    cot_t_ref,
    unit_ref,
    scale_ref,
    norm_ref,
    soft_ref,
    query_ref,
    out_w_ref,
    out_t_ref,
    up_ref,
    up_t_ref,
    down_ref,
    down_t_ref,
    cols_ref,
    output_ref,
    grad_ref,
    own_msg_ref,
    other_msg_ref,
    g_query_ref,
    g_out_ref,
    g_up_ref,
    g_down_ref,
    g_vec_ref,
    left_ref,
    back_ref,
    acc_ref,
    mix_ref,
    pull_ref,
    starts,
):
    tile, items, slots, steps = plan
    step = pl.program_id(0)
    first_row = scal_ref[1] * slots + scal_ref[0] * (tile * steps)

    @pl.when(step == 0)
    def _():
        store_starts(lambda item: count_ref[item], starts, items)
        acc_ref[...] = jnp.zeros(acc_ref.shape, F32)
        g_query_ref[...] = jnp.zeros(g_query_ref.shape, F32)
        g_out_ref[...] = jnp.zeros(g_out_ref.shape, F32)
        g_up_ref[...] = jnp.zeros(g_up_ref.shape, F32)
        g_down_ref[...] = jnp.zeros(g_down_ref.shape, F32)
        g_vec_ref[...] = jnp.zeros(g_vec_ref.shape, F32)
        mask = head_mask()
        low, high = item_span(starts, items, first_row, first_row + tile * steps)

        def build(item, carry):
            at = pl.multiple_of(item * HD, HD)
            for slot, source in enumerate((own_ref, other_ref)):
                block = spread_heads(source[pl.ds(at, HD), :], mask)
                total = source[pl.ds(items * HD + item, 1), :] * mask
                for kind, piece in enumerate((block, total)):
                    row = (2 * kind + slot) * D
                    high_part = piece.astype(BF16)
                    left_ref[item, row : row + D, :D] = high_part
                    left_ref[item, row : row + D, D:] = (piece - high_part.astype(F32)).astype(BF16)
                    turned_piece = jnp.transpose(piece)
                    if kind == 1:
                        turned_piece = turned_piece * (1.0 / HD)
                    back_ref[item, :, row : row + D] = turned_piece.astype(BF16)
            return carry

        lax.fori_loop(low, high, build, 0)

    cols = cols_ref[...]
    begin = first_row + step * tile
    soft = soft_ref[...]
    soft_low = soft.astype(BF16)
    soft_vals = soft_low.astype(F32)

    def forward(item, opening):
        masked = (soft_vals * item_row(starts, item, begin, tile)).astype(BF16)
        fresh = dot_nn(left_ref[item], jnp.concatenate([masked, masked], axis=0))
        mix_ref[...] = fresh if opening else mix_ref[...] + fresh

    over_items(starts, items, begin, tile, forward)
    numer_one, numer_two = mix_ref[:D, :], mix_ref[D : 2 * D, :]
    inv_one, inv_two = 1.0 / mix_ref[2 * D : 3 * D, :], 1.0 / mix_ref[3 * D :, :]
    own_one, own_two = numer_one * inv_one, numer_two * inv_two
    attended = (0.5 * (own_one + own_two)).astype(BF16)
    cot = cot_t_ref[...]
    residual = (
        token_t_ref[...].astype(F32)
        + dot_nn(out_t_ref[...], attended)
        + column(cols, COL_OUT_B, tile)
    )
    unit, scale = norm_unit(residual)
    gain_two = column(cols, COL_GAIN_TWO, tile)
    norm = (unit * gain_two + column(cols, COL_SHIFT_TWO, tile)).astype(BF16)
    ones = jnp.ones((16, tile), BF16)
    norm_ones = jnp.concatenate([norm, ones], axis=0)
    gates = gate_ref[...].astype(F32)
    gates = gates / jnp.sum(gates, axis=0, keepdims=True)
    mixture = residual
    grad_norm = jnp.zeros((D, tile), F32)
    for expert in range(E):
        bias = jnp.concatenate(
            [column(cols, COL_UP_B + 2 * expert + part, tile) for part in range(2)], axis=0
        )
        inner = dot_nn(up_t_ref[expert], norm) + bias
        active, slope = gelu_parts(inner)
        active = active.astype(BF16)
        result = dot_nn(down_t_ref[expert], active) + column(cols, COL_DOWN_B + expert, tile)
        gate = gates[expert : expert + 1, :]
        mixture = mixture + gate * result
        grad_result = (gate * cot).astype(BF16)
        g_down_ref[expert] += dot_nt(jnp.concatenate([active, ones], axis=0), grad_result)
        grad_inner = (slope * dot_nn(down_ref[expert], grad_result)).astype(BF16)
        g_up_ref[expert] += dot_nt(norm_ones, grad_inner)
        grad_norm = grad_norm + dot_nn(up_ref[expert], grad_inner)
    output_ref[...] = jnp.transpose(mixture).astype(BF16)
    g_vec_ref[2] += fold_lanes(grad_norm * unit)
    g_vec_ref[3] += fold_lanes(grad_norm)
    grad_residual = cot + norm_back(grad_norm * gain_two, unit, scale)
    grad_proj = grad_residual.astype(BF16)
    g_out_ref[...] += dot_nt(jnp.concatenate([attended, ones], axis=0), grad_proj)
    grad_own = 0.5 * dot_nn(out_w_ref[...], grad_proj)
    grad_one, grad_two = grad_own * inv_one, grad_own * inv_two
    sum_one = -head_sum(grad_one * own_one)
    sum_two = -head_sum(grad_two * own_two)
    grads = jnp.concatenate([grad_one, grad_two, sum_one, sum_two], axis=0).astype(BF16)

    def backward(item, opening):
        row = item_row(starts, item, begin, tile)
        masked = (soft_vals * row).astype(BF16)
        acc_ref[item] += dot_nt(grads, masked)
        fresh = row * dot_nn(back_ref[item], grads)
        pull_ref[...] = fresh if opening else pull_ref[...] + fresh

    over_items(starts, items, begin, tile, backward)
    pull = pull_ref[...]
    grad_query = (soft * (pull - head_sum(pull * soft))).astype(BF16)
    g_query_ref[...] += dot_nt(norm_ref[...], grad_query)
    grad_norm_one = dot_nn(query_ref[...], grad_query)
    unit_one = unit_ref[...]
    g_vec_ref[0] += fold_lanes(grad_norm_one * unit_one)
    g_vec_ref[1] += fold_lanes(grad_norm_one)
    grad_token = grad_residual + norm_back(
        grad_norm_one * column(cols, COL_GAIN_ONE, tile), unit_one, scale_ref[0:1, :]
    )
    grad_ref[...] = jnp.transpose(grad_token)

    @pl.when(step == steps - 1)
    def _():
        mask = head_mask()
        for slot, target in enumerate((own_msg_ref, other_msg_ref)):
            target[items * HD :, :] = jnp.zeros((target.shape[0] - items * HD, LANES), F32)
            for item in range(items):
                full = acc_ref[item, slot * D : (slot + 1) * D, :]
                target[item * HD : (item + 1) * HD, :] = fold_heads(full, mask)
                sums = acc_ref[item, (2 + slot) * D : (3 + slot) * D, :]
                target[items * HD + item : items * HD + item + 1, :] = fold_heads(sums, mask)[0:1]


def pack_kernel(
    plan,
    scal_ref,
    g_query_ref,
    g_out_ref,
    g_up_ref,
    g_down_ref,
    g_vec_ref,
    own_ref,
    other_ref,
    vec_ref,
    tmp_ref,
):
    parts, shard, half = plan
    vec_ref[SHARED_ROWS:, :] = jnp.zeros((vec_ref.shape[0] - SHARED_ROWS, LANES), F32)
    for slot, row in enumerate((ROW_GAIN_ONE, ROW_SHIFT_ONE, ROW_GAIN_TWO, ROW_SHIFT_TWO)):
        vec_ref[row : row + 1, :] = lane_total_row(g_vec_ref[slot])
    vec_ref[ROW_QUERY : ROW_QUERY + D, :] = g_query_ref[...]
    vec_ref[ROW_OUT : ROW_OUT + D + 1, :] = g_out_ref[: D + 1, :]
    for expert in range(E):
        for part in range(2):
            columns = slice(part * D, (part + 1) * D)
            vec_ref[pl.ds(ROW_UP + expert * 2 * D + part, D, stride=2), :] = g_up_ref[
                expert, :D, columns
            ]
            row = ROW_UP_B + 2 * expert + part
            vec_ref[row : row + 1, :] = g_up_ref[expert, D : D + 1, columns]
        row = ROW_DOWN + expert * FF
        vec_ref[row : row + FF, :] = g_down_ref[expert, :FF, :]
        row = ROW_DOWN_B + expert
        vec_ref[row : row + 1, :] = g_down_ref[expert, FF : FF + 1, :]
    core = scal_ref[0]
    own_at = pl.multiple_of(core * half, 8)
    other_at = pl.multiple_of((1 - core) * half, 8)
    for number in range(parts):
        tmp_ref[...] = take_shard(vec_ref, number, shard, 2 * half)
        own_ref[number] = tmp_ref[pl.ds(own_at, half), :]
        other_ref[number] = tmp_ref[pl.ds(other_at, half), :].astype(BF16)


def sample_backward_kernel(
    plan,
    scal_ref,
    count_ref,
    msg_ref,
    func_ref,
    keys_ref,
    vals_ref,
    first_ref,
    second_ref,
    slope_one_ref,
    slope_two_ref,
    hid_ref,
    pair_ref,
    own_ref,
    other_ref,
    out_own_ref,
    out_other_ref,
    grad_own_ref,
    grad_other_ref,
    send_ref,
    out_ref,
    grad_ref,
    vec_ref,
    left_keys_ref,
    left_vals_ref,
    shift_ref,
    keys_acc_ref,
    vals_acc_ref,
    g_pair_ref,
    g_hid_ref,
    g_in_ref,
    starts,
):
    tile, items, parts, shard, height, slots, steps = plan
    step = pl.program_id(0)
    core = scal_ref[0]
    out_ref[core] = out_own_ref[...]
    out_ref[1 - core] = out_other_ref[...]
    grad_ref[core] = grad_own_ref[...]
    grad_ref[1 - core] = grad_other_ref[...]

    @pl.when(step == 0)
    def _():
        store_starts(lambda item: count_ref[0, item], starts, items)
        g_pair_ref[...] = jnp.zeros(g_pair_ref.shape, F32)
        g_hid_ref[...] = jnp.zeros(g_hid_ref.shape, F32)
        g_in_ref[...] = jnp.zeros(g_in_ref.shape, F32)
        mask = head_mask()
        low, high = item_span(
            starts, items, scal_ref[1] * slots, scal_ref[1] * slots + tile * steps
        )

        def build(item, carry):
            at = pl.multiple_of(item * HD, HD)
            block = spread_heads(msg_ref[pl.ds(at, HD), :], mask)
            left_vals_ref[item] = block.astype(BF16)
            left_keys_ref[item] = jnp.transpose(block).astype(BF16)
            row = msg_ref[pl.ds(items * HD + item, 1), :]
            shift_ref[item] = jnp.transpose(jnp.broadcast_to(row, (D, D)))
            return carry

        @pl.when(high <= low)
        def _():
            last = items - 1
            left_vals_ref[last] = jnp.zeros((D, D), BF16)
            left_keys_ref[last] = jnp.zeros((D, D), BF16)
            shift_ref[last] = jnp.zeros((D, D), F32)

        lax.fori_loop(low, high, build, 0)

    keys = keys_ref[...]
    vals = vals_ref[...]
    begin = scal_ref[1] * slots + step * tile

    def visit(item, opening):
        row = item_row(starts, item, begin, tile)
        fresh_keys = row * (dot_nn(left_keys_ref[item], vals) + wide(shift_ref[item], tile))
        fresh_vals = row * dot_nn(left_vals_ref[item], keys)
        keys_acc_ref[...] = fresh_keys if opening else keys_acc_ref[...] + fresh_keys
        vals_acc_ref[...] = fresh_vals if opening else vals_acc_ref[...] + fresh_vals

    over_items(starts, items, begin, tile, visit)
    soft = keys.astype(F32)
    grad_keys = keys_acc_ref[...]
    grad_in = soft * (grad_keys - head_sum(grad_keys * soft))
    grad_pair = jnp.concatenate([grad_in, vals_acc_ref[...]], axis=0).astype(BF16)
    g_pair_ref[...] += dot_nt(second_ref[...], grad_pair)
    grad_second = (slope_two_ref[...].astype(F32) * dot_nn(pair_ref[...], grad_pair)).astype(BF16)
    first_ones = jnp.concatenate([first_ref[...], jnp.ones((16, tile), BF16)], axis=0)
    g_hid_ref[...] += dot_nt(first_ones, grad_second)
    grad_first = slope_one_ref[...].astype(F32) * dot_nn(hid_ref[...], grad_second)
    funcs = func_ref[0]
    for part in range(FIN):
        g_in_ref[part] += fold_lanes(grad_first * funcs[part : part + 1, :])
    g_in_ref[FIN] += fold_lanes(grad_first)

    @pl.when(step == steps - 1)
    def _():
        vec_ref[BRANCH_ROWS:, :] = jnp.zeros((vec_ref.shape[0] - BRANCH_ROWS, LANES), F32)
        for part in range(FIN + 1):
            vec_ref[part : part + 1, :] = lane_total_row(g_in_ref[part])
        vec_ref[ROW_HID : ROW_HID + D + 1, :] = g_hid_ref[: D + 1, :]
        for part in range(2):
            vec_ref[pl.ds(ROW_PAIR + part, D, stride=2), :] = g_pair_ref[
                :, part * D : (part + 1) * D
            ]
        for number in range(parts):
            send_ref[number, :height, :] = take_shard(vec_ref, number, shard, height).astype(BF16)
            send_ref[number, height:, :] = (
                own_ref[number] + other_ref[number].astype(F32)
            ).astype(BF16)


def sum_over_points(values, count):
    bit = 1
    while bit < count:
        masks = [bit] if 2 * bit >= count else [bit, 2 * bit, 3 * bit]
        pieces = [
            lax.ppermute(values, "pts", [(source, source ^ mask) for source in range(count)])
            for mask in masks
        ]
        values = functools.reduce(jnp.add, pieces, values)
        bit *= 4
    return values


def swap_cores(values):
    return lax.ppermute(values, "branch", [(0, 1), (1, 0)])


def whole(shape, kind=None):
    zeros = (0,) * len(shape)
    return pl.BlockSpec(shape, lambda *_: zeros)


def body(
    tokens,
    funcs,
    item_counts,
    func_counts,
    gate_ints,
    cotangent,
    shared_master,
    shared_m,
    shared_v,
    branch_master,
    branch_m,
    branch_v,
):
    count = lax.axis_size("pts")
    core = lax.axis_index("branch")
    scal = jnp.stack([core, lax.axis_index("pts")]).astype(jnp.int32)
    items = item_counts.shape[0]
    chip_rows = tokens.shape[0]
    rows = chip_rows // 2
    slots = funcs.shape[2]
    shared_len = shared_master.shape[0]
    branch_len = branch_master.shape[1]
    half = up_to(-(-shared_len // (2 * LANES)), 16)
    height = up_to(-(-branch_len // LANES), 16)
    msg_rows = items * HD + up_to(items, 8)
    params = pltpu.CompilerParams(vmem_limit_bytes=VMEM_LIMIT)
    shape = jax.ShapeDtypeStruct

    shared_pad = jnp.pad(shared_master.astype(BF16), (0, 2 * half * LANES - shared_len))
    shared_half = lax.dynamic_slice_in_dim(shared_pad, core * (half * LANES), half * LANES, 0)
    branch_pad = jnp.pad(
        branch_master.reshape(-1).astype(BF16), (0, height * LANES - branch_len)
    )
    send = jnp.concatenate([branch_pad, shared_half]).reshape(1, height + half, LANES)
    send = jnp.broadcast_to(send, (count, height + half, LANES))
    recv = lax.all_to_all(send, "pts", 0, 0)
    recv_other = swap_cores(recv)

    tile = min(SAMPLE_TILE, slots)
    steps = slots // tile
    stream = lambda height_: pl.BlockSpec((height_, tile), lambda i, *_: (0, i))
    vec_rows = up_to(BRANCH_ROWS + 2 * height + 8, 8)
    (
        msg,
        keys,
        vals,
        first,
        second,
        slope_one,
        slope_two,
        hid_w,
        pair_w,
    ) = pl.pallas_call(
        functools.partial(
            sample_forward_kernel, (tile, items, count, branch_len, height, slots)
        ),
        grid_spec=pltpu.PrefetchScalarGridSpec(
            num_scalar_prefetch=1,
            grid=(steps,),
            in_specs=[
                pl.BlockSpec(memory_space=pltpu.SMEM),
                pl.BlockSpec((count, height, LANES), lambda i, *_: (0, 0, 0)),
                pl.BlockSpec((1, FIN, tile), lambda i, *_: (0, 0, i)),
            ],
            out_specs=[
                whole((msg_rows, LANES)),
                stream(D),
                stream(D),
                stream(D),
                stream(D),
                stream(D),
                stream(D),
                whole((D, D)),
                whole((D, 2 * D)),
            ],
            scratch_shapes=[
                pltpu.VMEM((vec_rows, LANES), F32),
                pltpu.VMEM((8 + 2 * height, LANES), F32),
                pltpu.VMEM((5, D, D), F32),
                pltpu.VMEM((D, D), BF16),
                pltpu.VMEM((2 * D, D), BF16),
                pltpu.VMEM((items, D + 16, D), F32),
                pltpu.SMEM((items + 1,), jnp.int32),
            ],
        ),
        out_shape=[
            shape((msg_rows, LANES), F32),
            shape((D, slots), BF16),
            shape((D, slots), BF16),
            shape((D, slots), BF16),
            shape((D, slots), BF16),
            shape((D, slots), BF16),
            shape((D, slots), BF16),
            shape((D, D), BF16),
            shape((D, 2 * D), BF16),
        ],
        compiler_params=params,
        cost_estimate=pl.CostEstimate(
            flops=slots * D * D * 10, bytes_accessed=slots * D * 12, transcendentals=slots * D * 3
        ),
        name="sample_forward",
    )(scal, func_counts, recv, funcs)

    summary = sum_over_points(msg, count)
    summary_other = swap_cores(summary)

    shared_rows = up_to(SHARED_ROWS + 2 * half + 8, 8)
    (query_w, query_t, out_w, out_t, up_w, up_t, down_w, down_t, cols) = pl.pallas_call(
        functools.partial(weight_kernel, (count, shared_len, half, height)),
        in_specs=[
            pl.BlockSpec(memory_space=pltpu.SMEM),
            whole(recv.shape),
            whole(recv.shape),
        ],
        out_specs=[
            whole((D, D)),
            whole((D, D)),
            whole((D, D)),
            whole((D, D)),
            whole((E, D, FF)),
            whole((E, FF, D)),
            whole((E, FF, D)),
            whole((E, D, FF)),
            whole((D, D)),
        ],
        out_shape=[
            shape((D, D), BF16),
            shape((D, D), BF16),
            shape((D, D), BF16),
            shape((D, D), BF16),
            shape((E, D, FF), BF16),
            shape((E, FF, D), BF16),
            shape((E, FF, D), BF16),
            shape((E, D, FF), BF16),
            shape((D, D), F32),
        ],
        scratch_shapes=[
            pltpu.VMEM((shared_rows, LANES), F32),
            pltpu.VMEM((max(8 + 2 * half, D) + 8, LANES), F32),
        ],
        compiler_params=params,
        cost_estimate=pl.CostEstimate(flops=0, bytes_accessed=8 << 20, transcendentals=0),
        name="weights",
    )(scal, recv, recv_other)

    token_tile = min(TOKEN_TILE, rows)
    token_steps = rows // token_tile
    row_block = pl.BlockSpec(
        (token_tile, D), lambda i, scal_ref: (scal_ref[0] * token_steps + i, 0)
    )
    token_stream = lambda height_: pl.BlockSpec((height_, token_tile), lambda i, *_: (0, i))
    (token_t, cot_t, unit, scale, norm, soft) = pl.pallas_call(
        query_kernel,
        grid_spec=pltpu.PrefetchScalarGridSpec(
            num_scalar_prefetch=1,
            grid=(token_steps,),
            in_specs=[row_block, row_block, whole((D, D)), whole((D, D))],
            out_specs=[
                token_stream(D),
                token_stream(D),
                token_stream(D),
                token_stream(8),
                token_stream(D),
                token_stream(D),
            ],
        ),
        out_shape=[
            shape((D, rows), BF16),
            shape((D, rows), F32),
            shape((D, rows), F32),
            shape((8, rows), F32),
            shape((D, rows), BF16),
            shape((D, rows), F32),
        ],
        compiler_params=params,
        cost_estimate=pl.CostEstimate(
            flops=rows * D * D * 2, bytes_accessed=rows * D * 24, transcendentals=rows * D
        ),
        name="queries",
    )(scal, tokens, cotangent, query_t, cols)

    (
        output_own,
        grad_own,
        own_msg,
        other_msg,
        g_query,
        g_out,
        g_up,
        g_down,
        g_vec,
    ) = pl.pallas_call(
        functools.partial(token_kernel, (token_tile, items, chip_rows, token_steps)),
        grid_spec=pltpu.PrefetchScalarGridSpec(
            num_scalar_prefetch=1,
            grid=(token_steps,),
            in_specs=[
                pl.BlockSpec(memory_space=pltpu.SMEM),
                whole((msg_rows, LANES)),
                whole((msg_rows, LANES)),
                pl.BlockSpec((E, token_tile), lambda i, scal_ref: (0, scal_ref[0] * token_steps + i)),
                token_stream(D),
                token_stream(D),
                token_stream(D),
                token_stream(8),
                token_stream(D),
                token_stream(D),
                whole((D, D)),
                whole((D, D)),
                whole((D, D)),
                whole((E, D, FF)),
                whole((E, FF, D)),
                whole((E, FF, D)),
                whole((E, D, FF)),
                whole((D, D)),
            ],
            out_specs=[
                pl.BlockSpec((token_tile, D), lambda i, *_: (i, 0)),
                pl.BlockSpec((token_tile, D), lambda i, *_: (i, 0)),
                whole((msg_rows, LANES)),
                whole((msg_rows, LANES)),
                whole((D, D)),
                whole((D + 16, D)),
                whole((E, D + 16, FF)),
                whole((E, FF + 16, D)),
                whole((4, D, D)),
            ],
            scratch_shapes=[
                pltpu.VMEM((items, 4 * D, 2 * D), BF16),
                pltpu.VMEM((items, D, 4 * D), BF16),
                pltpu.VMEM((items, 4 * D, D), F32),
                pltpu.VMEM((4 * D, token_tile), F32),
                pltpu.VMEM((D, token_tile), F32),
                pltpu.SMEM((items + 1,), jnp.int32),
            ],
        ),
        out_shape=[
            shape((rows, D), BF16),
            shape((rows, D), F32),
            shape((msg_rows, LANES), F32),
            shape((msg_rows, LANES), F32),
            shape((D, D), F32),
            shape((D + 16, D), F32),
            shape((E, D + 16, FF), F32),
            shape((E, FF + 16, D), F32),
            shape((4, D, D), F32),
        ],
        compiler_params=params,
        cost_estimate=pl.CostEstimate(
            flops=rows * D * FF * 12 * E, bytes_accessed=rows * D * 24, transcendentals=rows * FF * E
        ),
        name="tokens",
    )(
        scal,
        item_counts,
        summary,
        summary_other,
        gate_ints.T,
        token_t,
        cot_t,
        unit,
        scale,
        norm,
        soft,
        query_w,
        out_w,
        out_t,
        up_w,
        up_t,
        down_w,
        down_t,
        cols,
    )

    summary_grad = sum_over_points(own_msg + swap_cores(other_msg), count)
    output_other = swap_cores(output_own)
    grad_other = swap_cores(grad_own)

    half_own, half_other = pl.pallas_call(
        functools.partial(pack_kernel, (count, shared_len, half)),
        in_specs=[pl.BlockSpec(memory_space=pltpu.SMEM)]
        + [whole(piece.shape) for piece in (g_query, g_out, g_up, g_down, g_vec)],
        out_specs=[whole((count, half, LANES)), whole((count, half, LANES))],
        out_shape=[shape((count, half, LANES), F32), shape((count, half, LANES), BF16)],
        scratch_shapes=[
            pltpu.VMEM((shared_rows, LANES), F32),
            pltpu.VMEM((2 * half, LANES), F32),
        ],
        compiler_params=params,
        cost_estimate=pl.CostEstimate(flops=0, bytes_accessed=4 << 20, transcendentals=0),
        name="pack",
    )(scal, g_query, g_out, g_up, g_down, g_vec)
    half_other = swap_cores(half_other)

    piece = pl.BlockSpec((rows // steps, D), lambda i, *_: (i, 0))
    both = pl.BlockSpec((2, rows // steps, D), lambda i, *_: (0, i, 0))
    grads_send, output, token_grad = pl.pallas_call(
        functools.partial(
            sample_backward_kernel,
            (tile, items, count, branch_len, height, slots, steps),
        ),
        grid_spec=pltpu.PrefetchScalarGridSpec(
            num_scalar_prefetch=1,
            grid=(steps,),
            in_specs=[
                pl.BlockSpec(memory_space=pltpu.SMEM),
                whole((msg_rows, LANES)),
                pl.BlockSpec((1, FIN, tile), lambda i, *_: (0, 0, i)),
                stream(D),
                stream(D),
                stream(D),
                stream(D),
                stream(D),
                stream(D),
                whole((D, D)),
                whole((D, 2 * D)),
                whole((count, half, LANES)),
                whole((count, half, LANES)),
                piece,
                piece,
                piece,
                piece,
            ],
            out_specs=[whole((count, height + half, LANES)), both, both],
            scratch_shapes=[
                pltpu.VMEM((vec_rows, LANES), F32),
                pltpu.VMEM((items, D, D), BF16),
                pltpu.VMEM((items, D, D), BF16),
                pltpu.VMEM((items, D, D), F32),
                pltpu.VMEM((D, tile), F32),
                pltpu.VMEM((D, tile), F32),
                pltpu.VMEM((D, 2 * D), F32),
                pltpu.VMEM((D + 16, D), F32),
                pltpu.VMEM((FIN + 1, D, D), F32),
                pltpu.SMEM((items + 1,), jnp.int32),
            ],
        ),
        out_shape=[
            shape((count, height + half, LANES), BF16),
            shape((2, rows, D), BF16),
            shape((2, rows, D), F32),
        ],
        compiler_params=params,
        cost_estimate=pl.CostEstimate(
            flops=slots * D * D * 16, bytes_accessed=slots * D * 12, transcendentals=0
        ),
        name="sample_backward",
    )(
        scal,
        func_counts,
        summary_grad,
        funcs,
        keys,
        vals,
        first,
        second,
        slope_one,
        slope_two,
        hid_w,
        pair_w,
        half_own,
        half_other,
        output_own,
        output_other,
        grad_own,
        grad_other,
    )

    grads = jnp.sum(lax.all_to_all(grads_send, "pts", 0, 0).astype(F32), axis=0)
    own_half = grads[height:].reshape(-1)
    other_half = swap_cores(own_half)
    shared_grad = jnp.where(
        core == 0,
        jnp.concatenate([own_half, other_half]),
        jnp.concatenate([other_half, own_half]),
    )[:shared_len]
    branch_grad = grads[:height].reshape(1, -1)[:, :branch_len]
    new_branch, new_branch_m, new_branch_v = adam_step(
        branch_master, branch_m, branch_v, branch_grad
    )
    new_shared, new_shared_m, new_shared_v = adam_step(
        shared_master, shared_m, shared_v, shared_grad
    )
    return (
        output.reshape(chip_rows, D),
        token_grad.reshape(chip_rows, D),
        new_shared,
        new_shared_m,
        new_shared_v,
        new_branch,
        new_branch_m,
        new_branch_v,
    )


def solution(mesh):
    in_specs = (
        P("pts", None),
        P("branch", None, "pts"),
        P(),
        P("branch", None),
        P("pts", None),
        P("pts", None),
        P("pts"),
        P("pts"),
        P("pts"),
        P("branch", "pts"),
        P("branch", "pts"),
        P("branch", "pts"),
    )
    out_specs = (
        P("pts", None),
        P("pts", None),
        P("pts"),
        P("pts"),
        P("pts"),
        P("branch", "pts"),
        P("branch", "pts"),
        P("branch", "pts"),
    )
    return jax.shard_map(body, mesh=mesh, in_specs=in_specs, out_specs=out_specs, check_vma=False)
```

time: 633 us -> 122 us (0.19); the launches traced: 623 us -> 121 us
  waiting for transfers between devices: 237 us -> 35.5 us
  blocking collectives: 159 us -> 0 us
  matrix products: 129 us -> 0 us
  Pallas kernels: 0 us -> 43.8 us
  other arithmetic: 41.8 us -> 5.22 us
  local copies, waits for them, and re-layouts: 38.1 us -> 5.91 us
  starting transfers between devices: 0.38 us -> 30 us
  between operations: 17.1 us -> 0.87 us
    psum x2 -> x0, blocking collectives: 159 us -> none  [the longest x1 80.5 us: body(): lax.psum((summary_grad_part, totals_grad_part), 'pts')]
    psum x3 -> x0, waiting for transfers between devices: 130 us -> none  [the longest x1 108 us: body(): shared_sum, branch_sum = lax.psum((shared_grad, branch_grad), 'pts')]
    dot_general x47 -> x0, matrix products: 126 us -> none  [the longest x12 22.1 us: right_product(): lax.dot_general(left, right, (((1,), (1,)), ((), ())), preferred_element_...]
    unnamed x5 -> x0, waiting for transfers between devices: 107 us -> none
    pallas_call x0 -> x6, Pallas kernels: none -> 43.8 us  [the longest x1 12.8 us: body(): pl.pallas_call(functools.partial(token_kernel, (token_tile, items, chip_r...]
    all_to_all x0 -> x2, waiting for transfers between devices: none -> 26.1 us  [the longest x1 13.5 us: body(): grads = jnp.sum(lax.all_to_all(grads_send, 'pts', 0, 0).astype(F32), axis=0)]
    unnamed x259 -> x31, local copies, waits for them, and re-layouts: 31.2 us -> 5.06 us
    ppermute x0 -> x19, starting transfers between devices: none -> 17.2 us  [the longest x12 15.9 us: sum_over_points(): lax.ppermute(values, 'pts', [(source, source ^ mask) for source in range(...]
  transfers between devices with their start and end apart: 4 -> 21, of which waited for: 4 -> 12; matrix products, arithmetic and copies ran while one was open for 3% -> 3% of each run, Pallas kernels for 0% -> 7%
where the time goes in v1:
time: 122 us; the launch traced here: 121 us
  Pallas kernels  43.8 us (36%)
  waiting for transfers between devices  35.5 us (29%)
  starting transfers between devices  30 us (25%)
  local copies, waits for them, and re-layouts  5.91 us (5%)
  other arithmetic  5.22 us (4%)
    ppermute x12, starting transfers between devices, sum_over_points(): lax.ppermute(values, 'pts', [(source, source ^ mask) for source in range(...  15.9 us
    all_to_all x1, waiting for transfers between devices, body(): grads = jnp.sum(lax.all_to_all(grads_send, 'pts', 0, 0).astype(F32), axis=0)  13.5 us
    pallas_call x1, Pallas kernels, body(): pl.pallas_call(functools.partial(token_kernel, (token_tile, items, chip_r...  12.8 us
    all_to_all x1, waiting for transfers between devices, body(): recv = lax.all_to_all(send, 'pts', 0, 0)  12.6 us
    pallas_call x1, Pallas kernels, body(): pl.pallas_call(functools.partial(sample_backward_kernel, (tile, items, co...  11.4 us
    pallas_call x1, Pallas kernels, body(): pl.pallas_call(functools.partial(sample_forward_kernel, (tile, items, cou...  10.6 us
    all_to_all x1, starting transfers between devices, body(): recv = lax.all_to_all(send, 'pts', 0, 0)  8.44 us
    ppermute x12, waiting for transfers between devices, sum_over_points(): lax.ppermute(values, 'pts', [(source, source ^ mask) for source in range(...  8.33 us
  transfers between devices with their start and end apart: 21, of which 12 were waited for; matrix products, arithmetic and copies ran while one was open for 3% of the time, Pallas kernels for 7%

profile of v1, /device:TPU:0, one launch (start us, length us, event | category | flops | bytes accessed | tf_op | source)
XLA Modules:
  0.0 121.4 jit_solution(7282310267059402233)
XLA Ops:
  0.6 0.7 copy-done.9
  1.4 0.9 convert_element_type.18
  2.3 0.8 broadcast_in_dim.8
  3.1 8.4 %all-to-all-start = ((bf16[16,112,128]{2,1,0:T(8,128)(2,1)}), bf16[16,112,128]{2,1,0:T(8,128)(2,1)S(1)}, u32[]{:S(2)}, u32[]{:S(2)}) async-start(bf16[16,112,128]{2,1,0:T(8,128)(2,1)} %broadcast_in_dim.8), calls=%async_computation | async-start | bytes 917504 | tf_op jit(solution)/shard_map/all_to_all | solution.py:776
  11.6 0.7 copy.20.func_ref
  12.3 0.6 pad_add_fusion.scal_ref
  12.9 12.6 %all-to-all-done.recv_ref.own_ref = bf16[16,112,128]{2,1,0:T(8,128)(2,1)S(1)} async-done(((bf16[16,112,128]{2,1,0:T(8,128)(2,1)}), bf16[16,112,128]{2,1,0:T(8,128)(2,1)S(1)}, u32[]{:S(2)}, u32[]{:S(2)}) %all-to-all-start) | async-done | bytes 458784 | tf_op jit(solution)/shard_map/all_to_all | solution.py:776
  25.5 0.8 copy-done
  26.2 10.6 %sample_forward.1 = (f32[72,128]{1,0:T(8,128)}, bf16[128,4096]{1,0:T(8,128)(2,1)}, bf16[128,4096]{1,0:T(8,128)(2,1)}, bf16[128,4096]{1,0:T(8,128)(2,1)}, bf16[12...) custom-call(s32[2]{0:T(128)} %pad_add_fusion.scal_ref, ...), custom_call_target="tpu_custom_call" | custom-call | flops 671088640 | bytes 6291456 | tf_op jit(solution)/shard_map/sample_forward/pallas_call | solution.py:793
  36.8 1.1 collective-permute-start.2
  38.0 1.0 collective-permute-start.1
  38.9 1.5 %collective-permute-start = (f32[72,128]{1,0:T(8,128)}, f32[72,128]{1,0:T(8,128)S(1)}, u32[]{:S(2)}, u32[]{:S(2)}) collective-permute-start(f32[72,128]{1,0:T(8,128)} %get-tuple-element.46), channel_id=1, source_target_pairs={{0,1},{1,0},{2,3},{3,2},{4,5},{5,4},{6,7},{7,6},{8,9},{9,8},{10,11... | collective-permute-start | bytes 110600 | tf_op jit(solution)/shard_map/ppermute | solution.py:723
  40.4 0.0 collective-permute-start.7
  40.4 1.6 %collective-permute-done.2 = f32[72,128]{1,0:T(8,128)S(1)} collective-permute-done((f32[72,128]{1,0:T(8,128)}, f32[72,128]{1,0:T(8,128)S(1)}, u32[]{:S(2)}, u32[]{:S(2)}) %collective-permute-start.2) | collective-permute-done | bytes 36896 | tf_op jit(solution)/shard_map/ppermute | solution.py:723
  42.0 0.4 collective-permute-done.1
  42.4 0.7 collective-permute-done
  43.1 0.8 add_add_fusion.3
  43.9 1.7 %collective-permute-start.5 = (f32[72,128]{1,0:T(8,128)S(1)}, f32[72,128]{1,0:T(8,128)S(1)}, u32[]{:S(2)}, u32[]{:S(2)}) collective-permute-start(f32[72,128]{1,0:T(8,128)S(1)} %add_add_fusion.3), channel_id=1, source_target_pairs={{0,12},{1,13},{2,14},{3,15},{4,8},{5,9},{6,10},{7,11},{8,4},{9,5},... | collective-permute-start | bytes 110600 | tf_op jit(solution)/shard_map/ppermute | solution.py:723
  45.5 1.2 %collective-permute-start.4 = (f32[72,128]{1,0:T(8,128)S(1)}, f32[72,128]{1,0:T(8,128)S(1)}, u32[]{:S(2)}, u32[]{:S(2)}) collective-permute-start(f32[72,128]{1,0:T(8,128)S(1)} %add_add_fusion.3), channel_id=1, source_target_pairs={{0,8},{1,9},{2,10},{3,11},{4,12},{5,13},{6,14},{7,15},{8,0},{9,1},... | collective-permute-start | bytes 110600 | tf_op jit(solution)/shard_map/ppermute | solution.py:723
  46.8 1.5 %collective-permute-start.3 = (f32[72,128]{1,0:T(8,128)S(1)}, f32[72,128]{1,0:T(8,128)S(1)}, u32[]{:S(2)}, u32[]{:S(2)}) collective-permute-start(f32[72,128]{1,0:T(8,128)S(1)} %add_add_fusion.3), channel_id=1, source_target_pairs={{0,4},{1,5},{2,6},{3,7},{4,0},{5,1},{6,2},{7,3},{8,12},{9,13},{10,... | collective-permute-start | bytes 110600 | tf_op jit(solution)/shard_map/ppermute | solution.py:723
  48.3 1.4 %collective-permute-done.5 = f32[72,128]{1,0:T(8,128)S(1)} collective-permute-done((f32[72,128]{1,0:T(8,128)S(1)}, f32[72,128]{1,0:T(8,128)S(1)}, u32[]{:S(2)}, u32[]{:S(2)}) %collective-permute-start.5) | collective-permute-done | bytes 36896 | tf_op jit(solution)/shard_map/ppermute | solution.py:723
  49.7 1.0 collective-permute-done.4
  50.7 0.4 collective-permute-done.3
  51.1 0.1 collective-permute-start.6
  51.2 0.0 copy-start.2
  51.2 0.8 copy-done.2
  51.9 2.6 %weights.1 = (bf16[128,128]{1,0:T(8,128)(2,1)}, bf16[128,128]{1,0:T(8,128)(2,1)}, bf16[128,128]{1,0:T(8,128)(2,1)}, bf16[128,128]{1,0:T(8,128)(2,1)}, bf16[4,128...) custom-call(s32[2]{0:T(128)} %pad_add_fusion.scal_ref, ...), custom_call_target="tpu_custom_call" | custom-call | bytes 8388608 | tf_op jit(solution)/shard_map/weights/pallas_call | solution.py:848
  54.6 3.5 %queries.1 = (bf16[128,1024]{1,0:T(8,128)(2,1)}, f32[128,1024]{1,0:T(8,128)}, f32[128,1024]{1,0:T(8,128)}, f32[8,1024]{1,0:T(8,128)}, bf16[128,1024]{1,0:T(8,128)(2,1)}, /*index=5*/f32[128,1024]{1,0:T(8,128)}) custom-call(s32[2]{0:T(128)} %pad_add_fusion.scal_ref, bf16[2048,128]{1,0:T(8,128)(2,1)} %token_ref.1, f32[2048,128]{1,0:T(8,128)} %cot_ref.1, ...), custom_call_target="tpu_custom_call" | custom-call | flops 33554432 | bytes 3145728 | tf_op jit(solution)/shard_map/queries/pallas_call | solution.py:892
  58.1 0.0 collective-permute-done.6.other_ref
  58.1 0.6 copy-done.14
  58.7 12.8 %tokens.1 = (bf16[1024,128]{1,0:T(8,128)(2,1)}, f32[1024,128]{1,0:T(8,128)}, f32[72,128]{1,0:T(8,128)}, f32[72,128]{1,0:T(8,128)}, f32[128,128]{1,0:T(8,128)}, /...) custom-call(s32[2]{0:T(128)} %pad_add_fusion.scal_ref, ...), custom_call_target="tpu_custom_call" | custom-call | flops 1610612736 | bytes 3145728 | tf_op jit(solution)/shard_map/tokens/pallas_call | solution.py:932
  71.5 0.6 collective-permute-start.8
  72.1 1.1 collective-permute-done.8
  73.2 0.8 add.83
  73.9 1.6 %collective-permute-start.11 = (f32[72,128]{1,0:T(8,128)S(1)}, f32[72,128]{1,0:T(8,128)S(1)}, u32[]{:S(2)}, u32[]{:S(2)}) collective-permute-start(f32[72,128]{1,0:T(8,128)S(1)} %add.83), channel_id=1, source_target_pairs={{0,3},{1,2},{2,1},{3,0},{4,7},{5,6},{6,5},{7,4},{8,11},{9,10},{10,... | collective-permute-start | bytes 110600 | tf_op jit(solution)/shard_map/ppermute | solution.py:723
  75.6 1.1 collective-permute-start.10
  76.7 0.8 collective-permute-start.9
  77.4 0.0 collective-permute-start.17
  77.4 2.9 %pack.1 = (f32[16,80,128]{2,1,0:T(8,128)}, bf16[16,80,128]{2,1,0:T(8,128)(2,1)}) custom-call(s32[2]{0:T(128)} %pad_add_fusion.scal_ref, f32[128,128]{1,0:T(8,128)} %get-tuple-element.72.g_query_ref, f32[144,128]{1,0:T(8,128)} %get-tuple-element.73.g_out_ref, f32[4,144,256]{2,1,0:T(8,128)} %get-tuple-element.74.g_up_ref, ...), custom_call_target="tpu_custom_call" | custom-call | bytes 4194304 | tf_op jit(solution)/shard_map/pack/pallas_call | solution.py:1019
  80.3 0.5 collective-permute-start.15
  80.8 0.0 collective-permute-done.11
  80.8 0.0 collective-permute-done.10
  80.8 0.0 collective-permute-done.9
  80.9 1.9 %collective-permute-start.14 = (f32[72,128]{1,0:T(8,128)S(1)}, f32[72,128]{1,0:T(8,128)S(1)}, u32[]{:S(2)}, u32[]{:S(2)}) collective-permute-start(f32[72,128]{1,0:T(8,128)S(1)} %add_add_fusion.1), channel_id=1, source_target_pairs={{0,12},{1,13},{2,14},{3,15},{4,8},{5,9},{6,10},{7,11},{8,4},{9,5},... | collective-permute-start | bytes 110600 | tf_op jit(solution)/shard_map/ppermute | solution.py:723
  82.8 0.8 collective-permute-start.13
  83.6 1.7 %collective-permute-start.12 = (f32[72,128]{1,0:T(8,128)S(1)}, f32[72,128]{1,0:T(8,128)S(1)}, u32[]{:S(2)}, u32[]{:S(2)}) collective-permute-start(f32[72,128]{1,0:T(8,128)S(1)} %add_add_fusion.1), channel_id=1, source_target_pairs={{0,4},{1,5},{2,6},{3,7},{4,0},{5,1},{6,2},{7,3},{8,12},{9,13},{10,... | collective-permute-start | bytes 110600 | tf_op jit(solution)/shard_map/ppermute | solution.py:723
  85.3 1.4 %collective-permute-done.14 = f32[72,128]{1,0:T(8,128)S(1)} collective-permute-done((f32[72,128]{1,0:T(8,128)S(1)}, f32[72,128]{1,0:T(8,128)S(1)}, u32[]{:S(2)}, u32[]{:S(2)}) %collective-permute-start.14) | collective-permute-done | bytes 36896 | tf_op jit(solution)/shard_map/ppermute | solution.py:723
  86.7 1.3 %collective-permute-done.13 = f32[72,128]{1,0:T(8,128)S(1)} collective-permute-done((f32[72,128]{1,0:T(8,128)S(1)}, f32[72,128]{1,0:T(8,128)S(1)}, u32[]{:S(2)}, u32[]{:S(2)}) %collective-permute-start.13) | collective-permute-done | bytes 36896 | tf_op jit(solution)/shard_map/ppermute | solution.py:723
  88.0 0.2 collective-permute-done.12
  88.2 0.6 add_add_fusion.msg_ref
  88.9 0.7 copy-done.6
  89.5 0.2 copy-done.3
  89.7 0.2 copy-done.1
  89.9 11.4 %sample_backward.1 = (bf16[16,112,128]{2,1,0:T(8,128)(2,1)}, bf16[2,1024,128]{2,1,0:T(8,128)(2,1)}, f32[2,1024,128]{2,1,0:T(8,128)}) custom-call(s32[2]{0:T(128)} %pad_add_fusion.scal_ref, s32[1,4]{1,0:T(1,128)} %count_ref.5, f32[72,128]{1,0:T(8,128)} %add_add_fusion.msg_ref, f32[1,3,4096]{2,1,0:T(4,128)} %copy.20.func_ref, ...), custom_call_target="tpu_custom_call" | custom-call | flops 1073741824 | bytes 6291456 | tf_op jit(solution)/shard_map/sample_backward/pallas_call | solution.py:1037
  101.2 4.4 %all-to-all-start.1 = ((bf16[16,112,128]{2,1,0:T(8,128)(2,1)}), bf16[16,112,128]{2,1,0:T(8,128)(2,1)S(1)}, u32[]{:S(2)}, u32[]{:S(2)}) async-start(bf16[16,112,128]{2,1,0:T(8,128)(2,1)} %get-tuple-element.83), calls=%async_computation.1 | async-start | bytes 917504 | tf_op jit(solution)/shard_map/all_to_all | solution.py:1109
  105.7 13.5 %all-to-all-done.1 = bf16[16,112,128]{2,1,0:T(8,128)(2,1)S(1)} async-done(((bf16[16,112,128]{2,1,0:T(8,128)(2,1)}), bf16[16,112,128]{2,1,0:T(8,128)(2,1)S(1)}, u32[]{:S(2)}, u32[]{:S(2)}) %all-to-all-start.1) | async-done | bytes 458784 | tf_op jit(solution)/shard_map/all_to_all | solution.py:1109
  119.2 0.1 convert_reduce_fusion
  119.3 0.0 copy-start.4
  119.3 0.0 copy-start.7
  119.3 0.1 collective-permute-start.18
  119.4 0.5 copy-done.12
  119.9 0.0 copy-done.13
  119.9 0.7 multiply_subtract_fusion.1
  120.7 0.7 multiply_subtract_fusion
  (31 shorter events, 0.2 us)
Async XLA Ops:
  0.6 0.7 copy-start.9
  3.1 8.5 %copy-start.10 = (f32[1,3,4096]{2,0,1:T(1,128)S(1)}, f32[1,3,4096]{2,0,1:T(1,128)}, u32[]{:S(2)}) copy-start(f32[1,3,4096]{2,0,1:T(1,128)} %param.13) | copy-start | bytes 147460
  3.1 22.3 %all-to-all-start = ((bf16[16,112,128]{2,1,0:T(8,128)(2,1)}), bf16[16,112,128]{2,1,0:T(8,128)(2,1)S(1)}, u32[]{:S(2)}, u32[]{:S(2)}) async-start(bf16[16,112,128]{2,1,0:T(8,128)(2,1)} %broadcast_in_dim.8), calls=%async_computation | async-start | bytes 917504 | tf_op jit(solution)/shard_map/all_to_all | solution.py:776
  25.5 0.8 copy-start
  36.8 5.2 %collective-permute-start.2 = (f32[72,128]{1,0:T(8,128)}, f32[72,128]{1,0:T(8,128)S(1)}, u32[]{:S(2)}, u32[]{:S(2)}) collective-permute-start(f32[72,128]{1,0:T(8,128)} %get-tuple-element.46), channel_id=1, source_target_pairs={{0,3},{1,2},{2,1},{3,0},{4,7},{5,6},{6,5},{7,4},{8,11},{9,10},{10,... | collective-permute-start | bytes 110600 | tf_op jit(solution)/shard_map/ppermute | solution.py:723
  38.0 4.4 %collective-permute-start.1 = (f32[72,128]{1,0:T(8,128)}, f32[72,128]{1,0:T(8,128)S(1)}, u32[]{:S(2)}, u32[]{:S(2)}) collective-permute-start(f32[72,128]{1,0:T(8,128)} %get-tuple-element.46), channel_id=1, source_target_pairs={{0,2},{1,3},{2,0},{3,1},{4,6},{5,7},{6,4},{7,5},{8,10},{9,11},{10,... | collective-permute-start | bytes 110600 | tf_op jit(solution)/shard_map/ppermute | solution.py:723
  38.9 4.2 %collective-permute-start = (f32[72,128]{1,0:T(8,128)}, f32[72,128]{1,0:T(8,128)S(1)}, u32[]{:S(2)}, u32[]{:S(2)}) collective-permute-start(f32[72,128]{1,0:T(8,128)} %get-tuple-element.46), channel_id=1, source_target_pairs={{0,1},{1,0},{2,3},{3,2},{4,5},{5,4},{6,7},{7,6},{8,9},{9,8},{10,11... | collective-permute-start | bytes 110600 | tf_op jit(solution)/shard_map/ppermute | solution.py:723
  40.4 10.8 %collective-permute-start.7 = (bf16[16,112,128]{2,1,0:T(8,128)(2,1)}, bf16[16,112,128]{2,1,0:T(8,128)(2,1)S(1)}, u32[]{:S(2)}, u32[]{:S(2)}) collective-permute-start(bf16[16,112,128]{2,1,0:T(8,128)(2,1)} %copy-done), channel_id=1, source_target_pairs={{0,16},{16,0},{1,17},{17,1},{2,18},{18,2},{3,19},{19,3},{4,20},{20... | collective-permute-start | bytes 1376264 | tf_op jit(solution)/shard_map/ppermute | solution.py:732
  43.9 5.8 %collective-permute-start.5 = (f32[72,128]{1,0:T(8,128)S(1)}, f32[72,128]{1,0:T(8,128)S(1)}, u32[]{:S(2)}, u32[]{:S(2)}) collective-permute-start(f32[72,128]{1,0:T(8,128)S(1)} %add_add_fusion.3), channel_id=1, source_target_pairs={{0,12},{1,13},{2,14},{3,15},{4,8},{5,9},{6,10},{7,11},{8,4},{9,5},... | collective-permute-start | bytes 110600 | tf_op jit(solution)/shard_map/ppermute | solution.py:723
  45.5 5.2 %collective-permute-start.4 = (f32[72,128]{1,0:T(8,128)S(1)}, f32[72,128]{1,0:T(8,128)S(1)}, u32[]{:S(2)}, u32[]{:S(2)}) collective-permute-start(f32[72,128]{1,0:T(8,128)S(1)} %add_add_fusion.3), channel_id=1, source_target_pairs={{0,8},{1,9},{2,10},{3,11},{4,12},{5,13},{6,14},{7,15},{8,0},{9,1},... | collective-permute-start | bytes 110600 | tf_op jit(solution)/shard_map/ppermute | solution.py:723
  46.8 4.3 %collective-permute-start.3 = (f32[72,128]{1,0:T(8,128)S(1)}, f32[72,128]{1,0:T(8,128)S(1)}, u32[]{:S(2)}, u32[]{:S(2)}) collective-permute-start(f32[72,128]{1,0:T(8,128)S(1)} %add_add_fusion.3), channel_id=1, source_target_pairs={{0,4},{1,5},{2,6},{3,7},{4,0},{5,1},{6,2},{7,3},{8,12},{9,13},{10,... | collective-permute-start | bytes 110600 | tf_op jit(solution)/shard_map/ppermute | solution.py:723
  51.1 3.5 %copy-start.11 = (f32[72,128]{1,0:T(8,128)}, f32[72,128]{1,0:T(8,128)S(1)}, u32[]{:S(2)}) copy-start(f32[72,128]{1,0:T(8,128)S(1)} %add_add_fusion.2.own_ref) | copy-start | bytes 110596
  51.1 7.0 %collective-permute-start.6 = (f32[72,128]{1,0:T(8,128)S(1)}, f32[72,128]{1,0:T(8,128)S(1)}, u32[]{:S(2)}, u32[]{:S(2)}) collective-permute-start(f32[72,128]{1,0:T(8,128)S(1)} %add_add_fusion.2.own_ref), channel_id=1, source_target_pairs={{0,16},{16,0},{1,17},{17,1},{2,18},{18,2},{3,19},{19,3},{4,20},{20... | collective-permute-start | bytes 110600 | tf_op jit(solution)/shard_map/ppermute | solution.py:732
  51.2 0.8 copy-start.2
  58.1 0.6 copy-start.14
  71.5 1.6 %collective-permute-start.8 = (f32[72,128]{1,0:T(8,128)}, f32[72,128]{1,0:T(8,128)S(1)}, u32[]{:S(2)}, u32[]{:S(2)}) collective-permute-start(f32[72,128]{1,0:T(8,128)} %get-tuple-element.63), channel_id=1, source_target_pairs={{0,16},{16,0},{1,17},{17,1},{2,18},{18,2},{3,19},{19,3},{4,20},{20... | collective-permute-start | bytes 110600 | tf_op jit(solution)/shard_map/ppermute | solution.py:732
  73.9 6.9 %collective-permute-start.11 = (f32[72,128]{1,0:T(8,128)S(1)}, f32[72,128]{1,0:T(8,128)S(1)}, u32[]{:S(2)}, u32[]{:S(2)}) collective-permute-start(f32[72,128]{1,0:T(8,128)S(1)} %add.83), channel_id=1, source_target_pairs={{0,3},{1,2},{2,1},{3,0},{4,7},{5,6},{6,5},{7,4},{8,11},{9,10},{10,... | collective-permute-start | bytes 110600 | tf_op jit(solution)/shard_map/ppermute | solution.py:723
  75.6 5.3 %collective-permute-start.10 = (f32[72,128]{1,0:T(8,128)S(1)}, f32[72,128]{1,0:T(8,128)S(1)}, u32[]{:S(2)}, u32[]{:S(2)}) collective-permute-start(f32[72,128]{1,0:T(8,128)S(1)} %add.83), channel_id=1, source_target_pairs={{0,2},{1,3},{2,0},{3,1},{4,6},{5,7},{6,4},{7,5},{8,10},{9,11},{10,... | collective-permute-start | bytes 110600 | tf_op jit(solution)/shard_map/ppermute | solution.py:723
  76.7 4.2 %collective-permute-start.9 = (f32[72,128]{1,0:T(8,128)S(1)}, f32[72,128]{1,0:T(8,128)S(1)}, u32[]{:S(2)}, u32[]{:S(2)}) collective-permute-start(f32[72,128]{1,0:T(8,128)S(1)} %add.83), channel_id=1, source_target_pairs={{0,1},{1,0},{2,3},{3,2},{4,5},{5,4},{6,7},{7,6},{8,9},{9,8},{10,11... | collective-permute-start | bytes 110600 | tf_op jit(solution)/shard_map/ppermute | solution.py:723
  77.4 11.4 %collective-permute-start.17 = (f32[1024,128]{1,0:T(8,128)}, f32[1024,128]{1,0:T(8,128)S(1)}, u32[]{:S(2)}, u32[]{:S(2)}) collective-permute-start(f32[1024,128]{1,0:T(8,128)} %get-tuple-element.80.grad_own_ref), channel_id=1, source_target_pairs={{0,16},{16,0},{1,17},{17,1},{2,18},{18,2},{3,19},{19,3},{4,20},{20... | collective-permute-start | bytes 1572872 | tf_op jit(solution)/shard_map/ppermute | solution.py:732
  77.4 9.3 %copy-start.5 = (bf16[1024,128]{1,0:T(8,128)(2,1)S(1)}, bf16[1024,128]{1,0:T(8,128)(2,1)}, u32[]{:S(2)}) copy-start(bf16[1024,128]{1,0:T(8,128)(2,1)} %get-tuple-element.79.out_own_ref) | copy-start | bytes 786436
  80.3 8.5 %collective-permute-start.15 = (bf16[16,80,128]{2,1,0:T(8,128)(2,1)}, bf16[16,80,128]{2,1,0:T(8,128)(2,1)S(1)}, u32[]{:S(2)}, u32[]{:S(2)}) collective-permute-start(bf16[16,80,128]{2,1,0:T(8,128)(2,1)} %get-tuple-element.78), channel_id=1, source_target_pairs={{0,16},{16,0},{1,17},{17,1},{2,18},{18,2},{3,19},{19,3},{4,20},{20... | collective-permute-start | bytes 983048 | tf_op jit(solution)/shard_map/ppermute | solution.py:732
  80.9 5.8 %collective-permute-start.14 = (f32[72,128]{1,0:T(8,128)S(1)}, f32[72,128]{1,0:T(8,128)S(1)}, u32[]{:S(2)}, u32[]{:S(2)}) collective-permute-start(f32[72,128]{1,0:T(8,128)S(1)} %add_add_fusion.1), channel_id=1, source_target_pairs={{0,12},{1,13},{2,14},{3,15},{4,8},{5,9},{6,10},{7,11},{8,4},{9,5},... | collective-permute-start | bytes 110600 | tf_op jit(solution)/shard_map/ppermute | solution.py:723
  82.8 5.2 %collective-permute-start.13 = (f32[72,128]{1,0:T(8,128)S(1)}, f32[72,128]{1,0:T(8,128)S(1)}, u32[]{:S(2)}, u32[]{:S(2)}) collective-permute-start(f32[72,128]{1,0:T(8,128)S(1)} %add_add_fusion.1), channel_id=1, source_target_pairs={{0,8},{1,9},{2,10},{3,11},{4,12},{5,13},{6,14},{7,15},{8,0},{9,1},... | collective-permute-start | bytes 110600 | tf_op jit(solution)/shard_map/ppermute | solution.py:723
  83.6 4.6 %collective-permute-start.12 = (f32[72,128]{1,0:T(8,128)S(1)}, f32[72,128]{1,0:T(8,128)S(1)}, u32[]{:S(2)}, u32[]{:S(2)}) collective-permute-start(f32[72,128]{1,0:T(8,128)S(1)} %add_add_fusion.1), channel_id=1, source_target_pairs={{0,4},{1,5},{2,6},{3,7},{4,0},{5,1},{6,2},{7,3},{8,12},{9,13},{10,... | collective-permute-start | bytes 110600 | tf_op jit(solution)/shard_map/ppermute | solution.py:723
  86.7 2.2 %collective-permute-start.16 = (bf16[1024,128]{1,0:T(8,128)(2,1)S(1)}, bf16[1024,128]{1,0:T(8,128)(2,1)S(1)}, u32[]{:S(2)}, u32[]{:S(2)}) collective-permute-start(bf16[1024,128]{1,0:T(8,128)(2,1)S(1)} %copy-done.5), channel_id=1, source_target_pairs={{0,16},{16,0},{1,17},{17,1},{2,18},{18,2},{3,19},{19,3},{4,20},{20... | collective-permute-start | bytes 786440 | tf_op jit(solution)/shard_map/ppermute | solution.py:732
  88.8 0.7 copy-start.6
  88.9 0.8 copy-start.3
  88.9 1.0 copy-start.1
  101.2 18.0 %all-to-all-start.1 = ((bf16[16,112,128]{2,1,0:T(8,128)(2,1)}), bf16[16,112,128]{2,1,0:T(8,128)(2,1)S(1)}, u32[]{:S(2)}, u32[]{:S(2)}) async-start(bf16[16,112,128]{2,1,0:T(8,128)(2,1)} %get-tuple-element.83), calls=%async_computation.1 | async-start | bytes 917504 | tf_op jit(solution)/shard_map/all_to_all | solution.py:1109
  119.2 0.7 copy-start.12
  119.2 0.7 copy-start.13
  119.2 1.4 %copy-start.8 = (f32[18568]{0:T(1024)S(1)}, f32[18568]{0:T(1024)}, u32[]{:S(2)}) copy-start(f32[18568]{0:T(1024)} %param.20) | copy-start | bytes 222820
  119.3 1.4 %copy-start.4 = (f32[18568]{0:T(1024)S(1)}, f32[18568]{0:T(1024)}, u32[]{:S(2)}) copy-start(f32[18568]{0:T(1024)} %param.18) | copy-start | bytes 222820
  119.3 1.3 %copy-start.7 = (f32[18568]{0:T(1024)S(1)}, f32[18568]{0:T(1024)}, u32[]{:S(2)}) copy-start(f32[18568]{0:T(1024)} %param.19) | copy-start | bytes 222820
  119.3 1.3 %collective-permute-start.18 = (f32[10240]{0:T(1024)S(1)}, f32[10240]{0:T(1024)S(1)}, u32[]{:S(2)}, u32[]{:S(2)}) collective-permute-start(f32[10240]{0:T(1024)S(1)} %slice_bitcast_fusion), channel_id=1, source_target_pairs={{0,16},{16,0},{1,17},{17,1},{2,18},{18,2},{3,19},{19,3},{4,20},{20... | collective-permute-start | bytes 122888 | tf_op jit(solution)/shard_map/ppermute | solution.py:732

commit v2 on v1

--- a/solution.py
+++ b/solution.py
@@ -24,9 +24,10 @@
 EPS_ADAM = 1e-08
 
 LANES = 128
-VMEM_LIMIT = 56 * 1024 * 1024
-SAMPLE_TILE = 512
-TOKEN_TILE = 512
+VMEM_BASE = 15 * 1024 * 1024
+VMEM_ITEM = 768 * 1024
+SAMPLE_TILE = 1024
+TOKEN_TILE = 1024
 
 F32 = jnp.float32
 BF16 = jnp.bfloat16
@@ -322,17 +323,17 @@
     vec_ref,
     tmp_ref,
 ):
-    parts, shard, half, offset = plan
+    parts, shard, half = plan
     core = scal_ref[0]
     own_at = pl.multiple_of(8 + core * half, 8)
     other_at = pl.multiple_of(8 + (1 - core) * half, 8)
     for number in range(parts):
         shift = (number * shard) % LANES
         tmp_ref[pl.ds(own_at, half), :] = turned(
-            own_ref[number, offset : offset + half, :].astype(F32), shift
+            own_ref[number].astype(F32), shift
         )
         tmp_ref[pl.ds(other_at, half), :] = turned(
-            other_ref[number, offset : offset + half, :].astype(F32), shift
+            other_ref[number].astype(F32), shift
         )
         put_shard(vec_ref, tmp_ref, number, shard, 2 * half)
     query = vec_ref[ROW_QUERY : ROW_QUERY + D, :]
@@ -615,8 +616,6 @@
     slope_two_ref,
     hid_ref,
     pair_ref,
-    own_ref,
-    other_ref,
     out_own_ref,
     out_other_ref,
     grad_own_ref,
@@ -709,23 +708,29 @@
                 :, part * D : (part + 1) * D
             ]
         for number in range(parts):
-            send_ref[number, :height, :] = take_shard(vec_ref, number, shard, height).astype(BF16)
-            send_ref[number, height:, :] = (
-                own_ref[number] + other_ref[number].astype(F32)
-            ).astype(BF16)
-
-
-def sum_over_points(values, count):
+            send_ref[number] = take_shard(vec_ref, number, shard, height).astype(BF16)
+
+
+def sum_over_points(values, count, besides):
     bit = 1
+    number = 0
     while bit < count:
         masks = [bit] if 2 * bit >= count else [bit, 2 * bit, 3 * bit]
         pieces = [
             lax.ppermute(values, "pts", [(source, source ^ mask) for source in range(count)])
             for mask in masks
         ]
+        if number < len(besides):
+            before = besides[number - 1] if number else None
+            pieces, besides[number] = lax.optimization_barrier((pieces, besides[number](before)))
         values = functools.reduce(jnp.add, pieces, values)
         bit *= 4
-    return values
+        number += 1
+    return values, besides
+
+
+def gather_blocks(block, count):
+    return lax.all_to_all(jnp.broadcast_to(block, (count,) + block.shape), "pts", 0, 0)
 
 
 def swap_cores(values):
@@ -763,7 +768,7 @@
     half = up_to(-(-shared_len // (2 * LANES)), 16)
     height = up_to(-(-branch_len // LANES), 16)
     msg_rows = items * HD + up_to(items, 8)
-    params = pltpu.CompilerParams(vmem_limit_bytes=VMEM_LIMIT)
+    params = pltpu.CompilerParams(vmem_limit_bytes=VMEM_BASE + items * VMEM_ITEM)
     shape = jax.ShapeDtypeStruct
 
     shared_pad = jnp.pad(shared_master.astype(BF16), (0, 2 * half * LANES - shared_len))
@@ -771,10 +776,9 @@
     branch_pad = jnp.pad(
         branch_master.reshape(-1).astype(BF16), (0, height * LANES - branch_len)
     )
-    send = jnp.concatenate([branch_pad, shared_half]).reshape(1, height + half, LANES)
-    send = jnp.broadcast_to(send, (count, height + half, LANES))
-    recv = lax.all_to_all(send, "pts", 0, 0)
-    recv_other = swap_cores(recv)
+    recv_branch = gather_blocks(branch_pad.reshape(height, LANES), count)
+    recv_branch, shared_half = lax.optimization_barrier((recv_branch, shared_half))
+    recv_shared = gather_blocks(shared_half.reshape(half, LANES), count)
 
     tile = min(SAMPLE_TILE, slots)
     steps = slots // tile
@@ -825,12 +829,12 @@
         ),
         out_shape=[
             shape((msg_rows, LANES), F32),
-            shape((D, slots), BF16),
-            shape((D, slots), BF16),
-            shape((D, slots), BF16),
-            shape((D, slots), BF16),
-            shape((D, slots), BF16),
-            shape((D, slots), BF16),
+            pltpu.HBM((D, slots), BF16),
+            pltpu.HBM((D, slots), BF16),
+            pltpu.HBM((D, slots), BF16),
+            pltpu.HBM((D, slots), BF16),
+            pltpu.HBM((D, slots), BF16),
+            pltpu.HBM((D, slots), BF16),
             shape((D, D), BF16),
             shape((D, 2 * D), BF16),
         ],
@@ -839,49 +843,48 @@
             flops=slots * D * D * 10, bytes_accessed=slots * D * 12, transcendentals=slots * D * 3
         ),
         name="sample_forward",
-    )(scal, func_counts, recv, funcs)
-
-    summary = sum_over_points(msg, count)
-    summary_other = swap_cores(summary)
+    )(scal, func_counts, recv_branch, funcs)
 
     shared_rows = up_to(SHARED_ROWS + 2 * half + 8, 8)
-    (query_w, query_t, out_w, out_t, up_w, up_t, down_w, down_t, cols) = pl.pallas_call(
-        functools.partial(weight_kernel, (count, shared_len, half, height)),
-        in_specs=[
-            pl.BlockSpec(memory_space=pltpu.SMEM),
-            whole(recv.shape),
-            whole(recv.shape),
-        ],
-        out_specs=[
-            whole((D, D)),
-            whole((D, D)),
-            whole((D, D)),
-            whole((D, D)),
-            whole((E, D, FF)),
-            whole((E, FF, D)),
-            whole((E, FF, D)),
-            whole((E, D, FF)),
-            whole((D, D)),
-        ],
-        out_shape=[
-            shape((D, D), BF16),
-            shape((D, D), BF16),
-            shape((D, D), BF16),
-            shape((D, D), BF16),
-            shape((E, D, FF), BF16),
-            shape((E, FF, D), BF16),
-            shape((E, FF, D), BF16),
-            shape((E, D, FF), BF16),
-            shape((D, D), F32),
-        ],
-        scratch_shapes=[
-            pltpu.VMEM((shared_rows, LANES), F32),
-            pltpu.VMEM((max(8 + 2 * half, D) + 8, LANES), F32),
-        ],
-        compiler_params=params,
-        cost_estimate=pl.CostEstimate(flops=0, bytes_accessed=8 << 20, transcendentals=0),
-        name="weights",
-    )(scal, recv, recv_other)
+
+    def make_weights():
+        return pl.pallas_call(
+            functools.partial(weight_kernel, (count, shared_len, half)),
+            in_specs=[
+                pl.BlockSpec(memory_space=pltpu.SMEM),
+                whole(recv_shared.shape),
+                whole(recv_shared.shape),
+            ],
+            out_specs=[
+                whole((D, D)),
+                whole((D, D)),
+                whole((D, D)),
+                whole((D, D)),
+                whole((E, D, FF)),
+                whole((E, FF, D)),
+                whole((E, FF, D)),
+                whole((E, D, FF)),
+                whole((D, D)),
+            ],
+            out_shape=[
+                shape((D, D), BF16),
+                shape((D, D), BF16),
+                shape((D, D), BF16),
+                shape((D, D), BF16),
+                shape((E, D, FF), BF16),
+                shape((E, FF, D), BF16),
+                shape((E, FF, D), BF16),
+                shape((E, D, FF), BF16),
+                shape((D, D), F32),
+            ],
+            scratch_shapes=[
+                pltpu.VMEM((shared_rows, LANES), F32),
+                pltpu.VMEM((max(8 + 2 * half, D) + 8, LANES), F32),
+            ],
+            compiler_params=params,
+            cost_estimate=pl.CostEstimate(flops=0, bytes_accessed=8 << 20, transcendentals=0),
+            name="weights",
+        )(scal, recv_shared, recv_other)
 
     token_tile = min(TOKEN_TILE, rows)
     token_steps = rows // token_tile
@@ -889,35 +892,47 @@
         (token_tile, D), lambda i, scal_ref: (scal_ref[0] * token_steps + i, 0)
     )
     token_stream = lambda height_: pl.BlockSpec((height_, token_tile), lambda i, *_: (0, i))
-    (token_t, cot_t, unit, scale, norm, soft) = pl.pallas_call(
-        query_kernel,
-        grid_spec=pltpu.PrefetchScalarGridSpec(
-            num_scalar_prefetch=1,
-            grid=(token_steps,),
-            in_specs=[row_block, row_block, whole((D, D)), whole((D, D))],
-            out_specs=[
-                token_stream(D),
-                token_stream(D),
-                token_stream(D),
-                token_stream(8),
-                token_stream(D),
-                token_stream(D),
-            ],
-        ),
-        out_shape=[
-            shape((D, rows), BF16),
-            shape((D, rows), F32),
-            shape((D, rows), F32),
-            shape((8, rows), F32),
-            shape((D, rows), BF16),
-            shape((D, rows), F32),
-        ],
-        compiler_params=params,
-        cost_estimate=pl.CostEstimate(
-            flops=rows * D * D * 2, bytes_accessed=rows * D * 24, transcendentals=rows * D
-        ),
-        name="queries",
-    )(scal, tokens, cotangent, query_t, cols)
+
+    def make_queries(weights):
+        return pl.pallas_call(
+            query_kernel,
+            grid_spec=pltpu.PrefetchScalarGridSpec(
+                num_scalar_prefetch=1,
+                grid=(token_steps,),
+                in_specs=[row_block, row_block, whole((D, D)), whole((D, D))],
+                out_specs=[
+                    token_stream(D),
+                    token_stream(D),
+                    token_stream(D),
+                    token_stream(8),
+                    token_stream(D),
+                    token_stream(D),
+                ],
+            ),
+            out_shape=[
+                shape((D, rows), BF16),
+                shape((D, rows), F32),
+                shape((D, rows), F32),
+                shape((8, rows), F32),
+                shape((D, rows), BF16),
+                shape((D, rows), F32),
+            ],
+            compiler_params=params,
+            cost_estimate=pl.CostEstimate(
+                flops=rows * D * D * 2, bytes_accessed=rows * D * 24, transcendentals=rows * D
+            ),
+            name="queries",
+        )(scal, tokens, cotangent, weights[1], weights[8])
+
+    msg, recv_shared = lax.optimization_barrier((msg, recv_shared))
+    recv_other = swap_cores(recv_shared)
+    weights = make_weights()
+    summary, (weights, queries) = sum_over_points(
+        msg, count, [lambda _: weights, make_queries]
+    )
+    query_w, query_t, out_w, out_t, up_w, up_t, down_w, down_t, cols = weights
+    token_t, cot_t, unit, scale, norm, soft = queries
+    summary_other = swap_cores(summary)
 
     (
         output_own,
@@ -1012,14 +1027,13 @@
         cols,
     )
 
-    summary_grad = sum_over_points(own_msg + swap_cores(other_msg), count)
-    output_other = swap_cores(output_own)
-    grad_other = swap_cores(grad_own)
-
+    both_msg, parts = lax.optimization_barrier(
+        (own_msg + swap_cores(other_msg), (g_query, g_out, g_up, g_down, g_vec))
+    )
     half_own, half_other = pl.pallas_call(
         functools.partial(pack_kernel, (count, shared_len, half)),
         in_specs=[pl.BlockSpec(memory_space=pltpu.SMEM)]
-        + [whole(piece.shape) for piece in (g_query, g_out, g_up, g_down, g_vec)],
+        + [whole(piece.shape) for piece in parts],
         out_specs=[whole((count, half, LANES)), whole((count, half, LANES))],
         out_shape=[shape((count, half, LANES), F32), shape((count, half, LANES), BF16)],
         scratch_shapes=[
@@ -1027,13 +1041,30 @@
             pltpu.VMEM((2 * half, LANES), F32),
         ],
         compiler_params=params,
-        cost_estimate=pl.CostEstimate(flops=0, bytes_accessed=4 << 20, transcendentals=0),
+        cost_estimate=pl.CostEstimate(flops=2 << 30, bytes_accessed=4 << 20, transcendentals=0),
         name="pack",
-    )(scal, g_query, g_out, g_up, g_down, g_vec)
-    half_other = swap_cores(half_other)
-
+    )(scal, *parts)
+
+    def add_halves(packed):
+        return (packed[0] + swap_cores(packed[1]).astype(F32)).astype(BF16)
+
+    output_other = swap_cores(output_own)
+    grad_other = swap_cores(grad_own)
+    packed = [half_own, half_other]
+    summary_grad, (_, half_sum) = sum_over_points(
+        both_msg,
+        count,
+        [lambda _: packed, lambda ready: (add_halves(ready), output_other, grad_other)],
+    )
+    half_sum, output_other, grad_other = half_sum
+    summary_grad, half_sum = lax.optimization_barrier((summary_grad, half_sum))
+    keys, vals, first, second, slope_one, slope_two = (
+        pltpu.with_memory_space_constraint(kept, pltpu.HBM)
+        for kept in (keys, vals, first, second, slope_one, slope_two)
+    )
     piece = pl.BlockSpec((rows // steps, D), lambda i, *_: (i, 0))
     both = pl.BlockSpec((2, rows // steps, D), lambda i, *_: (0, i, 0))
+    shared_recv = lax.all_to_all(half_sum, "pts", 0, 0)
     grads_send, output, token_grad = pl.pallas_call(
         functools.partial(
             sample_backward_kernel,
@@ -1054,14 +1085,12 @@
                 stream(D),
                 whole((D, D)),
                 whole((D, 2 * D)),
-                whole((count, half, LANES)),
-                whole((count, half, LANES)),
                 piece,
                 piece,
                 piece,
                 piece,
             ],
-            out_specs=[whole((count, height + half, LANES)), both, both],
+            out_specs=[whole((count, height, LANES)), both, both],
             scratch_shapes=[
                 pltpu.VMEM((vec_rows, LANES), F32),
                 pltpu.VMEM((items, D, D), BF16),
@@ -1076,13 +1105,13 @@
             ],
         ),
         out_shape=[
-            shape((count, height + half, LANES), BF16),
+            shape((count, height, LANES), BF16),
             shape((2, rows, D), BF16),
             shape((2, rows, D), F32),
         ],
         compiler_params=params,
         cost_estimate=pl.CostEstimate(
-            flops=slots * D * D * 16, bytes_accessed=slots * D * 12, transcendentals=0
+            flops=slots * D * D * 300, bytes_accessed=slots * D * 12, transcendentals=0
         ),
         name="sample_backward",
     )(
@@ -1098,23 +1127,22 @@
         slope_two,
         hid_w,
         pair_w,
-        half_own,
-        half_other,
         output_own,
         output_other,
         grad_own,
         grad_other,
     )
 
-    grads = jnp.sum(lax.all_to_all(grads_send, "pts", 0, 0).astype(F32), axis=0)
-    own_half = grads[height:].reshape(-1)
+    grads_send, shared_recv = lax.optimization_barrier((grads_send, shared_recv))
+    own_half = jnp.sum(shared_recv.astype(F32), axis=0).reshape(-1)
     other_half = swap_cores(own_half)
     shared_grad = jnp.where(
         core == 0,
         jnp.concatenate([own_half, other_half]),
         jnp.concatenate([other_half, own_half]),
     )[:shared_len]
-    branch_grad = grads[:height].reshape(1, -1)[:, :branch_len]
+    branch_recv = lax.all_to_all(grads_send, "pts", 0, 0)
+    branch_grad = jnp.sum(branch_recv.astype(F32), axis=0).reshape(1, -1)[:, :branch_len]
     new_branch, new_branch_m, new_branch_v = adam_step(
         branch_master, branch_m, branch_v, branch_grad
     )

time: 122 us -> 102 us (0.84)
  Pallas kernels: 43.8 us -> 27.3 us
  starting transfers between devices: 30 us -> 37 us
  waiting for transfers between devices: 35.5 us -> 30.6 us
  local copies, waits for them, and re-layouts: 5.91 us -> 2.13 us
  other arithmetic: 5.22 us -> 3.2 us
    all_to_all x2 -> x4, starting transfers between devices: 12.9 us -> 20.3 us  [the longest x2 12.1 us: gather_blocks(): lax.all_to_all(jnp.broadcast_to(block, (count,) + block.shape), 'pts', 0, 0)]
    all_to_all x2 -> x4, waiting for transfers between devices: 26.1 us -> 20.1 us  [the longest x2 9.3 us: gather_blocks(): lax.all_to_all(jnp.broadcast_to(block, (count,) + block.shape), 'pts', 0, 0)]
    pallas_call x1, Pallas kernels: 12.8 us -> 8.4 us  [body(): pl.pallas_call(functools.partial(token_kernel, (token_tile, items, chip_r...]
    unnamed x31 -> x25, local copies, waits for them, and re-layouts: 5.06 us -> 0.66 us
    pallas_call x2, Pallas kernels: 6.13 us -> 2.3 us  [the longest x1 1.17 us: make_queries(): pl.pallas_call(query_kernel, grid_spec=pltpu.PrefetchScalarGridSpec(num_s...]
    pallas_call x1, Pallas kernels: 11.4 us -> 7.64 us  [body(): pl.pallas_call(functools.partial(sample_backward_kernel, (tile, items, co...]
    pallas_call x1, Pallas kernels: 10.6 us -> 7.82 us  [body(): pl.pallas_call(functools.partial(sample_forward_kernel, (tile, items, cou...]
    pallas_call x1, Pallas kernels: 2.88 us -> 1.09 us  [body(): pl.pallas_call(functools.partial(pack_kernel, (count, shared_len, half)),...]
  transfers between devices with their start and end apart: 21 -> 23, of which waited for: 12 -> 16; matrix products, arithmetic and copies ran while one was open for 3% -> 2% of each run, Pallas kernels for 7% -> 19%
where the time goes in v2:
time: 102 us; the launch traced here: 101 us
  starting transfers between devices  37 us (36%)
  waiting for transfers between devices  30.6 us (30%)
  Pallas kernels  27.3 us (27%)
  other arithmetic  3.2 us (3%)
  local copies, waits for them, and re-layouts  2.13 us (2%)
    ppermute x12, starting transfers between devices, sum_over_points(): lax.ppermute(values, 'pts', [(source, source ^ mask) for source in range(...  15.9 us
    all_to_all x2, starting transfers between devices, gather_blocks(): lax.all_to_all(jnp.broadcast_to(block, (count,) + block.shape), 'pts', 0, 0)  12.1 us
    all_to_all x2, waiting for transfers between devices, gather_blocks(): lax.all_to_all(jnp.broadcast_to(block, (count,) + block.shape), 'pts', 0, 0)  9.3 us
    pallas_call x1, Pallas kernels, body(): pl.pallas_call(functools.partial(token_kernel, (token_tile, items, chip_r...  8.4 us
    ppermute x12, waiting for transfers between devices, sum_over_points(): lax.ppermute(values, 'pts', [(source, source ^ mask) for source in range(...  8.25 us
    pallas_call x1, Pallas kernels, body(): pl.pallas_call(functools.partial(sample_forward_kernel, (tile, items, cou...  7.82 us
    pallas_call x1, Pallas kernels, body(): pl.pallas_call(functools.partial(sample_backward_kernel, (tile, items, co...  7.64 us
    all_to_all x1, waiting for transfers between devices, body(): branch_recv = lax.all_to_all(grads_send, 'pts', 0, 0)  7.49 us
  transfers between devices with their start and end apart: 23, of which 16 were waited for; matrix products, arithmetic and copies ran while one was open for 2% of the time, Pallas kernels for 19%

profile of v2, /device:TPU:0, one launch (start us, length us, event | category | flops | bytes accessed | tf_op | source)
XLA Modules:
  0.0 101.1 jit_solution(14971893210539382060)
XLA Ops:
  0.6 0.8 convert_reduce_fusion.2
  1.4 0.7 broadcast_in_dim.6
  2.1 8.4 %all-to-all-start = ((bf16[16,32,128]{2,1,0:T(8,128)(2,1)}), bf16[16,32,128]{2,1,0:T(8,128)(2,1)S(1)}, u32[]{:S(2)}, u32[]{:S(2)}) async-start(bf16[16,32,128]{2,1,0:T(8,128)(2,1)} %broadcast_in_dim.6), calls=%async_computation | async-start | bytes 262144 | tf_op jit(solution)/shard_map/all_to_all | solution.py:733
  10.6 7.7 %all-to-all-done.recv_ref = bf16[16,32,128]{2,1,0:T(8,128)(2,1)S(1)} async-done(((bf16[16,32,128]{2,1,0:T(8,128)(2,1)}), bf16[16,32,128]{2,1,0:T(8,128)(2,1)S(1)}, u32[]{:S(2)}, u32[]{:S(2)}) %all-to-all-start) | async-done | bytes 131104 | tf_op jit(solution)/shard_map/all_to_all | solution.py:733
  18.3 0.8 broadcast_in_dim.7
  19.1 3.7 %all-to-all-start.1 = ((bf16[16,80,128]{2,1,0:T(8,128)(2,1)}), bf16[16,80,128]{2,1,0:T(8,128)(2,1)S(1)}, u32[]{:S(2)}, u32[]{:S(2)}) async-start(bf16[16,80,128]{2,1,0:T(8,128)(2,1)} %broadcast_in_dim.7), calls=%async_computation.1 | async-start | bytes 655360 | tf_op jit(solution)/shard_map/all_to_all | solution.py:733
  22.8 0.0 copy-start.4
  22.8 0.1 pad_add_fusion.scal_ref
  22.9 0.6 copy-done.4
  23.5 7.8 %sample_forward.1 = (f32[72,128]{1,0:T(8,128)S(1)}, bf16[128,4096]{1,0:T(8,128)(2,1)}, bf16[128,4096]{1,0:T(8,128)(2,1)}, bf16[128,4096]{1,0:T(8,128)(2,1)}, bf1...) custom-call(s32[2]{0:T(128)S(1)} %pad_add_fusion.scal_ref, ...), custom_call_target="tpu_custom_call" | custom-call | flops 671088640 | bytes 6291456 | tf_op jit(solution)/shard_map/sample_forward/pallas_call | solution.py:797
  31.3 1.6 %all-to-all-done.1.own_ref = bf16[16,80,128]{2,1,0:T(8,128)(2,1)S(1)} async-done(((bf16[16,80,128]{2,1,0:T(8,128)(2,1)}), bf16[16,80,128]{2,1,0:T(8,128)(2,1)S(1)}, u32[]{:S(2)}, u32[]{:S(2)}) %all-to-all-start.1) | async-done | bytes 327712 | tf_op jit(solution)/shard_map/all_to_all | solution.py:733
  32.9 0.0 collective-permute-start.3
  32.9 1.3 %collective-permute-start.2 = (f32[72,128]{1,0:T(8,128)S(1)}, f32[72,128]{1,0:T(8,128)S(1)}, u32[]{:S(2)}, u32[]{:S(2)}) collective-permute-start(f32[72,128]{1,0:T(8,128)S(1)} %get-tuple-element.95), channel_id=1, source_target_pairs={{0,3},{1,2},{2,1},{3,0},{4,7},{5,6},{6,5},{7,4},{8,11},{9,10},{10,... | collective-permute-start | bytes 110600 | tf_op jit(solution)/shard_map/ppermute | solution.py:720
  34.2 0.7 collective-permute-start.1
  34.9 1.5 %collective-permute-start = (f32[72,128]{1,0:T(8,128)S(1)}, f32[72,128]{1,0:T(8,128)S(1)}, u32[]{:S(2)}, u32[]{:S(2)}) collective-permute-start(f32[72,128]{1,0:T(8,128)S(1)} %get-tuple-element.95), channel_id=1, source_target_pairs={{0,1},{1,0},{2,3},{3,2},{4,5},{5,4},{6,7},{7,6},{8,9},{9,8},{10,11... | collective-permute-start | bytes 110600 | tf_op jit(solution)/shard_map/ppermute | solution.py:720
  36.4 0.0 collective-permute-done.3.other_ref
  36.4 1.1 %weights.1 = (bf16[128,128]{1,0:T(8,128)(2,1)S(1)}, bf16[128,128]{1,0:T(8,128)(2,1)S(1)}, bf16[128,128]{1,0:T(8,128)(2,1)S(1)}, bf16[128,128]{1,0:T(8,128)(2,1)S...) custom-call(s32[2]{0:T(128)S(1)} %pad_add_fusion.scal_ref, ...), custom_call_target="tpu_custom_call" | custom-call | bytes 8388608 | tf_op jit(solution)/shard_map/weights/pallas_call | solution.py:851
  37.5 0.3 collective-permute-done.2
  37.8 0.7 collective-permute-done.1
  38.5 0.4 collective-permute-done
  38.9 3.5 %collective-permute-start.6 = (f32[72,128]{1,0:T(8,128)S(1)}, f32[72,128]{1,0:T(8,128)S(1)}, u32[]{:S(2)}, u32[]{:S(2)}) collective-permute-start(f32[72,128]{1,0:T(8,128)S(1)} %add_add_fusion.3), channel_id=1, source_target_pairs={{0,12},{1,13},{2,14},{3,15},{4,8},{5,9},{6,10},{7,11},{8,4},{9,5},... | collective-permute-start | bytes 110600 | tf_op jit(solution)/shard_map/ppermute | solution.py:720
  42.4 0.0 collective-permute-start.5
  42.4 1.0 collective-permute-start.4
  43.3 1.2 %queries.1 = (bf16[128,1024]{1,0:T(8,128)(2,1)S(1)}, f32[128,1024]{1,0:T(8,128)S(1)}, f32[128,1024]{1,0:T(8,128)S(1)}, f32[8,1024]{1,0:T(8,128)S(1)}, bf16[128,1...) custom-call(s32[2]{0:T(128)S(1)} %pad_add_fusion.scal_ref, bf16[2048,128]{1,0:T(8,128)(2,1)S(1)} %copy-done.1, ...), custom_call_target="tpu_custom_call" | custom-call | flops 33554432 | bytes 3145728 | tf_op jit(solution)/shard_map/queries/pallas_call | solution.py:897
  44.5 0.2 collective-permute-done.6
  44.7 2.5 %collective-permute-done.5 = f32[72,128]{1,0:T(8,128)S(1)} collective-permute-done((f32[72,128]{1,0:T(8,128)S(1)}, f32[72,128]{1,0:T(8,128)S(1)}, u32[]{:S(2)}, u32[]{:S(2)}) %collective-permute-start.5) | collective-permute-done | bytes 36896 | tf_op jit(solution)/shard_map/ppermute | solution.py:720
  47.2 0.0 collective-permute-done.4
  47.2 0.0 copy-start.3
  47.2 0.1 collective-permute-start.7
  47.3 1.2 %collective-permute-done.7.other_ref = f32[72,128]{1,0:T(8,128)S(1)} collective-permute-done((f32[72,128]{1,0:T(8,128)S(1)}, f32[72,128]{1,0:T(8,128)S(1)}, u32[]{:S(2)}, u32[]{:S(2)}) %collective-permute-start.7) | collective-permute-done | bytes 36896 | tf_op jit(solution)/shard_map/ppermute | solution.py:737
  48.5 8.4 %tokens.1 = (bf16[1024,128]{1,0:T(8,128)(2,1)S(1)}, f32[1024,128]{1,0:T(8,128)S(1)}, f32[72,128]{1,0:T(8,128)S(1)}, f32[72,128]{1,0:T(8,128)S(1)}, f32[128,128]{...) custom-call(s32[2]{0:T(128)S(1)} %pad_add_fusion.scal_ref, ...), custom_call_target="tpu_custom_call" | custom-call | flops 1610612736 | bytes 3145728 | tf_op jit(solution)/shard_map/tokens/pallas_call | solution.py:947
  56.9 0.2 collective-permute-start.8
  57.2 1.0 %collective-permute-done.8 = f32[72,128]{1,0:T(8,128)S(1)} collective-permute-done((f32[72,128]{1,0:T(8,128)S(1)}, f32[72,128]{1,0:T(8,128)S(1)}, u32[]{:S(2)}, u32[]{:S(2)}) %collective-permute-start.8) | collective-permute-done | bytes 36896 | tf_op jit(solution)/shard_map/ppermute | solution.py:737
  58.2 1.2 %collective-permute-start.11 = (f32[72,128]{1,0:T(8,128)S(1)}, f32[72,128]{1,0:T(8,128)S(1)}, u32[]{:S(2)}, u32[]{:S(2)}) collective-permute-start(f32[72,128]{1,0:T(8,128)S(1)} %add.86), channel_id=1, source_target_pairs={{0,3},{1,2},{2,1},{3,0},{4,7},{5,6},{6,5},{7,4},{8,11},{9,10},{10,... | collective-permute-start | bytes 110600 | tf_op jit(solution)/shard_map/ppermute | solution.py:720
  59.4 1.5 %collective-permute-start.10 = (f32[72,128]{1,0:T(8,128)S(1)}, f32[72,128]{1,0:T(8,128)S(1)}, u32[]{:S(2)}, u32[]{:S(2)}) collective-permute-start(f32[72,128]{1,0:T(8,128)S(1)} %add.86), channel_id=1, source_target_pairs={{0,2},{1,3},{2,0},{3,1},{4,6},{5,7},{6,4},{7,5},{8,10},{9,11},{10,... | collective-permute-start | bytes 110600 | tf_op jit(solution)/shard_map/ppermute | solution.py:720
  61.0 0.7 collective-permute-start.9
  61.7 1.1 %pack.1 = (f32[16,80,128]{2,1,0:T(8,128)S(1)}, bf16[16,80,128]{2,1,0:T(8,128)(2,1)S(1)}) custom-call(s32[2]{0:T(128)S(1)} %pad_add_fusion.scal_ref, f32[128,128]{1,0:T(8,128)S(1)} %get-tuple-element.141.g_query_ref, f32[144,128]{1,0:T(8,128)S(1)} %get-tuple-element.142.g_out_ref, f32[4,144,256]{2,1,0:T(8,128)S(1)} %get-tuple-element.143.g_up_ref, ...), custom_call_target="tpu_custom_call" | custom-call | flops 2147483648 | bytes 4194304 | tf_op jit(solution)/shard_map/pack/pallas_call | solution.py:1033
  62.8 0.3 collective-permute-done.11
  63.1 0.4 collective-permute-done.10
  63.5 1.5 %collective-permute-done.9 = f32[72,128]{1,0:T(8,128)S(1)} collective-permute-done((f32[72,128]{1,0:T(8,128)S(1)}, f32[72,128]{1,0:T(8,128)S(1)}, u32[]{:S(2)}, u32[]{:S(2)}) %collective-permute-start.9) | collective-permute-done | bytes 36896 | tf_op jit(solution)/shard_map/ppermute | solution.py:720
  64.9 0.0 collective-permute-start.15
  64.9 0.5 collective-permute-start.17
  65.4 0.0 collective-permute-start.16
  65.5 1.5 %collective-permute-start.14 = (f32[72,128]{1,0:T(8,128)S(1)}, f32[72,128]{1,0:T(8,128)S(1)}, u32[]{:S(2)}, u32[]{:S(2)}) collective-permute-start(f32[72,128]{1,0:T(8,128)S(1)} %add_add_fusion.1), channel_id=1, source_target_pairs={{0,12},{1,13},{2,14},{3,15},{4,8},{5,9},{6,10},{7,11},{8,4},{9,5},... | collective-permute-start | bytes 110600 | tf_op jit(solution)/shard_map/ppermute | solution.py:720
  66.9 0.7 collective-permute-start.13
  67.6 0.0 collective-permute-done.15
  67.6 2.3 %collective-permute-start.12 = (f32[72,128]{1,0:T(8,128)S(1)}, f32[72,128]{1,0:T(8,128)S(1)}, u32[]{:S(2)}, u32[]{:S(2)}) collective-permute-start(f32[72,128]{1,0:T(8,128)S(1)} %add_add_fusion.1), channel_id=1, source_target_pairs={{0,4},{1,5},{2,6},{3,7},{4,0},{5,1},{6,2},{7,3},{8,12},{9,13},{10,... | collective-permute-start | bytes 110600 | tf_op jit(solution)/shard_map/ppermute | solution.py:720
  69.9 0.8 add_convert_fusion
  70.7 0.7 collective-permute-done.14
  71.4 1.4 %collective-permute-done.13 = f32[72,128]{1,0:T(8,128)S(1)} collective-permute-done((f32[72,128]{1,0:T(8,128)S(1)}, f32[72,128]{1,0:T(8,128)S(1)}, u32[]{:S(2)}, u32[]{:S(2)}) %collective-permute-start.13) | collective-permute-done | bytes 36896 | tf_op jit(solution)/shard_map/ppermute | solution.py:720
  72.8 0.0 collective-permute-done.12
  72.8 0.0 collective-permute-done.16.out_other_ref
  72.8 4.4 %all-to-all-start.2 = ((bf16[16,80,128]{2,1,0:T(8,128)(2,1)}), bf16[16,80,128]{2,1,0:T(8,128)(2,1)S(1)}, u32[]{:S(2)}, u32[]{:S(2)}) async-start(bf16[16,80,128]{2,1,0:T(8,128)(2,1)} %add_convert_fusion), calls=%async_computation.2 | async-start | bytes 655360 | tf_op jit(solution)/shard_map/all_to_all | solution.py:1067
  77.3 7.6 %sample_backward.1 = (bf16[16,32,128]{2,1,0:T(8,128)(2,1)}, bf16[2,1024,128]{2,1,0:T(8,128)(2,1)}, f32[2,1024,128]{2,1,0:T(8,128)}) custom-call(s32[2]{0:T(128)S(1)} %pad_add_fusion.scal_ref, s32[1,4]{1,0:T(1,128)S(1)} %copy-done.4, f32[72,128]{1,0:T(8,128)S(1)} %add_add_fusion.msg_ref, f32[1,3,4096]{2,1,0:T(4,128)S(1)} %copy.20.func_ref, ...), custom_call_target="tpu_custom_call" | custom-call | flops 20132659200 | bytes 6291456 | tf_op jit(solution)/shard_map/sample_backward/pallas_call | solution.py:1068
  84.9 3.3 %all-to-all-done.2 = bf16[16,80,128]{2,1,0:T(8,128)(2,1)S(1)} async-done(((bf16[16,80,128]{2,1,0:T(8,128)(2,1)}), bf16[16,80,128]{2,1,0:T(8,128)(2,1)S(1)}, u32[]{:S(2)}, u32[]{:S(2)}) %all-to-all-start.2) | async-done | bytes 327712 | tf_op jit(solution)/shard_map/all_to_all | solution.py:1067
  88.2 0.1 convert_reduce_fusion
  88.3 0.1 collective-permute-start.18
  88.4 0.0 copy-start.6
  88.4 0.0 copy-start.7
  88.4 3.7 %all-to-all-start.3 = ((bf16[16,32,128]{2,1,0:T(8,128)(2,1)}), bf16[16,32,128]{2,1,0:T(8,128)(2,1)S(1)}, u32[]{:S(2)}, u32[]{:S(2)}) async-start(bf16[16,32,128]{2,1,0:T(8,128)(2,1)} %get-tuple-element.175), calls=%async_computation.3 | async-start | bytes 262144 | tf_op jit(solution)/shard_map/all_to_all | solution.py:1144
  92.1 0.0 collective-permute-done.18
  92.2 0.7 multiply_subtract_fusion
  92.9 7.5 %all-to-all-done.3 = bf16[16,32,128]{2,1,0:T(8,128)(2,1)S(1)} async-done(((bf16[16,32,128]{2,1,0:T(8,128)(2,1)}), bf16[16,32,128]{2,1,0:T(8,128)(2,1)S(1)}, u32[]{:S(2)}, u32[]{:S(2)}) %all-to-all-start.3) | async-done | bytes 131104 | tf_op jit(solution)/shard_map/all_to_all | solution.py:1144
  100.4 0.7 multiply_subtract_fusion.1
  (30 shorter events, 0.2 us)
Async XLA Ops:
  2.1 8.5 %copy-start.5 = (f32[18568]{0:T(1024)S(1)}, f32[18568]{0:T(1024)}, u32[]{:S(2)}) copy-start(f32[18568]{0:T(1024)} %param.18) | copy-start | bytes 222820
  2.1 16.2 %all-to-all-start = ((bf16[16,32,128]{2,1,0:T(8,128)(2,1)}), bf16[16,32,128]{2,1,0:T(8,128)(2,1)S(1)}, u32[]{:S(2)}, u32[]{:S(2)}) async-start(bf16[16,32,128]{2,1,0:T(8,128)(2,1)} %broadcast_in_dim.6), calls=%async_computation | async-start | bytes 262144 | tf_op jit(solution)/shard_map/all_to_all | solution.py:733
  19.1 3.7 %copy-start.9 = (f32[1,3,4096]{2,0,1:T(1,128)S(1)}, f32[1,3,4096]{2,0,1:T(1,128)}, u32[]{:S(2)}) copy-start(f32[1,3,4096]{2,0,1:T(1,128)} %param.13) | copy-start | bytes 147460
  19.1 13.8 %all-to-all-start.1 = ((bf16[16,80,128]{2,1,0:T(8,128)(2,1)}), bf16[16,80,128]{2,1,0:T(8,128)(2,1)S(1)}, u32[]{:S(2)}, u32[]{:S(2)}) async-start(bf16[16,80,128]{2,1,0:T(8,128)(2,1)} %broadcast_in_dim.7), calls=%async_computation.1 | async-start | bytes 655360 | tf_op jit(solution)/shard_map/all_to_all | solution.py:733
  22.8 0.7 copy-start.4
  23.5 19.9 %copy-start = (f32[2048,128]{1,0:T(8,128)S(1)}, f32[2048,128]{1,0:T(8,128)}, u32[]{:S(2)}) copy-start(f32[2048,128]{1,0:T(8,128)} %cot_ref.1) | copy-start | bytes 3145732
  31.3 12.0 %copy-start.1 = (bf16[2048,128]{1,0:T(8,128)(2,1)S(1)}, bf16[2048,128]{1,0:T(8,128)(2,1)}, u32[]{:S(2)}) copy-start(bf16[2048,128]{1,0:T(8,128)(2,1)} %token_ref.1) | copy-start | bytes 1572868
  32.9 3.5 %collective-permute-start.3 = (bf16[16,80,128]{2,1,0:T(8,128)(2,1)S(1)}, bf16[16,80,128]{2,1,0:T(8,128)(2,1)S(1)}, u32[]{:S(2)}, u32[]{:S(2)}) collective-permute-start(bf16[16,80,128]{2,1,0:T(8,128)(2,1)S(1)} %all-to-all-done.1.own_ref), channel_id=1, source_target_pairs={{0,16},{16,0},{1,17},{17,1},{2,18},{18,2},{3,19},{19,3},{4,20},{20... | collective-permute-start | bytes 983048 | tf_op jit(solution)/shard_map/ppermute | solution.py:737
  32.9 4.9 %collective-permute-start.2 = (f32[72,128]{1,0:T(8,128)S(1)}, f32[72,128]{1,0:T(8,128)S(1)}, u32[]{:S(2)}, u32[]{:S(2)}) collective-permute-start(f32[72,128]{1,0:T(8,128)S(1)} %get-tuple-element.95), channel_id=1, source_target_pairs={{0,3},{1,2},{2,1},{3,0},{4,7},{5,6},{6,5},{7,4},{8,11},{9,10},{10,... | collective-permute-start | bytes 110600 | tf_op jit(solution)/shard_map/ppermute | solution.py:720
  34.2 4.3 %collective-permute-start.1 = (f32[72,128]{1,0:T(8,128)S(1)}, f32[72,128]{1,0:T(8,128)S(1)}, u32[]{:S(2)}, u32[]{:S(2)}) collective-permute-start(f32[72,128]{1,0:T(8,128)S(1)} %get-tuple-element.95), channel_id=1, source_target_pairs={{0,2},{1,3},{2,0},{3,1},{4,6},{5,7},{6,4},{7,5},{8,10},{9,11},{10,... | collective-permute-start | bytes 110600 | tf_op jit(solution)/shard_map/ppermute | solution.py:720
  34.9 4.0 %collective-permute-start = (f32[72,128]{1,0:T(8,128)S(1)}, f32[72,128]{1,0:T(8,128)S(1)}, u32[]{:S(2)}, u32[]{:S(2)}) collective-permute-start(f32[72,128]{1,0:T(8,128)S(1)} %get-tuple-element.95), channel_id=1, source_target_pairs={{0,1},{1,0},{2,3},{3,2},{4,5},{5,4},{6,7},{7,6},{8,9},{9,8},{10,11... | collective-permute-start | bytes 110600 | tf_op jit(solution)/shard_map/ppermute | solution.py:720
  38.9 5.8 %collective-permute-start.6 = (f32[72,128]{1,0:T(8,128)S(1)}, f32[72,128]{1,0:T(8,128)S(1)}, u32[]{:S(2)}, u32[]{:S(2)}) collective-permute-start(f32[72,128]{1,0:T(8,128)S(1)} %add_add_fusion.3), channel_id=1, source_target_pairs={{0,12},{1,13},{2,14},{3,15},{4,8},{5,9},{6,10},{7,11},{8,4},{9,5},... | collective-permute-start | bytes 110600 | tf_op jit(solution)/shard_map/ppermute | solution.py:720
  42.4 4.9 %collective-permute-start.5 = (f32[72,128]{1,0:T(8,128)S(1)}, f32[72,128]{1,0:T(8,128)S(1)}, u32[]{:S(2)}, u32[]{:S(2)}) collective-permute-start(f32[72,128]{1,0:T(8,128)S(1)} %add_add_fusion.3), channel_id=1, source_target_pairs={{0,8},{1,9},{2,10},{3,11},{4,12},{5,13},{6,14},{7,15},{8,0},{9,1},... | collective-permute-start | bytes 110600 | tf_op jit(solution)/shard_map/ppermute | solution.py:720
  42.4 4.9 %collective-permute-start.4 = (f32[72,128]{1,0:T(8,128)S(1)}, f32[72,128]{1,0:T(8,128)S(1)}, u32[]{:S(2)}, u32[]{:S(2)}) collective-permute-start(f32[72,128]{1,0:T(8,128)S(1)} %add_add_fusion.3), channel_id=1, source_target_pairs={{0,4},{1,5},{2,6},{3,7},{4,0},{5,1},{6,2},{7,3},{8,12},{9,13},{10,... | collective-permute-start | bytes 110600 | tf_op jit(solution)/shard_map/ppermute | solution.py:720
  47.2 1.3 %copy-start.2 = (s32[2048,4]{0,1:T(4,128)S(1)}, s32[2048,4]{0,1:T(4,128)}, u32[]{:S(2)}) copy-start(s32[2048,4]{0,1:T(4,128)} %param.16) | copy-start | bytes 98308
  47.2 1.3 %copy-start.3 = (s32[4]{0:T(128)S(1)}, s32[4]{0:T(128)}, u32[]{:S(2)}) copy-start(s32[4]{0:T(128)} %count_ref.4) | copy-start | bytes 52
  47.2 1.3 %collective-permute-start.7 = (f32[72,128]{1,0:T(8,128)S(1)}, f32[72,128]{1,0:T(8,128)S(1)}, u32[]{:S(2)}, u32[]{:S(2)}) collective-permute-start(f32[72,128]{1,0:T(8,128)S(1)} %add_add_fusion.2.own_ref), channel_id=1, source_target_pairs={{0,16},{16,0},{1,17},{17,1},{2,18},{18,2},{3,19},{19,3},{4,20},{20... | collective-permute-start | bytes 110600 | tf_op jit(solution)/shard_map/ppermute | solution.py:737
  56.9 1.3 %collective-permute-start.8 = (f32[72,128]{1,0:T(8,128)S(1)}, f32[72,128]{1,0:T(8,128)S(1)}, u32[]{:S(2)}, u32[]{:S(2)}) collective-permute-start(f32[72,128]{1,0:T(8,128)S(1)} %get-tuple-element.134), channel_id=1, source_target_pairs={{0,16},{16,0},{1,17},{17,1},{2,18},{18,2},{3,19},{19,3},{4,20},{20... | collective-permute-start | bytes 110600 | tf_op jit(solution)/shard_map/ppermute | solution.py:737
  58.2 4.9 %collective-permute-start.11 = (f32[72,128]{1,0:T(8,128)S(1)}, f32[72,128]{1,0:T(8,128)S(1)}, u32[]{:S(2)}, u32[]{:S(2)}) collective-permute-start(f32[72,128]{1,0:T(8,128)S(1)} %add.86), channel_id=1, source_target_pairs={{0,3},{1,2},{2,1},{3,0},{4,7},{5,6},{6,5},{7,4},{8,11},{9,10},{10,... | collective-permute-start | bytes 110600 | tf_op jit(solution)/shard_map/ppermute | solution.py:720
  59.4 4.0 %collective-permute-start.10 = (f32[72,128]{1,0:T(8,128)S(1)}, f32[72,128]{1,0:T(8,128)S(1)}, u32[]{:S(2)}, u32[]{:S(2)}) collective-permute-start(f32[72,128]{1,0:T(8,128)S(1)} %add.86), channel_id=1, source_target_pairs={{0,2},{1,3},{2,0},{3,1},{4,6},{5,7},{6,4},{7,5},{8,10},{9,11},{10,... | collective-permute-start | bytes 110600 | tf_op jit(solution)/shard_map/ppermute | solution.py:720
  61.0 4.0 %collective-permute-start.9 = (f32[72,128]{1,0:T(8,128)S(1)}, f32[72,128]{1,0:T(8,128)S(1)}, u32[]{:S(2)}, u32[]{:S(2)}) collective-permute-start(f32[72,128]{1,0:T(8,128)S(1)} %add.86), channel_id=1, source_target_pairs={{0,1},{1,0},{2,3},{3,2},{4,5},{5,4},{6,7},{7,6},{8,9},{9,8},{10,11... | collective-permute-start | bytes 110600 | tf_op jit(solution)/shard_map/ppermute | solution.py:720
  64.9 2.7 %collective-permute-start.15 = (bf16[16,80,128]{2,1,0:T(8,128)(2,1)S(1)}, bf16[16,80,128]{2,1,0:T(8,128)(2,1)S(1)}, u32[]{:S(2)}, u32[]{:S(2)}) collective-permute-start(bf16[16,80,128]{2,1,0:T(8,128)(2,1)S(1)} %get-tuple-element.152), channel_id=1, source_target_pairs={{0,16},{16,0},{1,17},{17,1},{2,18},{18,2},{3,19},{19,3},{4,20},{20... | collective-permute-start | bytes 983048 | tf_op jit(solution)/shard_map/ppermute | solution.py:737
  64.9 7.9 %collective-permute-start.17 = (f32[1024,128]{1,0:T(8,128)S(1)}, f32[1024,128]{1,0:T(8,128)S(1)}, u32[]{:S(2)}, u32[]{:S(2)}) collective-permute-start(f32[1024,128]{1,0:T(8,128)S(1)} %get-tuple-element.154.grad_own_ref), channel_id=1, source_target_pairs={{0,16},{16,0},{1,17},{17,1},{2,18},{18,2},{3,19},{19,3},{4,20},{20... | collective-permute-start | bytes 1572872 | tf_op jit(solution)/shard_map/ppermute | solution.py:737
  65.4 7.4 %collective-permute-start.16 = (bf16[1024,128]{1,0:T(8,128)(2,1)S(1)}, bf16[1024,128]{1,0:T(8,128)(2,1)S(1)}, u32[]{:S(2)}, u32[]{:S(2)}) collective-permute-start(bf16[1024,128]{1,0:T(8,128)(2,1)S(1)} %get-tuple-element.153.out_own_ref), channel_id=1, source_target_pairs={{0,16},{16,0},{1,17},{17,1},{2,18},{18,2},{3,19},{19,3},{4,20},{20... | collective-permute-start | bytes 786440 | tf_op jit(solution)/shard_map/ppermute | solution.py:737
  65.5 5.9 %collective-permute-start.14 = (f32[72,128]{1,0:T(8,128)S(1)}, f32[72,128]{1,0:T(8,128)S(1)}, u32[]{:S(2)}, u32[]{:S(2)}) collective-permute-start(f32[72,128]{1,0:T(8,128)S(1)} %add_add_fusion.1), channel_id=1, source_target_pairs={{0,12},{1,13},{2,14},{3,15},{4,8},{5,9},{6,10},{7,11},{8,4},{9,5},... | collective-permute-start | bytes 110600 | tf_op jit(solution)/shard_map/ppermute | solution.py:720
  66.9 5.9 %collective-permute-start.13 = (f32[72,128]{1,0:T(8,128)S(1)}, f32[72,128]{1,0:T(8,128)S(1)}, u32[]{:S(2)}, u32[]{:S(2)}) collective-permute-start(f32[72,128]{1,0:T(8,128)S(1)} %add_add_fusion.1), channel_id=1, source_target_pairs={{0,8},{1,9},{2,10},{3,11},{4,12},{5,13},{6,14},{7,15},{8,0},{9,1},... | collective-permute-start | bytes 110600 | tf_op jit(solution)/shard_map/ppermute | solution.py:720
  67.6 5.2 %collective-permute-start.12 = (f32[72,128]{1,0:T(8,128)S(1)}, f32[72,128]{1,0:T(8,128)S(1)}, u32[]{:S(2)}, u32[]{:S(2)}) collective-permute-start(f32[72,128]{1,0:T(8,128)S(1)} %add_add_fusion.1), channel_id=1, source_target_pairs={{0,4},{1,5},{2,6},{3,7},{4,0},{5,1},{6,2},{7,3},{8,12},{9,13},{10,... | collective-permute-start | bytes 110600 | tf_op jit(solution)/shard_map/ppermute | solution.py:720
  72.8 15.4 %all-to-all-start.2 = ((bf16[16,80,128]{2,1,0:T(8,128)(2,1)}), bf16[16,80,128]{2,1,0:T(8,128)(2,1)S(1)}, u32[]{:S(2)}, u32[]{:S(2)}) async-start(bf16[16,80,128]{2,1,0:T(8,128)(2,1)} %add_convert_fusion), calls=%async_computation.2 | async-start | bytes 655360 | tf_op jit(solution)/shard_map/all_to_all | solution.py:1067
  88.3 3.8 %collective-permute-start.18 = (f32[10240]{0:T(1024)S(1)}, f32[10240]{0:T(1024)S(1)}, u32[]{:S(2)}, u32[]{:S(2)}) collective-permute-start(f32[10240]{0:T(1024)S(1)} %bitcast.11), channel_id=1, source_target_pairs={{0,16},{16,0},{1,17},{17,1},{2,18},{18,2},{3,19},{19,3},{4,20},{20... | collective-permute-start | bytes 122888 | tf_op jit(solution)/shard_map/ppermute | solution.py:737
  88.4 3.8 %copy-start.6 = (f32[18568]{0:T(1024)S(1)}, f32[18568]{0:T(1024)}, u32[]{:S(2)}) copy-start(f32[18568]{0:T(1024)} %param.19) | copy-start | bytes 222820
  88.4 3.8 %copy-start.7 = (f32[18568]{0:T(1024)S(1)}, f32[18568]{0:T(1024)}, u32[]{:S(2)}) copy-start(f32[18568]{0:T(1024)} %param.20) | copy-start | bytes 222820
  88.4 12.0 %all-to-all-start.3 = ((bf16[16,32,128]{2,1,0:T(8,128)(2,1)}), bf16[16,32,128]{2,1,0:T(8,128)(2,1)S(1)}, u32[]{:S(2)}, u32[]{:S(2)}) async-start(bf16[16,32,128]{2,1,0:T(8,128)(2,1)} %get-tuple-element.175), calls=%async_computation.3 | async-start | bytes 262144 | tf_op jit(solution)/shard_map/all_to_all | solution.py:1144
  92.9 7.5 %copy-start.8 = (f32[1,3112]{1,0:T(1,128)S(1)}, f32[1,3112]{1,0:T(1,128)}, u32[]{:S(2)}) copy-start(f32[1,3112]{1,0:T(1,128)} %param.21) | copy-start | bytes 37348
  92.9 7.5 %copy-start.10 = (f32[1,3112]{1,0:T(1,128)S(1)}, f32[1,3112]{1,0:T(1,128)}, u32[]{:S(2)}) copy-start(f32[1,3112]{1,0:T(1,128)} %param.22) | copy-start | bytes 37348
  92.9 7.5 %copy-start.11 = (f32[1,3112]{1,0:T(1,128)S(1)}, f32[1,3112]{1,0:T(1,128)}, u32[]{:S(2)}) copy-start(f32[1,3112]{1,0:T(1,128)} %param.23) | copy-start | bytes 37348

commit v3 on v2

--- a/solution.py
+++ b/solution.py
@@ -24,10 +24,12 @@
 EPS_ADAM = 1e-08
 
 LANES = 128
-VMEM_BASE = 15 * 1024 * 1024
+VMEM_BASE = 16 * 1024 * 1024
 VMEM_ITEM = 768 * 1024
-SAMPLE_TILE = 1024
+SAMPLE_TILE = 2048
+BACK_TILE = 2048
 TOKEN_TILE = 1024
+CHUNK = 256
 
 F32 = jnp.float32
 BF16 = jnp.bfloat16
@@ -101,14 +103,45 @@
     return (raised * (1.0 / total)).reshape(values.shape)
 
 
+def gelu_value(inner):
+    square = inner * inner
+    bend = inner * (TANH_C + (TANH_C * TANH_CUBE) * square)
+    return inner * (0.5 + 0.5 * jnp.tanh(bend))
+
+
 def gelu_parts(inner):
     square = inner * inner
-    bend = TANH_C + (TANH_C * TANH_CUBE) * square
-    curve = jnp.tanh(inner * bend)
-    gate = 0.5 + 0.5 * curve
-    slope = (TANH_C) + (3.0 * TANH_C * TANH_CUBE) * square
-    grad = gate + inner * (0.5 - 0.5 * curve * curve) * slope
-    return inner * gate, grad
+    bend = inner * (TANH_C + (TANH_C * TANH_CUBE) * square)
+    gate = 0.5 + 0.5 * jnp.tanh(bend)
+    rise = inner * (2.0 * TANH_C + (6.0 * TANH_C * TANH_CUBE) * square)
+    return inner * gate, gate + (gate - gate * gate) * rise
+
+
+def split_samples(funcs, parts_ref):
+    high = funcs.astype(BF16).astype(F32)
+    middle = (funcs - high).astype(BF16).astype(F32)
+    parts_ref[0:FIN, :] = high
+    parts_ref[FIN : 2 * FIN, :] = middle
+    parts_ref[2 * FIN : 3 * FIN, :] = funcs - high - middle
+    parts_ref[3 * FIN : 3 * FIN + 1, :] = jnp.ones((1, funcs.shape[1]), F32)
+    parts_ref[3 * FIN + 1 :, :] = jnp.zeros((15 - 3 * FIN, funcs.shape[1]), F32)
+    return parts_ref[...].astype(BF16)
+
+
+def staggered(programs):
+    waiting = list(programs)
+    running = []
+    while waiting or running:
+        if waiting:
+            running.append(waiting.pop(0))
+        still = []
+        for program in running:
+            try:
+                next(program)
+                still.append(program)
+            except StopIteration:
+                pass
+        running = still
 
 
 def wide(tile, length):
@@ -191,6 +224,16 @@
         return carry
 
     lax.fori_loop(low + 1, high, step, 0)
+
+
+def over_parts(starts, item, begin, length, visit):
+    width = min(256, length)
+    for at in range(0, length, width):
+        start = begin + at
+
+        @pl.when((starts[item] < start + width) & (starts[item + 1] > start))
+        def _(at=at, start=start):
+            visit(slice(at, at + width), start)
 
 
 def put_shard(vec_ref, tmp_ref, number, shard, height):
@@ -227,41 +270,46 @@
 def sample_forward_kernel(
     plan,
     scal_ref,
-    count_ref,
+    count_hbm,
     recv_ref,
     func_ref,
     msg_ref,
     keys_ref,
     vals_ref,
-    first_ref,
-    second_ref,
-    slope_one_ref,
-    slope_two_ref,
     hid_ref,
     pair_ref,
+    in_t_ref,
+    hid_t_ref,
+    col_ref,
     vec_ref,
     tmp_ref,
-    col_ref,
-    hid_t_ref,
+    parts_ref,
     pair_t_ref,
     acc_ref,
     starts,
+    count_ref,
+    sem,
 ):
     tile, items, parts, shard, height, slots = plan
     step = pl.program_id(0)
 
     @pl.when(step == 0)
     def _():
-        store_starts(lambda item: count_ref[0, item], starts, items)
+        fetch = pltpu.make_async_copy(count_hbm, count_ref, sem)
+        fetch.start()
         acc_ref[...] = jnp.zeros(acc_ref.shape, F32)
         for number in range(parts):
             shift = (number * shard) % LANES
             tmp_ref[8 : 8 + height, :] = turned(recv_ref[number].astype(F32), shift)
             put_shard(vec_ref, tmp_ref, number, shard, height)
-        for slot, row in enumerate((0, 1, 2, ROW_IN_B, ROW_HID_B)):
-            col_ref[slot] = jnp.transpose(
-                jnp.broadcast_to(vec_ref[row : row + 1, :], (D, D))
-            )
+        col_ref[...] = jnp.transpose(
+            jnp.broadcast_to(vec_ref[ROW_HID_B : ROW_HID_B + 1, :], (D, D))
+        )
+        tmp_ref[0:16, :] = jnp.zeros((16, LANES), F32)
+        for part in range(3):
+            tmp_ref[part * FIN : (part + 1) * FIN, :] = vec_ref[ROW_IN : ROW_IN + FIN, :]
+        tmp_ref[3 * FIN : 3 * FIN + 1, :] = vec_ref[ROW_IN_B : ROW_IN_B + 1, :]
+        in_t_ref[...] = jnp.transpose(tmp_ref[0:16, :]).astype(BF16)
         hid = vec_ref[ROW_HID : ROW_HID + D, :]
         hid_ref[...] = hid.astype(BF16)
         hid_t_ref[...] = jnp.transpose(hid).astype(BF16)
@@ -269,30 +317,34 @@
             piece = vec_ref[pl.ds(ROW_PAIR + part, D, stride=2), :]
             pair_ref[:, part * D : (part + 1) * D] = piece.astype(BF16)
             pair_t_ref[part * D : (part + 1) * D, :] = jnp.transpose(piece).astype(BF16)
-
-    funcs = func_ref[0]
-    first_in = wide(col_ref[3], tile)
-    for part in range(FIN):
-        first_in = first_in + wide(col_ref[part], tile) * funcs[part : part + 1, :]
-    first, slope_one = gelu_parts(first_in)
-    first = first.astype(BF16)
-    first_ref[...] = first
-    slope_one_ref[...] = slope_one.astype(slope_one_ref.dtype)
-    second_in = dot_nn(hid_t_ref[...], first) + wide(col_ref[4], tile)
-    second, slope_two = gelu_parts(second_in)
-    second = second.astype(BF16)
-    second_ref[...] = second
-    slope_two_ref[...] = slope_two.astype(slope_two_ref.dtype)
-    pair = dot_nn(pair_t_ref[...], second)
-    keys = head_softmax(pair[:D])
-    keys_ref[...] = keys.astype(BF16)
-    vals = pair[D:].astype(BF16)
-    vals_ref[...] = vals
-    vals_ones = jnp.concatenate([vals, jnp.ones((16, tile), BF16)], axis=0)
+        fetch.wait()
+        store_starts(lambda item: count_ref[0, item], starts, items)
+
+    samples = split_samples(func_ref[0], parts_ref)
+    chunk = min(CHUNK, tile)
+
+    def forward(start):
+        at = slice(start, start + chunk)
+        first_in = dot_nn(in_t_ref[...], samples[:, at])
+        yield
+        first = gelu_value(first_in).astype(BF16)
+        yield
+        second_in = dot_nn(hid_t_ref[...], first)
+        yield
+        second = gelu_value(second_in + wide(col_ref[...], chunk)).astype(BF16)
+        yield
+        pair = dot_nn(pair_t_ref[...], second)
+        yield
+        vals_ref[:, at] = pair[D:].astype(BF16)
+        keys_ref[:, at] = head_softmax(pair[:D]).astype(BF16)
+
+    staggered([forward(start) for start in range(0, tile, chunk)])
+    keys = keys_ref[...]
+    vals_ones = jnp.concatenate([vals_ref[...], jnp.ones((16, tile), BF16)], axis=0)
     begin = scal_ref[1] * slots + step * tile
 
     def visit(item, _):
-        masked = (keys * item_row(starts, item, begin, tile)).astype(BF16)
+        masked = keys * item_row(starts, item, begin, tile).astype(BF16)
         acc_ref[item] += dot_nt(vals_ones, masked)
 
     over_items(starts, items, begin, tile, visit)
@@ -304,6 +356,29 @@
         for item in range(items):
             msg_ref[item * HD : (item + 1) * HD, :] = fold_heads(acc_ref[item, :D, :], mask)
             msg_ref[items * HD + item : items * HD + item + 1, :] = acc_ref[item, D : D + 1, :]
+
+
+def slope_kernel(func_ref, in_t_ref, hid_t_ref, col_ref, *refs):
+    first_ref, second_ref, slope_one_ref, slope_two_ref, parts_ref = refs[-5:]
+    samples = split_samples(func_ref[0], parts_ref)
+    chunk = min(CHUNK, samples.shape[1])
+
+    def slopes(start):
+        at = slice(start, start + chunk)
+        first_in = dot_nn(in_t_ref[...], samples[:, at])
+        yield
+        first, slope_one = gelu_parts(first_in)
+        first = first.astype(BF16)
+        first_ref[:, at] = first
+        slope_one_ref[:, at] = slope_one.astype(BF16)
+        yield
+        second_in = dot_nn(hid_t_ref[...], first)
+        yield
+        second, slope_two = gelu_parts(second_in + wide(col_ref[...], chunk))
+        second_ref[:, at] = second.astype(BF16)
+        slope_two_ref[:, at] = slope_two.astype(BF16)
+
+    staggered([slopes(start) for start in range(0, samples.shape[1], chunk)])
 
 
 def weight_kernel(
@@ -346,7 +421,7 @@
         for part in range(2):
             up = vec_ref[pl.ds(ROW_UP + expert * 2 * D + part, D, stride=2), :]
             up_ref[expert, :, part * D : (part + 1) * D] = up.astype(BF16)
-            up_t_ref[expert, part * D : (part + 1) * D, :] = jnp.transpose(up).astype(BF16)
+            up_t_ref[expert, part * D : (part + 1) * D, :D] = jnp.transpose(up).astype(BF16)
             row = ROW_DOWN + expert * FF + part * D
             down = vec_ref[row : row + D, :]
             down_ref[expert, part * D : (part + 1) * D, :] = down.astype(BF16)
@@ -357,7 +432,13 @@
     rows += [ROW_DOWN_B + number for number in range(E)]
     for slot, row in enumerate(rows):
         tmp_ref[slot : slot + 1, :] = vec_ref[row : row + 1, :]
-    cols_ref[...] = jnp.transpose(tmp_ref[0:D, :])
+    cols = jnp.transpose(tmp_ref[0:D, :])
+    cols_ref[...] = cols
+    lane = lax.broadcasted_iota(jnp.int32, (D, 16), 1)
+    for expert in range(E):
+        for part in range(2):
+            bias = jnp.where(lane == COL_UP_B + 2 * expert + part, cols[:, :16], 0.0)
+            up_t_ref[expert, part * D : (part + 1) * D, D:] = bias.astype(BF16)
 
 
 def norm_unit(values):
@@ -404,7 +485,6 @@
 def token_kernel(
     plan,
     scal_ref,
-    count_ref,
     own_ref,
     other_ref,
     gate_ref,
@@ -436,6 +516,7 @@
     acc_ref,
     mix_ref,
     pull_ref,
+    grads_ref,
     starts,
 ):
     tile, items, slots, steps = plan
@@ -444,7 +525,7 @@
 
     @pl.when(step == 0)
     def _():
-        store_starts(lambda item: count_ref[item], starts, items)
+        store_starts(lambda item: scal_ref[2 + item], starts, items)
         acc_ref[...] = jnp.zeros(acc_ref.shape, F32)
         g_query_ref[...] = jnp.zeros(g_query_ref.shape, F32)
         g_out_ref[...] = jnp.zeros(g_out_ref.shape, F32)
@@ -475,13 +556,21 @@
     cols = cols_ref[...]
     begin = first_row + step * tile
     soft = soft_ref[...]
-    soft_low = soft.astype(BF16)
-    soft_vals = soft_low.astype(F32)
+
+    def attend(item, lanes, start):
+        length = lanes.stop - lanes.start
+        masked = soft_ref[:, lanes].astype(BF16) * item_row(starts, item, start, length).astype(BF16)
+        return dot_nn(left_ref[item], jnp.concatenate([masked, masked], axis=0))
 
     def forward(item, opening):
-        masked = (soft_vals * item_row(starts, item, begin, tile)).astype(BF16)
-        fresh = dot_nn(left_ref[item], jnp.concatenate([masked, masked], axis=0))
-        mix_ref[...] = fresh if opening else mix_ref[...] + fresh
+        if opening:
+            mix_ref[...] = attend(item, slice(0, tile), begin)
+            return
+
+        def add(lanes, start):
+            mix_ref[:, lanes] += attend(item, lanes, start)
+
+        over_parts(starts, item, begin, tile, add)
 
     over_items(starts, items, begin, tile, forward)
     numer_one, numer_two = mix_ref[:D, :], mix_ref[D : 2 * D, :]
@@ -504,10 +593,7 @@
     mixture = residual
     grad_norm = jnp.zeros((D, tile), F32)
     for expert in range(E):
-        bias = jnp.concatenate(
-            [column(cols, COL_UP_B + 2 * expert + part, tile) for part in range(2)], axis=0
-        )
-        inner = dot_nn(up_t_ref[expert], norm) + bias
+        inner = dot_nn(up_t_ref[expert], norm_ones)
         active, slope = gelu_parts(inner)
         active = active.astype(BF16)
         result = dot_nn(down_t_ref[expert], active) + column(cols, COL_DOWN_B + expert, tile)
@@ -530,12 +616,27 @@
     sum_two = -head_sum(grad_two * own_two)
     grads = jnp.concatenate([grad_one, grad_two, sum_one, sum_two], axis=0).astype(BF16)
 
+    grads_ref[...] = grads
+
+    def pull_back(item, lanes, start):
+        length = lanes.stop - lanes.start
+        row = item_row(starts, item, start, length)
+        part = grads_ref[:, lanes]
+        masked = soft_ref[:, lanes].astype(BF16) * row.astype(BF16)
+        return dot_nt(part, masked), row * dot_nn(back_ref[item], part)
+
     def backward(item, opening):
-        row = item_row(starts, item, begin, tile)
-        masked = (soft_vals * row).astype(BF16)
-        acc_ref[item] += dot_nt(grads, masked)
-        fresh = row * dot_nn(back_ref[item], grads)
-        pull_ref[...] = fresh if opening else pull_ref[...] + fresh
+        if opening:
+            sums, pull_ref[...] = pull_back(item, slice(0, tile), begin)
+            acc_ref[item] += sums
+            return
+
+        def add(lanes, start):
+            sums, pull = pull_back(item, lanes, start)
+            acc_ref[item] += sums
+            pull_ref[:, lanes] += pull
+
+        over_parts(starts, item, begin, tile, add)
 
     over_items(starts, items, begin, tile, backward)
     pull = pull_ref[...]
@@ -605,46 +706,52 @@
 def sample_backward_kernel(
     plan,
     scal_ref,
-    count_ref,
     msg_ref,
     func_ref,
-    keys_ref,
-    vals_ref,
-    first_ref,
-    second_ref,
-    slope_one_ref,
-    slope_two_ref,
+    keys_hbm,
+    vals_hbm,
+    first_hbm,
+    second_hbm,
+    slope_one_hbm,
+    slope_two_hbm,
     hid_ref,
     pair_ref,
-    out_own_ref,
-    out_other_ref,
-    grad_own_ref,
-    grad_other_ref,
     send_ref,
-    out_ref,
-    grad_ref,
+    kept_ref,
     vec_ref,
     left_keys_ref,
     left_vals_ref,
-    shift_ref,
     keys_acc_ref,
     vals_acc_ref,
     g_pair_ref,
     g_hid_ref,
     g_in_ref,
+    parts_ref,
+    pairs_ref,
+    seconds_ref,
+    firsts_ref,
     starts,
+    sems,
 ):
     tile, items, parts, shard, height, slots, steps = plan
-    step = pl.program_id(0)
-    core = scal_ref[0]
-    out_ref[core] = out_own_ref[...]
-    out_ref[1 - core] = out_other_ref[...]
-    grad_ref[core] = grad_own_ref[...]
-    grad_ref[1 - core] = grad_other_ref[...]
-
-    @pl.when(step == 0)
-    def _():
-        store_starts(lambda item: count_ref[0, item], starts, items)
+    sources = (keys_hbm, vals_hbm, second_hbm, slope_two_hbm, first_hbm, slope_one_hbm)
+    fetches = [
+        [
+            pltpu.make_async_copy(
+                source.at[:, step * tile : (step + 1) * tile],
+                kept_ref.at[number, :, step * tile : (step + 1) * tile],
+                sems.at[number, step],
+            )
+            for number, source in enumerate(sources)
+        ]
+        for step in range(steps)
+    ]
+    for group in fetches:
+        for fetch in group:
+            fetch.start()
+
+    def prepare():
+        store_starts(lambda item: scal_ref[2 + items + item], starts, items)
         g_pair_ref[...] = jnp.zeros(g_pair_ref.shape, F32)
         g_hid_ref[...] = jnp.zeros(g_hid_ref.shape, F32)
         g_in_ref[...] = jnp.zeros(g_in_ref.shape, F32)
@@ -657,61 +764,87 @@
             at = pl.multiple_of(item * HD, HD)
             block = spread_heads(msg_ref[pl.ds(at, HD), :], mask)
             left_vals_ref[item] = block.astype(BF16)
-            left_keys_ref[item] = jnp.transpose(block).astype(BF16)
             row = msg_ref[pl.ds(items * HD + item, 1), :]
-            shift_ref[item] = jnp.transpose(jnp.broadcast_to(row, (D, D)))
+            both = jnp.concatenate([block, row, jnp.zeros((D - 1, D), F32)], axis=0)
+            left_keys_ref[item] = jnp.transpose(both)[:, : D + 16].astype(BF16)
             return carry
 
         @pl.when(high <= low)
         def _():
             last = items - 1
             left_vals_ref[last] = jnp.zeros((D, D), BF16)
-            left_keys_ref[last] = jnp.zeros((D, D), BF16)
-            shift_ref[last] = jnp.zeros((D, D), F32)
+            left_keys_ref[last] = jnp.zeros((D, D + 16), BF16)
 
         lax.fori_loop(low, high, build, 0)
 
-    keys = keys_ref[...]
-    vals = vals_ref[...]
-    begin = scal_ref[1] * slots + step * tile
-
-    def visit(item, opening):
-        row = item_row(starts, item, begin, tile)
-        fresh_keys = row * (dot_nn(left_keys_ref[item], vals) + wide(shift_ref[item], tile))
-        fresh_vals = row * dot_nn(left_vals_ref[item], keys)
-        keys_acc_ref[...] = fresh_keys if opening else keys_acc_ref[...] + fresh_keys
-        vals_acc_ref[...] = fresh_vals if opening else vals_acc_ref[...] + fresh_vals
-
-    over_items(starts, items, begin, tile, visit)
-    soft = keys.astype(F32)
-    grad_keys = keys_acc_ref[...]
-    grad_in = soft * (grad_keys - head_sum(grad_keys * soft))
-    grad_pair = jnp.concatenate([grad_in, vals_acc_ref[...]], axis=0).astype(BF16)
-    g_pair_ref[...] += dot_nt(second_ref[...], grad_pair)
-    grad_second = (slope_two_ref[...].astype(F32) * dot_nn(pair_ref[...], grad_pair)).astype(BF16)
-    first_ones = jnp.concatenate([first_ref[...], jnp.ones((16, tile), BF16)], axis=0)
-    g_hid_ref[...] += dot_nt(first_ones, grad_second)
-    grad_first = slope_one_ref[...].astype(F32) * dot_nn(hid_ref[...], grad_second)
-    funcs = func_ref[0]
-    for part in range(FIN):
-        g_in_ref[part] += fold_lanes(grad_first * funcs[part : part + 1, :])
-    g_in_ref[FIN] += fold_lanes(grad_first)
-
-    @pl.when(step == steps - 1)
-    def _():
-        vec_ref[BRANCH_ROWS:, :] = jnp.zeros((vec_ref.shape[0] - BRANCH_ROWS, LANES), F32)
-        for part in range(FIN + 1):
-            vec_ref[part : part + 1, :] = lane_total_row(g_in_ref[part])
-        vec_ref[ROW_HID : ROW_HID + D + 1, :] = g_hid_ref[: D + 1, :]
-        for part in range(2):
-            vec_ref[pl.ds(ROW_PAIR + part, D, stride=2), :] = g_pair_ref[
-                :, part * D : (part + 1) * D
-            ]
-        for number in range(parts):
-            send_ref[number] = take_shard(vec_ref, number, shard, height).astype(BF16)
-
-
-def sum_over_points(values, count, besides):
+    def work(step):
+        def part(number):
+            return kept_ref.at[number, :, step * tile : (step + 1) * tile]
+
+        keys_ref, vals_ref, second_ref, slope_two_ref, first_ref, slope_one_ref = (
+            part(number) for number in range(6)
+        )
+        fetches[step][0].wait()
+        fetches[step][1].wait()
+        keys = keys_ref[...]
+        ones = jnp.ones((16, tile), BF16)
+        vals_ones = jnp.concatenate([vals_ref[...], ones], axis=0)
+        begin = scal_ref[1] * slots + step * tile
+
+        def visit(item, opening):
+            row = item_row(starts, item, begin, tile)
+            fresh_keys = row * dot_nn(left_keys_ref[item], vals_ones)
+            fresh_vals = row * dot_nn(left_vals_ref[item], keys)
+            keys_acc_ref[...] = fresh_keys if opening else keys_acc_ref[...] + fresh_keys
+            vals_acc_ref[...] = fresh_vals if opening else vals_acc_ref[...] + fresh_vals
+
+        over_items(starts, items, begin, tile, visit)
+        samples = split_samples(func_ref[0, :, step * tile : (step + 1) * tile], parts_ref)
+        for number in range(2, 6):
+            fetches[step][number].wait()
+        chunk = min(CHUNK, tile)
+
+        def backward(start):
+            at = slice(start, start + chunk)
+            soft = keys_ref[:, at].astype(F32)
+            grad_keys = keys_acc_ref[:, at]
+            grad_in = soft * (grad_keys - head_sum(grad_keys * soft))
+            grad_pair = jnp.concatenate([grad_in, vals_acc_ref[:, at]], axis=0).astype(BF16)
+            pairs_ref[:, at] = grad_pair
+            yield
+            grad_second = dot_nn(pair_ref[...], grad_pair)
+            yield
+            grad_second = (slope_two_ref[:, at].astype(F32) * grad_second).astype(BF16)
+            seconds_ref[:, at] = grad_second
+            yield
+            grad_first = dot_nn(hid_ref[...], grad_second)
+            yield
+            firsts_ref[:, at] = (slope_one_ref[:, at].astype(F32) * grad_first).astype(BF16)
+
+        staggered([backward(start) for start in range(0, tile, chunk)])
+        g_pair_ref[...] += dot_nt(second_ref[...], pairs_ref[...])
+        first_ones = jnp.concatenate([first_ref[...], ones], axis=0)
+        g_hid_ref[...] += dot_nt(first_ones, seconds_ref[...])
+        g_in_ref[...] += dot_nt(samples, firsts_ref[...])
+
+    prepare()
+    for step in range(steps):
+        work(step)
+    vec_ref[BRANCH_ROWS:, :] = jnp.zeros((vec_ref.shape[0] - BRANCH_ROWS, LANES), F32)
+    vec_ref[ROW_IN : ROW_IN + FIN, :] = (
+        g_in_ref[0:FIN, :] + g_in_ref[FIN : 2 * FIN, :] + g_in_ref[2 * FIN : 3 * FIN, :]
+    )
+    vec_ref[ROW_IN_B : ROW_IN_B + 1, :] = g_in_ref[3 * FIN : 3 * FIN + 1, :]
+    vec_ref[ROW_HID : ROW_HID + D + 1, :] = g_hid_ref[: D + 1, :]
+    for part in range(2):
+        vec_ref[pl.ds(ROW_PAIR + part, D, stride=2), :] = g_pair_ref[
+            :, part * D : (part + 1) * D
+        ]
+    for number in range(parts):
+        send_ref[number] = take_shard(vec_ref, number, shard, height).astype(BF16)
+
+
+def sum_over_points(values, count, besides, early=3):
     bit = 1
     number = 0
     while bit < count:
@@ -722,15 +855,18 @@
         ]
         if number < len(besides):
             before = besides[number - 1] if number else None
-            pieces, besides[number] = lax.optimization_barrier((pieces, besides[number](before)))
+            some = early if number else len(masks)
+            pieces[:some], besides[number] = lax.optimization_barrier(
+                (pieces[:some], besides[number](before))
+            )
         values = functools.reduce(jnp.add, pieces, values)
         bit *= 4
         number += 1
     return values, besides
 
 
-def gather_blocks(block, count):
-    return lax.all_to_all(jnp.broadcast_to(block, (count,) + block.shape), "pts", 0, 0)
+def copies(block, count):
+    return jnp.broadcast_to(block, (count,) + block.shape)
 
 
 def swap_cores(values):
@@ -758,8 +894,8 @@
 ):
     count = lax.axis_size("pts")
     core = lax.axis_index("branch")
-    scal = jnp.stack([core, lax.axis_index("pts")]).astype(jnp.int32)
     items = item_counts.shape[0]
+    place = jnp.stack([core, lax.axis_index("pts")]).astype(jnp.int32)
     chip_rows = tokens.shape[0]
     rows = chip_rows // 2
     slots = funcs.shape[2]
@@ -774,11 +910,12 @@
     shared_pad = jnp.pad(shared_master.astype(BF16), (0, 2 * half * LANES - shared_len))
     shared_half = lax.dynamic_slice_in_dim(shared_pad, core * (half * LANES), half * LANES, 0)
     branch_pad = jnp.pad(
-        branch_master.reshape(-1).astype(BF16), (0, height * LANES - branch_len)
-    )
-    recv_branch = gather_blocks(branch_pad.reshape(height, LANES), count)
-    recv_branch, shared_half = lax.optimization_barrier((recv_branch, shared_half))
-    recv_shared = gather_blocks(shared_half.reshape(half, LANES), count)
+        branch_master.astype(BF16), ((0, 0), (0, height * LANES - branch_len))
+    )
+    recv_branch = lax.all_to_all(copies(branch_pad.reshape(height, LANES), count), "pts", 0, 0)
+    shared_send = copies(shared_half.reshape(half, LANES), count)
+    recv_branch, shared_send = lax.optimization_barrier((recv_branch, shared_send))
+    recv_shared = lax.all_to_all(shared_send, "pts", 0, 0)
 
     tile = min(SAMPLE_TILE, slots)
     steps = slots // tile
@@ -788,12 +925,11 @@
         msg,
         keys,
         vals,
-        first,
-        second,
-        slope_one,
-        slope_two,
         hid_w,
         pair_w,
+        in_t,
+        hid_t,
+        hid_col,
     ) = pl.pallas_call(
         functools.partial(
             sample_forward_kernel, (tile, items, count, branch_len, height, slots)
@@ -802,7 +938,7 @@
             num_scalar_prefetch=1,
             grid=(steps,),
             in_specs=[
-                pl.BlockSpec(memory_space=pltpu.SMEM),
+                pl.BlockSpec(memory_space=pl.ANY),
                 pl.BlockSpec((count, height, LANES), lambda i, *_: (0, 0, 0)),
                 pl.BlockSpec((1, FIN, tile), lambda i, *_: (0, 0, i)),
             ],
@@ -810,44 +946,75 @@
                 whole((msg_rows, LANES)),
                 stream(D),
                 stream(D),
-                stream(D),
-                stream(D),
-                stream(D),
-                stream(D),
                 whole((D, D)),
                 whole((D, 2 * D)),
+                whole((D, 16)),
+                whole((D, D)),
+                whole((D, D)),
             ],
             scratch_shapes=[
                 pltpu.VMEM((vec_rows, LANES), F32),
                 pltpu.VMEM((8 + 2 * height, LANES), F32),
-                pltpu.VMEM((5, D, D), F32),
-                pltpu.VMEM((D, D), BF16),
+                pltpu.VMEM((16, tile), F32),
                 pltpu.VMEM((2 * D, D), BF16),
                 pltpu.VMEM((items, D + 16, D), F32),
                 pltpu.SMEM((items + 1,), jnp.int32),
+                pltpu.SMEM((1, items), jnp.int32),
+                pltpu.SemaphoreType.DMA,
             ],
         ),
         out_shape=[
-            shape((msg_rows, LANES), F32),
-            pltpu.HBM((D, slots), BF16),
-            pltpu.HBM((D, slots), BF16),
-            pltpu.HBM((D, slots), BF16),
-            pltpu.HBM((D, slots), BF16),
+            pltpu.VMEM((msg_rows, LANES), F32),
             pltpu.HBM((D, slots), BF16),
             pltpu.HBM((D, slots), BF16),
             shape((D, D), BF16),
             shape((D, 2 * D), BF16),
+            shape((D, 16), BF16),
+            shape((D, D), BF16),
+            shape((D, D), F32),
         ],
         compiler_params=params,
         cost_estimate=pl.CostEstimate(
             flops=slots * D * D * 10, bytes_accessed=slots * D * 12, transcendentals=slots * D * 3
         ),
         name="sample_forward",
-    )(scal, func_counts, recv_branch, funcs)
+    )(
+        place,
+        pltpu.with_memory_space_constraint(func_counts, pltpu.HBM),
+        recv_branch,
+        funcs,
+    )
+    in_t, place, item_counts, func_counts = lax.optimization_barrier(
+        (in_t, place, item_counts, func_counts)
+    )
+    scal = jnp.concatenate([place, item_counts, func_counts.reshape(-1)])
+
+
+    def make_slopes(start, stop, sources, given):
+        return pl.pallas_call(
+            slope_kernel,
+            grid=(stop - start,),
+            in_specs=[
+                pl.BlockSpec((1, FIN, tile), lambda i: (0, 0, i + start)),
+                whole((D, 16)),
+                whole((D, D)),
+                whole((D, D)),
+            ]
+            + [pl.BlockSpec(memory_space=pl.ANY)] * len(given),
+            out_specs=[pl.BlockSpec((D, tile), lambda i: (0, i + start))] * 4,
+            out_shape=[pltpu.HBM((D, slots), BF16)] * 4,
+            scratch_shapes=[pltpu.VMEM((16, tile), F32)],
+            input_output_aliases={4 + number: number for number in range(len(given))},
+            compiler_params=params,
+            cost_estimate=pl.CostEstimate(
+                flops=4 << 30, bytes_accessed=slots * D * 4, transcendentals=slots * D
+            ),
+            name="slopes",
+        )(*sources, *given)
 
     shared_rows = up_to(SHARED_ROWS + 2 * half + 8, 8)
 
-    def make_weights():
+    def make_weights(recv_shared, recv_other):
         return pl.pallas_call(
             functools.partial(weight_kernel, (count, shared_len, half)),
             in_specs=[
@@ -861,7 +1028,7 @@
                 whole((D, D)),
                 whole((D, D)),
                 whole((E, D, FF)),
-                whole((E, FF, D)),
+                whole((E, FF, D + 16)),
                 whole((E, FF, D)),
                 whole((E, D, FF)),
                 whole((D, D)),
@@ -872,7 +1039,7 @@
                 shape((D, D), BF16),
                 shape((D, D), BF16),
                 shape((E, D, FF), BF16),
-                shape((E, FF, D), BF16),
+                shape((E, FF, D + 16), BF16),
                 shape((E, FF, D), BF16),
                 shape((E, D, FF), BF16),
                 shape((D, D), F32),
@@ -924,15 +1091,24 @@
             name="queries",
         )(scal, tokens, cotangent, weights[1], weights[8])
 
-    msg, recv_shared = lax.optimization_barrier((msg, recv_shared))
-    recv_other = swap_cores(recv_shared)
-    weights = make_weights()
-    summary, (weights, queries) = sum_over_points(
-        msg, count, [lambda _: weights, make_queries]
+    sources = (funcs, in_t, hid_t, hid_col)
+    cut = (steps + 1) // 2
+
+    def beside_one(_):
+        return swap_cores(recv_shared), recv_shared, make_slopes(0, cut, sources, ())
+
+    def beside_two(ready):
+        weights = make_weights(ready[1], ready[0])
+        rest = make_slopes(cut, steps, sources, ready[2]) if cut < steps else ready[2]
+        return weights, make_queries(weights), rest
+
+    summary, (_, (weights, queries, slopes)) = sum_over_points(
+        msg, count, [beside_one, beside_two]
     )
     query_w, query_t, out_w, out_t, up_w, up_t, down_w, down_t, cols = weights
     token_t, cot_t, unit, scale, norm, soft = queries
     summary_other = swap_cores(summary)
+    first, second, slope_one, slope_two = slopes
 
     (
         output_own,
@@ -950,7 +1126,6 @@
             num_scalar_prefetch=1,
             grid=(token_steps,),
             in_specs=[
-                pl.BlockSpec(memory_space=pltpu.SMEM),
                 whole((msg_rows, LANES)),
                 whole((msg_rows, LANES)),
                 pl.BlockSpec((E, token_tile), lambda i, scal_ref: (0, scal_ref[0] * token_steps + i)),
@@ -964,7 +1139,7 @@
                 whole((D, D)),
                 whole((D, D)),
                 whole((E, D, FF)),
-                whole((E, FF, D)),
+                whole((E, FF, D + 16)),
                 whole((E, FF, D)),
                 whole((E, D, FF)),
                 whole((D, D)),
@@ -986,14 +1161,15 @@
                 pltpu.VMEM((items, 4 * D, D), F32),
                 pltpu.VMEM((4 * D, token_tile), F32),
                 pltpu.VMEM((D, token_tile), F32),
+                pltpu.VMEM((4 * D, token_tile), BF16),
                 pltpu.SMEM((items + 1,), jnp.int32),
             ],
         ),
         out_shape=[
             shape((rows, D), BF16),
             shape((rows, D), F32),
-            shape((msg_rows, LANES), F32),
-            shape((msg_rows, LANES), F32),
+            pltpu.VMEM((msg_rows, LANES), F32),
+            pltpu.VMEM((msg_rows, LANES), F32),
             shape((D, D), F32),
             shape((D + 16, D), F32),
             shape((E, D + 16, FF), F32),
@@ -1007,7 +1183,6 @@
         name="tokens",
     )(
         scal,
-        item_counts,
         summary,
         summary_other,
         gate_ints.T,
@@ -1045,70 +1220,64 @@
         name="pack",
     )(scal, *parts)
 
-    def add_halves(packed):
-        return (packed[0] + swap_cores(packed[1]).astype(F32)).astype(BF16)
-
     output_other = swap_cores(output_own)
     grad_other = swap_cores(grad_own)
-    packed = [half_own, half_other]
-    summary_grad, (_, half_sum) = sum_over_points(
-        both_msg,
-        count,
-        [lambda _: packed, lambda ready: (add_halves(ready), output_other, grad_other)],
-    )
-    half_sum, output_other, grad_other = half_sum
-    summary_grad, half_sum = lax.optimization_barrier((summary_grad, half_sum))
+
+    def add_halves(packed):
+        half_sum = (packed[0] + swap_cores(packed[1]).astype(F32)).astype(BF16)
+        return half_sum, output_other, grad_other
+
+    summary_grad, (_, tail) = sum_over_points(
+        both_msg, count, [lambda _: [half_own, half_other], add_halves], 1
+    )
+    half_sum, output_other, grad_other = tail
     keys, vals, first, second, slope_one, slope_two = (
         pltpu.with_memory_space_constraint(kept, pltpu.HBM)
         for kept in (keys, vals, first, second, slope_one, slope_two)
     )
-    piece = pl.BlockSpec((rows // steps, D), lambda i, *_: (i, 0))
-    both = pl.BlockSpec((2, rows // steps, D), lambda i, *_: (0, i, 0))
+    back_tile = min(BACK_TILE, slots)
+    back_steps = slots // back_tile
     shared_recv = lax.all_to_all(half_sum, "pts", 0, 0)
-    grads_send, output, token_grad = pl.pallas_call(
+    grads_send = pl.pallas_call(
         functools.partial(
             sample_backward_kernel,
-            (tile, items, count, branch_len, height, slots, steps),
+            (back_tile, items, count, branch_len, height, slots, back_steps),
         ),
         grid_spec=pltpu.PrefetchScalarGridSpec(
             num_scalar_prefetch=1,
-            grid=(steps,),
+            grid=(1,),
             in_specs=[
-                pl.BlockSpec(memory_space=pltpu.SMEM),
                 whole((msg_rows, LANES)),
-                pl.BlockSpec((1, FIN, tile), lambda i, *_: (0, 0, i)),
-                stream(D),
-                stream(D),
-                stream(D),
-                stream(D),
-                stream(D),
-                stream(D),
+                whole((1, FIN, slots)),
+                pl.BlockSpec(memory_space=pl.ANY),
+                pl.BlockSpec(memory_space=pl.ANY),
+                pl.BlockSpec(memory_space=pl.ANY),
+                pl.BlockSpec(memory_space=pl.ANY),
+                pl.BlockSpec(memory_space=pl.ANY),
+                pl.BlockSpec(memory_space=pl.ANY),
                 whole((D, D)),
                 whole((D, 2 * D)),
-                piece,
-                piece,
-                piece,
-                piece,
             ],
-            out_specs=[whole((count, height, LANES)), both, both],
+            out_specs=whole((count, height, LANES)),
             scratch_shapes=[
+                pltpu.VMEM((6, D, slots), BF16),
                 pltpu.VMEM((vec_rows, LANES), F32),
+                pltpu.VMEM((items, D, D + 16), BF16),
                 pltpu.VMEM((items, D, D), BF16),
-                pltpu.VMEM((items, D, D), BF16),
-                pltpu.VMEM((items, D, D), F32),
-                pltpu.VMEM((D, tile), F32),
-                pltpu.VMEM((D, tile), F32),
+                pltpu.VMEM((D, back_tile), F32),
+                pltpu.VMEM((D, back_tile), F32),
                 pltpu.VMEM((D, 2 * D), F32),
                 pltpu.VMEM((D + 16, D), F32),
-                pltpu.VMEM((FIN + 1, D, D), F32),
+                pltpu.VMEM((16, D), F32),
+                pltpu.VMEM((16, back_tile), F32),
+                pltpu.VMEM((2 * D, back_tile), BF16),
+                pltpu.VMEM((D, back_tile), BF16),
+                pltpu.VMEM((D, back_tile), BF16),
                 pltpu.SMEM((items + 1,), jnp.int32),
+                pltpu.SemaphoreType.DMA((6, back_steps)),
             ],
         ),
-        out_shape=[
-            shape((count, height, LANES), BF16),
-            shape((2, rows, D), BF16),
-            shape((2, rows, D), F32),
-        ],
+        out_shape=shape((count, height, LANES), BF16),
         compiler_params=params,
         cost_estimate=pl.CostEstimate(
             flops=slots * D * D * 300, bytes_accessed=slots * D * 12, transcendentals=0
@@ -1116,7 +1285,6 @@
         name="sample_backward",
     )(
         scal,
-        func_counts,
         summary_grad,
         funcs,
         keys,
@@ -1127,13 +1295,22 @@
         slope_two,
         hid_w,
         pair_w,
-        output_own,
-        output_other,
-        grad_own,
-        grad_other,
-    )
-
-    grads_send, shared_recv = lax.optimization_barrier((grads_send, shared_recv))
+    )
+
+    grads_send, shared_recv, halves = lax.optimization_barrier(
+        (grads_send, shared_recv, (output_own, output_other, grad_own, grad_other))
+    )
+    output_own, output_other, grad_own, grad_other = halves
+    output = jnp.where(
+        core == 0,
+        jnp.concatenate([output_own, output_other]),
+        jnp.concatenate([output_other, output_own]),
+    )
+    token_grad = jnp.where(
+        core == 0,
+        jnp.concatenate([grad_own, grad_other]),
+        jnp.concatenate([grad_other, grad_own]),
+    )
     own_half = jnp.sum(shared_recv.astype(F32), axis=0).reshape(-1)
     other_half = swap_cores(own_half)
     shared_grad = jnp.where(
@@ -1150,8 +1327,8 @@
         shared_master, shared_m, shared_v, shared_grad
     )
     return (
-        output.reshape(chip_rows, D),
-        token_grad.reshape(chip_rows, D),
+        output,
+        token_grad,
         new_shared,
         new_shared_m,
         new_shared_v,

time: 102 us -> 98.4 us (0.965)
  waiting for transfers between devices: 30.6 us -> 24.5 us
  other arithmetic: 3.2 us -> 5.27 us
    ppermute x12, waiting for transfers between devices: 8.25 us -> 3.53 us  [sum_over_points(): lax.ppermute(values, 'pts', [(source, source ^ mask) for source in range(...]
    pallas_call x1 -> x3, Pallas kernels: 7.64 us -> 11.3 us  [the longest x1 6.3 us: body(): pl.pallas_call(functools.partial(sample_backward_kernel, (back_tile, item...]
    pallas_call x1, Pallas kernels: 7.82 us -> 5.54 us  [body(): pl.pallas_call(functools.partial(sample_forward_kernel, (tile, items, cou...]
    all_to_all x1, waiting for transfers between devices: 7.49 us -> 5.46 us  [body(): branch_recv = lax.all_to_all(grads_send, 'pts', 0, 0)]
    select_n x0 -> x2, other arithmetic: none -> 2.03 us  [the longest x1 1.1 us: body(): jnp.where(core == 0, jnp.concatenate([grad_own, grad_other]), jnp.concate...]
    all_to_all x1, waiting for transfers between devices: 3.34 us -> 4.8 us  [body(): shared_recv = lax.all_to_all(half_sum, 'pts', 0, 0)]
  transfers between devices with their start and end apart: 23 -> 23, of which waited for: 16 -> 10; matrix products, arithmetic and copies ran while one was open for 2% -> 4% of each run, Pallas kernels for 19% -> 21%
where the time goes in v3:
time: 98.4 us; the launch traced here: 97.9 us
  starting transfers between devices  37 us (38%)
  Pallas kernels  28 us (28%)
  waiting for transfers between devices  24.5 us (25%)
  other arithmetic  5.27 us (5%)
  local copies, waits for them, and re-layouts  2.27 us (2%)
    ppermute x12, starting transfers between devices, sum_over_points(): lax.ppermute(values, 'pts', [(source, source ^ mask) for source in range(...  16.1 us
    all_to_all x1, starting transfers between devices, body(): lax.all_to_all(copies(branch_pad.reshape(height, LANES), count), 'pts', 0...  8.44 us
    all_to_all x1, waiting for transfers between devices, body(): lax.all_to_all(copies(branch_pad.reshape(height, LANES), count), 'pts', 0...  7.73 us
    pallas_call x1, Pallas kernels, body(): pl.pallas_call(functools.partial(token_kernel, (token_tile, items, chip_r...  7.71 us
    pallas_call x1, Pallas kernels, body(): pl.pallas_call(functools.partial(sample_backward_kernel, (back_tile, item...  6.3 us
    pallas_call x1, Pallas kernels, body(): pl.pallas_call(functools.partial(sample_forward_kernel, (tile, items, cou...  5.54 us
    all_to_all x1, waiting for transfers between devices, body(): branch_recv = lax.all_to_all(grads_send, 'pts', 0, 0)  5.46 us
    pallas_call x2, Pallas kernels, make_slopes(): pl.pallas_call(slope_kernel, grid=(stop - start,), in_specs=[pl.BlockSpec...  4.96 us
  transfers between devices with their start and end apart: 23, of which 10 were waited for; matrix products, arithmetic and copies ran while one was open for 4% of the time, Pallas kernels for 21%

profile of v3, /device:TPU:0, one launch (start us, length us, event | category | flops | bytes accessed | tf_op | source)
XLA Modules:
  0.0 97.9 jit_solution(4367460370132430908)
XLA Ops:
  0.6 0.7 convert_element_type.22
  1.4 0.1 pad_reduce_fusion
  1.4 0.7 broadcast_in_dim.6
  2.1 8.4 %all-to-all-start = ((bf16[16,32,128]{2,1,0:T(8,128)(2,1)}), bf16[16,32,128]{2,1,0:T(8,128)(2,1)S(1)}, u32[]{:S(2)}, u32[]{:S(2)}) async-start(bf16[16,32,128]{2,1,0:T(8,128)(2,1)} %broadcast_in_dim.6), calls=%async_computation | async-start | bytes 262144 | tf_op jit(solution)/shard_map/all_to_all | solution.py:915
  10.6 7.7 %all-to-all-done.recv_ref = bf16[16,32,128]{2,1,0:T(8,128)(2,1)S(1)} async-done(((bf16[16,32,128]{2,1,0:T(8,128)(2,1)}), bf16[16,32,128]{2,1,0:T(8,128)(2,1)S(1)}, u32[]{:S(2)}, u32[]{:S(2)}) %all-to-all-start) | async-done | bytes 131104 | tf_op jit(solution)/shard_map/all_to_all | solution.py:915
  18.3 0.8 broadcast_in_dim.7
  19.1 3.7 %all-to-all-start.1 = ((bf16[16,80,128]{2,1,0:T(8,128)(2,1)}), bf16[16,80,128]{2,1,0:T(8,128)(2,1)S(1)}, u32[]{:S(2)}, u32[]{:S(2)}) async-start(bf16[16,80,128]{2,1,0:T(8,128)(2,1)} %broadcast_in_dim.7), calls=%async_computation.1 | async-start | bytes 655360 | tf_op jit(solution)/shard_map/all_to_all | solution.py:918
  22.8 0.1 pad_add_fusion.scal_ref
  22.9 5.5 %sample_forward.1 = (f32[72,128]{1,0:T(8,128)S(1)}, bf16[128,4096]{1,0:T(8,128)(2,1)}, bf16[128,4096]{1,0:T(8,128)(2,1)}, bf16[128,128]{1,0:T(8,128)(2,1)S(1)}, ...) custom-call(s32[2]{0:T(128)S(1)} %pad_add_fusion.scal_ref, ...), custom_call_target="tpu_custom_call" | custom-call | flops 671088640 | bytes 6291456 | tf_op jit(solution)/shard_map/sample_forward/pallas_call | solution.py:933
  28.5 1.9 %collective-permute-start = (f32[72,128]{1,0:T(8,128)S(1)}, f32[72,128]{1,0:T(8,128)S(1)}, u32[]{:S(2)}, u32[]{:S(2)}) collective-permute-start(f32[72,128]{1,0:T(8,128)S(1)} %get-tuple-element.112), channel_id=1, source_target_pairs={{0,1},{1,0},{2,3},{3,2},{4,5},{5,4},{6,7},{7,6},{8,9},{9,8},{10,11... | collective-permute-start | bytes 110600 | tf_op jit(solution)/shard_map/ppermute | solution.py:853
  30.3 1.8 %collective-permute-start.1 = (f32[72,128]{1,0:T(8,128)S(1)}, f32[72,128]{1,0:T(8,128)S(1)}, u32[]{:S(2)}, u32[]{:S(2)}) collective-permute-start(f32[72,128]{1,0:T(8,128)S(1)} %get-tuple-element.112), channel_id=1, source_target_pairs={{0,2},{1,3},{2,0},{3,1},{4,6},{5,7},{6,4},{7,5},{8,10},{9,11},{10,... | collective-permute-start | bytes 110600 | tf_op jit(solution)/shard_map/ppermute | solution.py:853
  32.1 0.0 collective-permute-start.2
  32.1 0.8 all-to-all-done.1.own_ref
  32.9 0.0 collective-permute-start.3
  32.9 2.5 %slopes.2 = (bf16[128,4096]{1,0:T(8,128)(2,1)}, bf16[128,4096]{1,0:T(8,128)(2,1)}, bf16[128,4096]{1,0:T(8,128)(2,1)}, bf16[128,4096]{1,0:T(8,128)(2,1)}) custom-call(f32[1,3,4096]{2,1,0:T(4,128)S(1)} %copy.24.func_ref, bf16[128,16]{1,0:T(8,128)(2,1)S(1)} %get-tuple-element.114.in_t_ref, bf16[128,128]{1,0:T(8,128)(2,1)S(1)} %get-tuple-element.115.hid_t_ref, ...), custom_call_target="tpu_custom_call" | custom-call | flops 4294967296 | bytes 2097152 | tf_op jit(solution)/shard_map/slopes/pallas_call | solution.py:994
  35.4 0.7 copy-done.10
  36.0 0.0 copy-done.11
  36.0 0.1 pad_add_fusion.1.scal_ref
  36.1 0.0 collective-permute-done
  36.1 0.0 collective-permute-done.1
  36.1 0.9 collective-permute-done.2
  37.0 0.0 collective-permute-done.3.other_ref
  37.0 1.2 %collective-permute-start.4 = (f32[72,128]{1,0:T(8,128)S(1)}, f32[72,128]{1,0:T(8,128)S(1)}, u32[]{:S(2)}, u32[]{:S(2)}) collective-permute-start(f32[72,128]{1,0:T(8,128)S(1)} %add_add_fusion.3), channel_id=1, source_target_pairs={{0,4},{1,5},{2,6},{3,7},{4,0},{5,1},{6,2},{7,3},{8,12},{9,13},{10,... | collective-permute-start | bytes 110600 | tf_op jit(solution)/shard_map/ppermute | solution.py:853
  38.2 2.4 %collective-permute-start.5 = (f32[72,128]{1,0:T(8,128)S(1)}, f32[72,128]{1,0:T(8,128)S(1)}, u32[]{:S(2)}, u32[]{:S(2)}) collective-permute-start(f32[72,128]{1,0:T(8,128)S(1)} %add_add_fusion.3), channel_id=1, source_target_pairs={{0,8},{1,9},{2,10},{3,11},{4,12},{5,13},{6,14},{7,15},{8,0},{9,1},... | collective-permute-start | bytes 110600 | tf_op jit(solution)/shard_map/ppermute | solution.py:853
  40.7 0.8 collective-permute-start.6
  41.5 2.5 %slopes.3 = (bf16[128,4096]{1,0:T(8,128)(2,1)}, bf16[128,4096]{1,0:T(8,128)(2,1)}, bf16[128,4096]{1,0:T(8,128)(2,1)}, bf16[128,4096]{1,0:T(8,128)(2,1)}) custom-call(f32[1,3,4096]{2,1,0:T(4,128)S(1)} %copy.24.func_ref, bf16[128,16]{1,0:T(8,128)(2,1)S(1)} %get-tuple-element.114.in_t_ref, ...), custom_call_target="tpu_custom_call", output_to_operand_aliasing={{0}: (4, {}), {1}: (5, {}), {2}: (6, {}), {3}: (7, {})} | custom-call | flops 4294967296 | bytes 2097152 | tf_op jit(solution)/shard_map/slopes/pallas_call | solution.py:994
  44.0 1.1 %weights.1 = (bf16[128,128]{1,0:T(8,128)(2,1)S(1)}, bf16[128,128]{1,0:T(8,128)(2,1)S(1)}, bf16[128,128]{1,0:T(8,128)(2,1)S(1)}, bf16[128,128]{1,0:T(8,128)(2,1)S...) custom-call(s32[10]{0:T(128)S(1)} %pad_add_fusion.1.scal_ref, ...), custom_call_target="tpu_custom_call" | custom-call | bytes 8388608 | tf_op jit(solution)/shard_map/weights/pallas_call | solution.py:1018
  45.1 1.2 %queries.1 = (bf16[128,1024]{1,0:T(8,128)(2,1)S(1)}, f32[128,1024]{1,0:T(8,128)S(1)}, f32[128,1024]{1,0:T(8,128)S(1)}, f32[8,1024]{1,0:T(8,128)S(1)}, bf16[128,1...) custom-call(s32[10]{0:T(128)S(1)} %pad_add_fusion.1.scal_ref, bf16[2048,128]{1,0:T(8,128)(2,1)S(1)} %copy-done.1, ...), custom_call_target="tpu_custom_call" | custom-call | flops 33554432 | bytes 3145728 | tf_op jit(solution)/shard_map/queries/pallas_call | solution.py:1064
  46.3 0.0 collective-permute-done.4
  46.3 0.0 collective-permute-done.5
  46.3 0.1 collective-permute-done.6
  46.4 0.1 collective-permute-start.7
  46.5 1.2 %collective-permute-done.7.other_ref = f32[72,128]{1,0:T(8,128)S(1)} collective-permute-done((f32[72,128]{1,0:T(8,128)S(1)}, f32[72,128]{1,0:T(8,128)S(1)}, u32[]{:S(2)}, u32[]{:S(2)}) %collective-permute-start.7) | collective-permute-done | bytes 36896 | tf_op jit(solution)/shard_map/ppermute | solution.py:873
  47.7 7.7 %tokens.1 = (bf16[1024,128]{1,0:T(8,128)(2,1)S(1)}, f32[1024,128]{1,0:T(8,128)S(1)}, f32[72,128]{1,0:T(8,128)S(1)}, f32[72,128]{1,0:T(8,128)S(1)}, f32[128,128]{...) custom-call(s32[10]{0:T(128)S(1)} %pad_add_fusion.1.scal_ref, ...), custom_call_target="tpu_custom_call" | custom-call | flops 1610612736 | bytes 3145728 | tf_op jit(solution)/shard_map/tokens/pallas_call | solution.py:1123
  55.4 0.2 collective-permute-start.8
  55.6 1.1 %collective-permute-done.8 = f32[72,128]{1,0:T(8,128)S(1)} collective-permute-done((f32[72,128]{1,0:T(8,128)S(1)}, f32[72,128]{1,0:T(8,128)S(1)}, u32[]{:S(2)}, u32[]{:S(2)}) %collective-permute-start.8) | collective-permute-done | bytes 36896 | tf_op jit(solution)/shard_map/ppermute | solution.py:873
  56.7 0.9 collective-permute-start.10
  57.6 2.4 %collective-permute-start.11 = (f32[72,128]{1,0:T(8,128)S(1)}, f32[72,128]{1,0:T(8,128)S(1)}, u32[]{:S(2)}, u32[]{:S(2)}) collective-permute-start(f32[72,128]{1,0:T(8,128)S(1)} %add.86), channel_id=1, source_target_pairs={{0,3},{1,2},{2,1},{3,0},{4,7},{5,6},{6,5},{7,4},{8,11},{9,10},{10,... | collective-permute-start | bytes 110600 | tf_op jit(solution)/shard_map/ppermute | solution.py:853
  59.9 0.3 collective-permute-start.9
  60.2 1.1 %pack.1 = (f32[16,80,128]{2,1,0:T(8,128)S(1)}, bf16[16,80,128]{2,1,0:T(8,128)(2,1)S(1)}) custom-call(s32[10]{0:T(128)S(1)} %pad_add_fusion.1.scal_ref, f32[128,128]{1,0:T(8,128)S(1)} %get-tuple-element.174.g_query_ref, f32[144,128]{1,0:T(8,128)S(1)} %get-tuple-element.175.g_out_ref, f32[4,144,256]{2,1,0:T(8,128)S(1)} %get-tuple-element.176.g_up_ref, ...), custom_call_target="tpu_custom_call" | custom-call | flops 2147483648 | bytes 4194304 | tf_op jit(solution)/shard_map/pack/pallas_call | solution.py:1208
  61.3 0.0 collective-permute-done.10
  61.3 1.1 %collective-permute-done.11 = f32[72,128]{1,0:T(8,128)S(1)} collective-permute-done((f32[72,128]{1,0:T(8,128)S(1)}, f32[72,128]{1,0:T(8,128)S(1)}, u32[]{:S(2)}, u32[]{:S(2)}) %collective-permute-start.11) | collective-permute-done | bytes 36896 | tf_op jit(solution)/shard_map/ppermute | solution.py:853
  62.4 1.5 %collective-permute-done.9 = f32[72,128]{1,0:T(8,128)S(1)} collective-permute-done((f32[72,128]{1,0:T(8,128)S(1)}, f32[72,128]{1,0:T(8,128)S(1)}, u32[]{:S(2)}, u32[]{:S(2)}) %collective-permute-start.9) | collective-permute-done | bytes 36896 | tf_op jit(solution)/shard_map/ppermute | solution.py:853
  63.9 0.0 collective-permute-start.13
  63.9 0.5 collective-permute-start.15
  64.4 0.0 collective-permute-start.14
  64.4 0.1 collective-permute-start.12
  64.5 2.5 %collective-permute-start.16 = (f32[72,128]{1,0:T(8,128)S(1)}, f32[72,128]{1,0:T(8,128)S(1)}, u32[]{:S(2)}, u32[]{:S(2)}) collective-permute-start(f32[72,128]{1,0:T(8,128)S(1)} %add_add_fusion.1), channel_id=1, source_target_pairs={{0,8},{1,9},{2,10},{3,11},{4,12},{5,13},{6,14},{7,15},{8,0},{9,1},... | collective-permute-start | bytes 110600 | tf_op jit(solution)/shard_map/ppermute | solution.py:853
  67.0 0.0 collective-permute-done.13
  67.0 1.9 %collective-permute-start.17 = (f32[72,128]{1,0:T(8,128)S(1)}, f32[72,128]{1,0:T(8,128)S(1)}, u32[]{:S(2)}, u32[]{:S(2)}) collective-permute-start(f32[72,128]{1,0:T(8,128)S(1)} %add_add_fusion.1), channel_id=1, source_target_pairs={{0,12},{1,13},{2,14},{3,15},{4,8},{5,9},{6,10},{7,11},{8,4},{9,5},... | collective-permute-start | bytes 110600 | tf_op jit(solution)/shard_map/ppermute | solution.py:853
  68.9 0.8 add_convert_fusion
  69.7 0.0 collective-permute-done.12
  69.7 4.4 %all-to-all-start.2 = ((bf16[16,80,128]{2,1,0:T(8,128)(2,1)}), bf16[16,80,128]{2,1,0:T(8,128)(2,1)S(1)}, u32[]{:S(2)}, u32[]{:S(2)}) async-start(bf16[16,80,128]{2,1,0:T(8,128)(2,1)} %add_convert_fusion), calls=%async_computation.2 | async-start | bytes 655360 | tf_op jit(solution)/shard_map/all_to_all | solution.py:1240
  74.1 0.0 collective-permute-done.16
  74.1 6.3 %sample_backward.1 = bf16[16,32,128]{2,1,0:T(8,128)(2,1)} custom-call(s32[10]{0:T(128)S(1)} %pad_add_fusion.1.scal_ref, f32[72,128]{1,0:T(8,128)S(1)} %add_add_fusion.msg_ref, f32[1,3,4096]{2,1,0:T(4,128)S(1)} %copy.24.func_ref, bf16[128,4096]{1,0:T(8,128)(2,1)} %get-tuple-element.189.keys_hbm, bf16[128,4096]{1,0:T(8,128)(2,1)} %get-tuple-element.190.vals_hbm, ...), custom_call_target="tpu_custom_call" | custom-call | flops 20132659200 | bytes 6291456 | tf_op jit(solution)/shard_map/sample_backward/pallas_call | solution.py:1241
  80.4 4.8 %all-to-all-done.2 = bf16[16,80,128]{2,1,0:T(8,128)(2,1)S(1)} async-done(((bf16[16,80,128]{2,1,0:T(8,128)(2,1)}), bf16[16,80,128]{2,1,0:T(8,128)(2,1)S(1)}, u32[]{:S(2)}, u32[]{:S(2)}) %all-to-all-start.2) | async-done | bytes 327712 | tf_op jit(solution)/shard_map/all_to_all | solution.py:1240
  85.2 0.1 convert_reduce_fusion
  85.3 0.1 collective-permute-start.18
  85.4 3.5 %all-to-all-start.3 = ((bf16[16,32,128]{2,1,0:T(8,128)(2,1)}), bf16[16,32,128]{2,1,0:T(8,128)(2,1)S(1)}, u32[]{:S(2)}, u32[]{:S(2)}) async-start(bf16[16,32,128]{2,1,0:T(8,128)(2,1)} %sample_backward.1), calls=%async_computation.3 | async-start | bytes 262144 | tf_op jit(solution)/shard_map/all_to_all | solution.py:1321
  88.9 1.1 %maximum_select_fusion = f32[2048,128]{1,0:T(8,128)} fusion(f32[1024,128]{1,0:T(8,128)S(1)} %collective-permute-done.15, f32[1024,128]{1,0:T(8,128)S(1)} %get-tuple-element.202, pred[]{:T(512)S(6)} %eq.2), kind=kLoop, calls=%fused_computation | loop fusion | flops 786432 | bytes 2097153 | tf_op jit(solution)/shard_map/jit(_where)/select_n | solution.py:1309
  90.0 0.9 maximum_select_fusion.1
  90.9 0.7 multiply_subtract_fusion
  91.7 5.5 %all-to-all-done.3 = bf16[16,32,128]{2,1,0:T(8,128)(2,1)S(1)} async-done(((bf16[16,32,128]{2,1,0:T(8,128)(2,1)}), bf16[16,32,128]{2,1,0:T(8,128)(2,1)S(1)}, u32[]{:S(2)}, u32[]{:S(2)}) %all-to-all-start.3) | async-done | bytes 131104 | tf_op jit(solution)/shard_map/all_to_all | solution.py:1321
  97.2 0.7 multiply_subtract_fusion.1
  (35 shorter events, 0.2 us)
Async XLA Ops:
  2.1 8.5 %copy-start.3 = (f32[18568]{0:T(1024)S(1)}, f32[18568]{0:T(1024)}, u32[]{:S(2)}) copy-start(f32[18568]{0:T(1024)} %param.18) | copy-start | bytes 222820
  2.1 16.2 %all-to-all-start = ((bf16[16,32,128]{2,1,0:T(8,128)(2,1)}), bf16[16,32,128]{2,1,0:T(8,128)(2,1)S(1)}, u32[]{:S(2)}, u32[]{:S(2)}) async-start(bf16[16,32,128]{2,1,0:T(8,128)(2,1)} %broadcast_in_dim.6), calls=%async_computation | async-start | bytes 262144 | tf_op jit(solution)/shard_map/all_to_all | solution.py:915
  19.1 3.7 %copy-start.7 = (f32[1,3,4096]{2,0,1:T(1,128)S(1)}, f32[1,3,4096]{2,0,1:T(1,128)}, u32[]{:S(2)}) copy-start(f32[1,3,4096]{2,0,1:T(1,128)} %param.13) | copy-start | bytes 147460
  19.1 13.8 %all-to-all-start.1 = ((bf16[16,80,128]{2,1,0:T(8,128)(2,1)}), bf16[16,80,128]{2,1,0:T(8,128)(2,1)S(1)}, u32[]{:S(2)}, u32[]{:S(2)}) async-start(bf16[16,80,128]{2,1,0:T(8,128)(2,1)} %broadcast_in_dim.7), calls=%async_computation.1 | async-start | bytes 655360 | tf_op jit(solution)/shard_map/all_to_all | solution.py:918
  28.5 7.7 %collective-permute-start = (f32[72,128]{1,0:T(8,128)S(1)}, f32[72,128]{1,0:T(8,128)S(1)}, u32[]{:S(2)}, u32[]{:S(2)}) collective-permute-start(f32[72,128]{1,0:T(8,128)S(1)} %get-tuple-element.112), channel_id=1, source_target_pairs={{0,1},{1,0},{2,3},{3,2},{4,5},{5,4},{6,7},{7,6},{8,9},{9,8},{10,11... | collective-permute-start | bytes 110600 | tf_op jit(solution)/shard_map/ppermute | solution.py:853
  30.3 5.8 %collective-permute-start.1 = (f32[72,128]{1,0:T(8,128)S(1)}, f32[72,128]{1,0:T(8,128)S(1)}, u32[]{:S(2)}, u32[]{:S(2)}) collective-permute-start(f32[72,128]{1,0:T(8,128)S(1)} %get-tuple-element.112), channel_id=1, source_target_pairs={{0,2},{1,3},{2,0},{3,1},{4,6},{5,7},{6,4},{7,5},{8,10},{9,11},{10,... | collective-permute-start | bytes 110600 | tf_op jit(solution)/shard_map/ppermute | solution.py:853
  32.1 4.9 %collective-permute-start.2 = (f32[72,128]{1,0:T(8,128)S(1)}, f32[72,128]{1,0:T(8,128)S(1)}, u32[]{:S(2)}, u32[]{:S(2)}) collective-permute-start(f32[72,128]{1,0:T(8,128)S(1)} %get-tuple-element.112), channel_id=1, source_target_pairs={{0,3},{1,2},{2,1},{3,0},{4,7},{5,6},{6,5},{7,4},{8,11},{9,10},{10,... | collective-permute-start | bytes 110600 | tf_op jit(solution)/shard_map/ppermute | solution.py:853
  32.9 4.1 %collective-permute-start.3 = (bf16[16,80,128]{2,1,0:T(8,128)(2,1)S(1)}, bf16[16,80,128]{2,1,0:T(8,128)(2,1)S(1)}, u32[]{:S(2)}, u32[]{:S(2)}) collective-permute-start(bf16[16,80,128]{2,1,0:T(8,128)(2,1)S(1)} %all-to-all-done.1.own_ref), channel_id=1, source_target_pairs={{0,16},{16,0},{1,17},{17,1},{2,18},{18,2},{3,19},{19,3},{4,20},{20... | collective-permute-start | bytes 983048 | tf_op jit(solution)/shard_map/ppermute | solution.py:873
  35.4 0.7 copy-start.10
  35.4 0.7 copy-start.11
  37.0 9.3 %collective-permute-start.4 = (f32[72,128]{1,0:T(8,128)S(1)}, f32[72,128]{1,0:T(8,128)S(1)}, u32[]{:S(2)}, u32[]{:S(2)}) collective-permute-start(f32[72,128]{1,0:T(8,128)S(1)} %add_add_fusion.3), channel_id=1, source_target_pairs={{0,4},{1,5},{2,6},{3,7},{4,0},{5,1},{6,2},{7,3},{8,12},{9,13},{10,... | collective-permute-start | bytes 110600 | tf_op jit(solution)/shard_map/ppermute | solution.py:853
  38.2 8.1 %collective-permute-start.5 = (f32[72,128]{1,0:T(8,128)S(1)}, f32[72,128]{1,0:T(8,128)S(1)}, u32[]{:S(2)}, u32[]{:S(2)}) collective-permute-start(f32[72,128]{1,0:T(8,128)S(1)} %add_add_fusion.3), channel_id=1, source_target_pairs={{0,8},{1,9},{2,10},{3,11},{4,12},{5,13},{6,14},{7,15},{8,0},{9,1},... | collective-permute-start | bytes 110600 | tf_op jit(solution)/shard_map/ppermute | solution.py:853
  40.7 5.8 %collective-permute-start.6 = (f32[72,128]{1,0:T(8,128)S(1)}, f32[72,128]{1,0:T(8,128)S(1)}, u32[]{:S(2)}, u32[]{:S(2)}) collective-permute-start(f32[72,128]{1,0:T(8,128)S(1)} %add_add_fusion.3), channel_id=1, source_target_pairs={{0,12},{1,13},{2,14},{3,15},{4,8},{5,9},{6,10},{7,11},{8,4},{9,5},... | collective-permute-start | bytes 110600 | tf_op jit(solution)/shard_map/ppermute | solution.py:853
  41.5 3.6 %copy-start = (f32[2048,128]{1,0:T(8,128)S(1)}, f32[2048,128]{1,0:T(8,128)}, u32[]{:S(2)}) copy-start(f32[2048,128]{1,0:T(8,128)} %cot_ref.1) | copy-start | bytes 3145732
  44.0 1.2 %copy-start.1 = (bf16[2048,128]{1,0:T(8,128)(2,1)S(1)}, bf16[2048,128]{1,0:T(8,128)(2,1)}, u32[]{:S(2)}) copy-start(bf16[2048,128]{1,0:T(8,128)(2,1)} %token_ref.1) | copy-start | bytes 1572868
  46.4 1.3 %copy-start.2 = (s32[2048,4]{0,1:T(4,128)S(1)}, s32[2048,4]{0,1:T(4,128)}, u32[]{:S(2)}) copy-start(s32[2048,4]{0,1:T(4,128)} %param.16) | copy-start | bytes 98308
  46.4 1.3 %collective-permute-start.7 = (f32[72,128]{1,0:T(8,128)S(1)}, f32[72,128]{1,0:T(8,128)S(1)}, u32[]{:S(2)}, u32[]{:S(2)}) collective-permute-start(f32[72,128]{1,0:T(8,128)S(1)} %add_add_fusion.2.own_ref), channel_id=1, source_target_pairs={{0,16},{16,0},{1,17},{17,1},{2,18},{18,2},{3,19},{19,3},{4,20},{20... | collective-permute-start | bytes 110600 | tf_op jit(solution)/shard_map/ppermute | solution.py:873
  55.4 1.3 %collective-permute-start.8 = (f32[72,128]{1,0:T(8,128)S(1)}, f32[72,128]{1,0:T(8,128)S(1)}, u32[]{:S(2)}, u32[]{:S(2)}) collective-permute-start(f32[72,128]{1,0:T(8,128)S(1)} %get-tuple-element.167), channel_id=1, source_target_pairs={{0,16},{16,0},{1,17},{17,1},{2,18},{18,2},{3,19},{19,3},{4,20},{20... | collective-permute-start | bytes 110600 | tf_op jit(solution)/shard_map/ppermute | solution.py:873
  56.7 4.6 %collective-permute-start.10 = (f32[72,128]{1,0:T(8,128)S(1)}, f32[72,128]{1,0:T(8,128)S(1)}, u32[]{:S(2)}, u32[]{:S(2)}) collective-permute-start(f32[72,128]{1,0:T(8,128)S(1)} %add.86), channel_id=1, source_target_pairs={{0,2},{1,3},{2,0},{3,1},{4,6},{5,7},{6,4},{7,5},{8,10},{9,11},{10,... | collective-permute-start | bytes 110600 | tf_op jit(solution)/shard_map/ppermute | solution.py:853
  57.6 4.9 %collective-permute-start.11 = (f32[72,128]{1,0:T(8,128)S(1)}, f32[72,128]{1,0:T(8,128)S(1)}, u32[]{:S(2)}, u32[]{:S(2)}) collective-permute-start(f32[72,128]{1,0:T(8,128)S(1)} %add.86), channel_id=1, source_target_pairs={{0,3},{1,2},{2,1},{3,0},{4,7},{5,6},{6,5},{7,4},{8,11},{9,10},{10,... | collective-permute-start | bytes 110600 | tf_op jit(solution)/shard_map/ppermute | solution.py:853
  59.9 4.0 %collective-permute-start.9 = (f32[72,128]{1,0:T(8,128)S(1)}, f32[72,128]{1,0:T(8,128)S(1)}, u32[]{:S(2)}, u32[]{:S(2)}) collective-permute-start(f32[72,128]{1,0:T(8,128)S(1)} %add.86), channel_id=1, source_target_pairs={{0,1},{1,0},{2,3},{3,2},{4,5},{5,4},{6,7},{7,6},{8,9},{9,8},{10,11... | collective-permute-start | bytes 110600 | tf_op jit(solution)/shard_map/ppermute | solution.py:853
  63.9 3.1 %collective-permute-start.13 = (bf16[16,80,128]{2,1,0:T(8,128)(2,1)S(1)}, bf16[16,80,128]{2,1,0:T(8,128)(2,1)S(1)}, u32[]{:S(2)}, u32[]{:S(2)}) collective-permute-start(bf16[16,80,128]{2,1,0:T(8,128)(2,1)S(1)} %get-tuple-element.185), channel_id=1, source_target_pairs={{0,16},{16,0},{1,17},{17,1},{2,18},{18,2},{3,19},{19,3},{4,20},{20... | collective-permute-start | bytes 983048 | tf_op jit(solution)/shard_map/ppermute | solution.py:873
  63.9 5.8 %collective-permute-start.15 = (f32[1024,128]{1,0:T(8,128)S(1)}, f32[1024,128]{1,0:T(8,128)S(1)}, u32[]{:S(2)}, u32[]{:S(2)}) collective-permute-start(f32[1024,128]{1,0:T(8,128)S(1)} %get-tuple-element.202), channel_id=1, source_target_pairs={{0,16},{16,0},{1,17},{17,1},{2,18},{18,2},{3,19},{19,3},{4,20},{20... | collective-permute-start | bytes 1572872 | tf_op jit(solution)/shard_map/ppermute | solution.py:873
  64.4 5.3 %collective-permute-start.14 = (bf16[1024,128]{1,0:T(8,128)(2,1)S(1)}, bf16[1024,128]{1,0:T(8,128)(2,1)S(1)}, u32[]{:S(2)}, u32[]{:S(2)}) collective-permute-start(bf16[1024,128]{1,0:T(8,128)(2,1)S(1)} %get-tuple-element.200), channel_id=1, source_target_pairs={{0,16},{16,0},{1,17},{17,1},{2,18},{18,2},{3,19},{19,3},{4,20},{20... | collective-permute-start | bytes 786440 | tf_op jit(solution)/shard_map/ppermute | solution.py:873
  64.4 5.3 %collective-permute-start.12 = (f32[72,128]{1,0:T(8,128)S(1)}, f32[72,128]{1,0:T(8,128)S(1)}, u32[]{:S(2)}, u32[]{:S(2)}) collective-permute-start(f32[72,128]{1,0:T(8,128)S(1)} %add_add_fusion.1), channel_id=1, source_target_pairs={{0,4},{1,5},{2,6},{3,7},{4,0},{5,1},{6,2},{7,3},{8,12},{9,13},{10,... | collective-permute-start | bytes 110600 | tf_op jit(solution)/shard_map/ppermute | solution.py:853
  64.5 9.6 %collective-permute-start.16 = (f32[72,128]{1,0:T(8,128)S(1)}, f32[72,128]{1,0:T(8,128)S(1)}, u32[]{:S(2)}, u32[]{:S(2)}) collective-permute-start(f32[72,128]{1,0:T(8,128)S(1)} %add_add_fusion.1), channel_id=1, source_target_pairs={{0,8},{1,9},{2,10},{3,11},{4,12},{5,13},{6,14},{7,15},{8,0},{9,1},... | collective-permute-start | bytes 110600 | tf_op jit(solution)/shard_map/ppermute | solution.py:853
  67.0 7.1 %collective-permute-start.17 = (f32[72,128]{1,0:T(8,128)S(1)}, f32[72,128]{1,0:T(8,128)S(1)}, u32[]{:S(2)}, u32[]{:S(2)}) collective-permute-start(f32[72,128]{1,0:T(8,128)S(1)} %add_add_fusion.1), channel_id=1, source_target_pairs={{0,12},{1,13},{2,14},{3,15},{4,8},{5,9},{6,10},{7,11},{8,4},{9,5},... | collective-permute-start | bytes 110600 | tf_op jit(solution)/shard_map/ppermute | solution.py:853
  69.7 15.5 %all-to-all-start.2 = ((bf16[16,80,128]{2,1,0:T(8,128)(2,1)}), bf16[16,80,128]{2,1,0:T(8,128)(2,1)S(1)}, u32[]{:S(2)}, u32[]{:S(2)}) async-start(bf16[16,80,128]{2,1,0:T(8,128)(2,1)} %add_convert_fusion), calls=%async_computation.2 | async-start | bytes 655360 | tf_op jit(solution)/shard_map/all_to_all | solution.py:1240
  85.3 5.6 %collective-permute-start.18 = (f32[10240]{0:T(1024)S(1)}, f32[10240]{0:T(1024)S(1)}, u32[]{:S(2)}, u32[]{:S(2)}) collective-permute-start(f32[10240]{0:T(1024)S(1)} %bitcast.10), channel_id=1, source_target_pairs={{0,16},{16,0},{1,17},{17,1},{2,18},{18,2},{3,19},{19,3},{4,20},{20... | collective-permute-start | bytes 122888 | tf_op jit(solution)/shard_map/ppermute | solution.py:873
  85.4 11.8 %all-to-all-start.3 = ((bf16[16,32,128]{2,1,0:T(8,128)(2,1)}), bf16[16,32,128]{2,1,0:T(8,128)(2,1)S(1)}, u32[]{:S(2)}, u32[]{:S(2)}) async-start(bf16[16,32,128]{2,1,0:T(8,128)(2,1)} %sample_backward.1), calls=%async_computation.3 | async-start | bytes 262144 | tf_op jit(solution)/shard_map/all_to_all | solution.py:1321
  90.0 0.9 copy-start.4
  90.0 0.9 copy-start.5
  91.7 5.5 %copy-start.6 = (f32[1,3112]{1,0:T(1,128)S(1)}, f32[1,3112]{1,0:T(1,128)}, u32[]{:S(2)}) copy-start(f32[1,3112]{1,0:T(1,128)} %param.21) | copy-start | bytes 37348
  91.7 5.5 %copy-start.8 = (f32[1,3112]{1,0:T(1,128)S(1)}, f32[1,3112]{1,0:T(1,128)}, u32[]{:S(2)}) copy-start(f32[1,3112]{1,0:T(1,128)} %param.22) | copy-start | bytes 37348
  91.7 5.5 %copy-start.9 = (f32[1,3112]{1,0:T(1,128)S(1)}, f32[1,3112]{1,0:T(1,128)}, u32[]{:S(2)}) copy-start(f32[1,3112]{1,0:T(1,128)} %param.23) | copy-start | bytes 37348

commit v4 on v3

--- a/solution.py
+++ b/solution.py
@@ -27,7 +27,7 @@
 VMEM_BASE = 16 * 1024 * 1024
 VMEM_ITEM = 768 * 1024
 SAMPLE_TILE = 2048
-BACK_TILE = 2048
+BACK_TILE = 4096
 TOKEN_TILE = 1024
 CHUNK = 256
 
@@ -356,29 +356,6 @@
         for item in range(items):
             msg_ref[item * HD : (item + 1) * HD, :] = fold_heads(acc_ref[item, :D, :], mask)
             msg_ref[items * HD + item : items * HD + item + 1, :] = acc_ref[item, D : D + 1, :]
-
-
-def slope_kernel(func_ref, in_t_ref, hid_t_ref, col_ref, *refs):
-    first_ref, second_ref, slope_one_ref, slope_two_ref, parts_ref = refs[-5:]
-    samples = split_samples(func_ref[0], parts_ref)
-    chunk = min(CHUNK, samples.shape[1])
-
-    def slopes(start):
-        at = slice(start, start + chunk)
-        first_in = dot_nn(in_t_ref[...], samples[:, at])
-        yield
-        first, slope_one = gelu_parts(first_in)
-        first = first.astype(BF16)
-        first_ref[:, at] = first
-        slope_one_ref[:, at] = slope_one.astype(BF16)
-        yield
-        second_in = dot_nn(hid_t_ref[...], first)
-        yield
-        second, slope_two = gelu_parts(second_in + wide(col_ref[...], chunk))
-        second_ref[:, at] = second.astype(BF16)
-        slope_two_ref[:, at] = slope_two.astype(BF16)
-
-    staggered([slopes(start) for start in range(0, samples.shape[1], chunk)])
 
 
 def weight_kernel(
@@ -710,10 +687,9 @@
     func_ref,
     keys_hbm,
     vals_hbm,
-    first_hbm,
-    second_hbm,
-    slope_one_hbm,
-    slope_two_hbm,
+    in_t_ref,
+    hid_t_ref,
+    col_ref,
     hid_ref,
     pair_ref,
     send_ref,
@@ -730,11 +706,13 @@
     pairs_ref,
     seconds_ref,
     firsts_ref,
+    first_ref,
+    second_ref,
     starts,
     sems,
 ):
     tile, items, parts, shard, height, slots, steps = plan
-    sources = (keys_hbm, vals_hbm, second_hbm, slope_two_hbm, first_hbm, slope_one_hbm)
+    sources = (keys_hbm, vals_hbm)
     fetches = [
         [
             pltpu.make_async_copy(
@@ -781,9 +759,7 @@
         def part(number):
             return kept_ref.at[number, :, step * tile : (step + 1) * tile]
 
-        keys_ref, vals_ref, second_ref, slope_two_ref, first_ref, slope_one_ref = (
-            part(number) for number in range(6)
-        )
+        keys_ref, vals_ref = part(0), part(1)
         fetches[step][0].wait()
         fetches[step][1].wait()
         keys = keys_ref[...]
@@ -800,12 +776,20 @@
 
         over_items(starts, items, begin, tile, visit)
         samples = split_samples(func_ref[0, :, step * tile : (step + 1) * tile], parts_ref)
-        for number in range(2, 6):
-            fetches[step][number].wait()
         chunk = min(CHUNK, tile)
 
         def backward(start):
             at = slice(start, start + chunk)
+            first_in = dot_nn(in_t_ref[...], samples[:, at])
+            yield
+            first, slope_one = gelu_parts(first_in)
+            first = first.astype(BF16)
+            first_ref[:, at] = first
+            yield
+            second_in = dot_nn(hid_t_ref[...], first)
+            yield
+            second, slope_two = gelu_parts(second_in + wide(col_ref[...], chunk))
+            second_ref[:, at] = second.astype(BF16)
             soft = keys_ref[:, at].astype(F32)
             grad_keys = keys_acc_ref[:, at]
             grad_in = soft * (grad_keys - head_sum(grad_keys * soft))
@@ -814,12 +798,12 @@
             yield
             grad_second = dot_nn(pair_ref[...], grad_pair)
             yield
-            grad_second = (slope_two_ref[:, at].astype(F32) * grad_second).astype(BF16)
+            grad_second = (slope_two * grad_second).astype(BF16)
             seconds_ref[:, at] = grad_second
             yield
             grad_first = dot_nn(hid_ref[...], grad_second)
             yield
-            firsts_ref[:, at] = (slope_one_ref[:, at].astype(F32) * grad_first).astype(BF16)
+            firsts_ref[:, at] = (slope_one * grad_first).astype(BF16)
 
         staggered([backward(start) for start in range(0, tile, chunk)])
         g_pair_ref[...] += dot_nt(second_ref[...], pairs_ref[...])
@@ -844,7 +828,7 @@
         send_ref[number] = take_shard(vec_ref, number, shard, height).astype(BF16)
 
 
-def sum_over_points(values, count, besides, early=3):
+def sum_over_points(values, count, besides, early):
     bit = 1
     number = 0
     while bit < count:
@@ -854,10 +838,10 @@
             for mask in masks
         ]
         if number < len(besides):
+            some = early[number]
             before = besides[number - 1] if number else None
-            some = early if number else len(masks)
-            pieces[:some], besides[number] = lax.optimization_barrier(
-                (pieces[:some], besides[number](before))
+            pieces[some], besides[number] = lax.optimization_barrier(
+                (pieces[some], besides[number](before))
             )
         values = functools.reduce(jnp.add, pieces, values)
         bit *= 4
@@ -990,28 +974,6 @@
     scal = jnp.concatenate([place, item_counts, func_counts.reshape(-1)])
 
 
-    def make_slopes(start, stop, sources, given):
-        return pl.pallas_call(
-            slope_kernel,
-            grid=(stop - start,),
-            in_specs=[
-                pl.BlockSpec((1, FIN, tile), lambda i: (0, 0, i + start)),
-                whole((D, 16)),
-                whole((D, D)),
-                whole((D, D)),
-            ]
-            + [pl.BlockSpec(memory_space=pl.ANY)] * len(given),
-            out_specs=[pl.BlockSpec((D, tile), lambda i: (0, i + start))] * 4,
-            out_shape=[pltpu.HBM((D, slots), BF16)] * 4,
-            scratch_shapes=[pltpu.VMEM((16, tile), F32)],
-            input_output_aliases={4 + number: number for number in range(len(given))},
-            compiler_params=params,
-            cost_estimate=pl.CostEstimate(
-                flops=4 << 30, bytes_accessed=slots * D * 4, transcendentals=slots * D
-            ),
-            name="slopes",
-        )(*sources, *given)
-
     shared_rows = up_to(SHARED_ROWS + 2 * half + 8, 8)
 
     def make_weights(recv_shared, recv_other):
@@ -1091,24 +1053,16 @@
             name="queries",
         )(scal, tokens, cotangent, weights[1], weights[8])
 
-    sources = (funcs, in_t, hid_t, hid_col)
-    cut = (steps + 1) // 2
-
-    def beside_one(_):
-        return swap_cores(recv_shared), recv_shared, make_slopes(0, cut, sources, ())
-
-    def beside_two(ready):
-        weights = make_weights(ready[1], ready[0])
-        rest = make_slopes(cut, steps, sources, ready[2]) if cut < steps else ready[2]
-        return weights, make_queries(weights), rest
-
-    summary, (_, (weights, queries, slopes)) = sum_over_points(
-        msg, count, [beside_one, beside_two]
+    def beside_two(received):
+        weights = make_weights(received, swap_cores(received))
+        return weights, make_queries(weights)
+
+    summary, (_, (weights, queries)) = sum_over_points(
+        msg, count, [lambda _: recv_shared, beside_two], (slice(1), slice(3))
     )
     query_w, query_t, out_w, out_t, up_w, up_t, down_w, down_t, cols = weights
     token_t, cot_t, unit, scale, norm, soft = queries
     summary_other = swap_cores(summary)
-    first, second, slope_one, slope_two = slopes
 
     (
         output_own,
@@ -1228,13 +1182,10 @@
         return half_sum, output_other, grad_other
 
     summary_grad, (_, tail) = sum_over_points(
-        both_msg, count, [lambda _: [half_own, half_other], add_halves], 1
+        both_msg, count, [lambda _: [half_own, half_other], add_halves], (slice(3), slice(2, 3))
     )
     half_sum, output_other, grad_other = tail
-    keys, vals, first, second, slope_one, slope_two = (
-        pltpu.with_memory_space_constraint(kept, pltpu.HBM)
-        for kept in (keys, vals, first, second, slope_one, slope_two)
-    )
+    keys, vals = (pltpu.with_memory_space_constraint(kept, pltpu.HBM) for kept in (keys, vals))
     back_tile = min(BACK_TILE, slots)
     back_steps = slots // back_tile
     shared_recv = lax.all_to_all(half_sum, "pts", 0, 0)
@@ -1251,16 +1202,15 @@
                 whole((1, FIN, slots)),
                 pl.BlockSpec(memory_space=pl.ANY),
                 pl.BlockSpec(memory_space=pl.ANY),
-                pl.BlockSpec(memory_space=pl.ANY),
-                pl.BlockSpec(memory_space=pl.ANY),
-                pl.BlockSpec(memory_space=pl.ANY),
-                pl.BlockSpec(memory_space=pl.ANY),
+                whole((D, 16)),
+                whole((D, D)),
+                whole((D, D)),
                 whole((D, D)),
                 whole((D, 2 * D)),
             ],
             out_specs=whole((count, height, LANES)),
             scratch_shapes=[
-                pltpu.VMEM((6, D, slots), BF16),
+                pltpu.VMEM((2, D, slots), BF16),
                 pltpu.VMEM((vec_rows, LANES), F32),
                 pltpu.VMEM((items, D, D + 16), BF16),
                 pltpu.VMEM((items, D, D), BF16),
@@ -1273,12 +1223,16 @@
                 pltpu.VMEM((2 * D, back_tile), BF16),
                 pltpu.VMEM((D, back_tile), BF16),
                 pltpu.VMEM((D, back_tile), BF16),
+                pltpu.VMEM((D, back_tile), BF16),
+                pltpu.VMEM((D, back_tile), BF16),
                 pltpu.SMEM((items + 1,), jnp.int32),
-                pltpu.SemaphoreType.DMA((6, back_steps)),
+                pltpu.SemaphoreType.DMA((2, back_steps)),
             ],
         ),
         out_shape=shape((count, height, LANES), BF16),
-        compiler_params=params,
+        compiler_params=pltpu.CompilerParams(
+            vmem_limit_bytes=2 * VMEM_BASE + items * VMEM_ITEM
+        ),
         cost_estimate=pl.CostEstimate(
             flops=slots * D * D * 300, bytes_accessed=slots * D * 12, transcendentals=0
         ),
@@ -1289,10 +1243,9 @@
         funcs,
         keys,
         vals,
-        first,
-        second,
-        slope_one,
-        slope_two,
+        in_t,
+        hid_t,
+        hid_col,
         hid_w,
         pair_w,
     )

time: 98.4 us -> 96 us (0.976)
  Pallas kernels: 28 us -> 24.8 us
  starting transfers between devices: 37 us -> 38.6 us
    pallas_call x2 -> x0, Pallas kernels: 4.96 us -> none  [make_slopes(): pl.pallas_call(slope_kernel, grid=(stop - start,), in_specs=[pl.BlockSpec...]
    ppermute x12, waiting for transfers between devices: 3.53 us -> 6.93 us  [sum_over_points(): lax.ppermute(values, 'pts', [(source, source ^ mask) for source in range(...]
    all_to_all x1, waiting for transfers between devices: 4.8 us -> 2.57 us  [body(): shared_recv = lax.all_to_all(half_sum, 'pts', 0, 0)]
    pallas_call x1, Pallas kernels: 6.3 us -> 8.14 us  [body(): pl.pallas_call(functools.partial(sample_backward_kernel, (back_tile, item...]
    ppermute x7, starting transfers between devices: 0.88 us -> 2.63 us  [swap_cores(): return lax.ppermute(values, 'branch', [(0, 1), (1, 0)])]
  transfers between devices with their start and end apart: 23 -> 23, of which waited for: 10 -> 12; matrix products, arithmetic and copies ran while one was open for 4% -> 4% of each run, Pallas kernels for 21% -> 18%
where the time goes in v4:
time: 96 us; the launch traced here: 95.3 us
  starting transfers between devices  38.6 us (40%)
  Pallas kernels  24.8 us (26%)
  waiting for transfers between devices  24.2 us (25%)
  other arithmetic  5.28 us (6%)
  local copies, waits for them, and re-layouts  1.61 us (2%)
    ppermute x12, starting transfers between devices, sum_over_points(): lax.ppermute(values, 'pts', [(source, source ^ mask) for source in range(...  15.9 us
    all_to_all x1, starting transfers between devices, body(): lax.all_to_all(copies(branch_pad.reshape(height, LANES), count), 'pts', 0...  8.44 us
    pallas_call x1, Pallas kernels, body(): pl.pallas_call(functools.partial(sample_backward_kernel, (back_tile, item...  8.14 us
    all_to_all x1, waiting for transfers between devices, body(): lax.all_to_all(copies(branch_pad.reshape(height, LANES), count), 'pts', 0...  7.73 us
    pallas_call x1, Pallas kernels, body(): pl.pallas_call(functools.partial(token_kernel, (token_tile, items, chip_r...  7.7 us
    ppermute x12, waiting for transfers between devices, sum_over_points(): lax.ppermute(values, 'pts', [(source, source ^ mask) for source in range(...  6.93 us
    pallas_call x1, Pallas kernels, body(): pl.pallas_call(functools.partial(sample_forward_kernel, (tile, items, cou...  5.51 us
    all_to_all x1, waiting for transfers between devices, body(): branch_recv = lax.all_to_all(grads_send, 'pts', 0, 0)  4.88 us
  transfers between devices with their start and end apart: 23, of which 12 were waited for; matrix products, arithmetic and copies ran while one was open for 4% of the time, Pallas kernels for 18%

profile of v4, /device:TPU:0, one launch (start us, length us, event | category | flops | bytes accessed | tf_op | source)
XLA Modules:
  0.0 95.3 jit_solution(11762405296848004059)
XLA Ops:
  0.6 0.7 convert_element_type.22
  1.4 0.1 pad_reduce_fusion
  1.4 0.7 broadcast_in_dim.6
  2.1 8.4 %all-to-all-start = ((bf16[16,32,128]{2,1,0:T(8,128)(2,1)}), bf16[16,32,128]{2,1,0:T(8,128)(2,1)S(1)}, u32[]{:S(2)}, u32[]{:S(2)}) async-start(bf16[16,32,128]{2,1,0:T(8,128)(2,1)} %broadcast_in_dim.6), calls=%async_computation | async-start | bytes 262144 | tf_op jit(solution)/shard_map/all_to_all | solution.py:899
  10.6 7.7 %all-to-all-done.recv_ref = bf16[16,32,128]{2,1,0:T(8,128)(2,1)S(1)} async-done(((bf16[16,32,128]{2,1,0:T(8,128)(2,1)}), bf16[16,32,128]{2,1,0:T(8,128)(2,1)S(1)}, u32[]{:S(2)}, u32[]{:S(2)}) %all-to-all-start) | async-done | bytes 131104 | tf_op jit(solution)/shard_map/all_to_all | solution.py:899
  18.3 0.8 broadcast_in_dim.7
  19.1 3.7 %all-to-all-start.1 = ((bf16[16,80,128]{2,1,0:T(8,128)(2,1)}), bf16[16,80,128]{2,1,0:T(8,128)(2,1)S(1)}, u32[]{:S(2)}, u32[]{:S(2)}) async-start(bf16[16,80,128]{2,1,0:T(8,128)(2,1)} %broadcast_in_dim.7), calls=%async_computation.1 | async-start | bytes 655360 | tf_op jit(solution)/shard_map/all_to_all | solution.py:902
  22.8 0.1 pad_add_fusion.scal_ref
  22.9 5.5 %sample_forward.1 = (f32[72,128]{1,0:T(8,128)S(1)}, bf16[128,4096]{1,0:T(8,128)(2,1)}, bf16[128,4096]{1,0:T(8,128)(2,1)}, bf16[128,128]{1,0:T(8,128)(2,1)S(1)}, ...) custom-call(s32[2]{0:T(128)S(1)} %pad_add_fusion.scal_ref, ...), custom_call_target="tpu_custom_call" | custom-call | flops 671088640 | bytes 6291456 | tf_op jit(solution)/shard_map/sample_forward/pallas_call | solution.py:917
  28.4 0.0 copy-start.1
  28.5 1.9 %collective-permute-start = (f32[72,128]{1,0:T(8,128)S(1)}, f32[72,128]{1,0:T(8,128)S(1)}, u32[]{:S(2)}, u32[]{:S(2)}) collective-permute-start(f32[72,128]{1,0:T(8,128)S(1)} %get-tuple-element.93), channel_id=1, source_target_pairs={{0,1},{1,0},{2,3},{3,2},{4,5},{5,4},{6,7},{7,6},{8,9},{9,8},{10,11... | collective-permute-start | bytes 110600 | tf_op jit(solution)/shard_map/ppermute | solution.py:837
  30.3 1.5 %collective-permute-start.2 = (f32[72,128]{1,0:T(8,128)S(1)}, f32[72,128]{1,0:T(8,128)S(1)}, u32[]{:S(2)}, u32[]{:S(2)}) collective-permute-start(f32[72,128]{1,0:T(8,128)S(1)} %get-tuple-element.93), channel_id=1, source_target_pairs={{0,3},{1,2},{2,1},{3,0},{4,7},{5,6},{6,5},{7,4},{8,11},{9,10},{10,... | collective-permute-start | bytes 110600 | tf_op jit(solution)/shard_map/ppermute | solution.py:837
  31.8 0.2 collective-permute-start.1
  32.0 0.9 collective-permute-done
  32.9 0.0 all-to-all-done.1.own_ref
  32.9 0.0 collective-permute-start.6
  32.9 2.3 %collective-permute-done.2 = f32[72,128]{1,0:T(8,128)S(1)} collective-permute-done((f32[72,128]{1,0:T(8,128)S(1)}, f32[72,128]{1,0:T(8,128)S(1)}, u32[]{:S(2)}, u32[]{:S(2)}) %collective-permute-start.2) | collective-permute-done | bytes 36896 | tf_op jit(solution)/shard_map/ppermute | solution.py:837
  35.2 0.6 collective-permute-done.1
  35.8 3.6 %collective-permute-start.5 = (f32[72,128]{1,0:T(8,128)S(1)}, f32[72,128]{1,0:T(8,128)S(1)}, u32[]{:S(2)}, u32[]{:S(2)}) collective-permute-start(f32[72,128]{1,0:T(8,128)S(1)} %add_add_fusion.3), channel_id=1, source_target_pairs={{0,12},{1,13},{2,14},{3,15},{4,8},{5,9},{6,10},{7,11},{8,4},{9,5},... | collective-permute-start | bytes 110600 | tf_op jit(solution)/shard_map/ppermute | solution.py:837
  39.3 0.0 collective-permute-start.4
  39.3 0.9 collective-permute-start.3
  40.2 0.1 pad_add_fusion.1.scal_ref
  40.3 0.0 collective-permute-done.6.other_ref
  40.3 1.1 %weights.1 = (bf16[128,128]{1,0:T(8,128)(2,1)S(1)}, bf16[128,128]{1,0:T(8,128)(2,1)S(1)}, bf16[128,128]{1,0:T(8,128)(2,1)S(1)}, bf16[128,128]{1,0:T(8,128)(2,1)S...) custom-call(s32[10]{0:T(128)S(1)} %pad_add_fusion.1.scal_ref, ...), custom_call_target="tpu_custom_call" | custom-call | bytes 8388608 | tf_op jit(solution)/shard_map/weights/pallas_call | solution.py:980
  41.5 1.2 %queries.1 = (bf16[128,1024]{1,0:T(8,128)(2,1)S(1)}, f32[128,1024]{1,0:T(8,128)S(1)}, f32[128,1024]{1,0:T(8,128)S(1)}, f32[8,1024]{1,0:T(8,128)S(1)}, bf16[128,1...) custom-call(s32[10]{0:T(128)S(1)} %pad_add_fusion.1.scal_ref, bf16[2048,128]{1,0:T(8,128)(2,1)S(1)} %copy-done.1, ...), custom_call_target="tpu_custom_call" | custom-call | flops 33554432 | bytes 3145728 | tf_op jit(solution)/shard_map/queries/pallas_call | solution.py:1026
  42.7 0.0 collective-permute-done.5
  42.7 1.5 %collective-permute-done.4 = f32[72,128]{1,0:T(8,128)S(1)} collective-permute-done((f32[72,128]{1,0:T(8,128)S(1)}, f32[72,128]{1,0:T(8,128)S(1)}, u32[]{:S(2)}, u32[]{:S(2)}) %collective-permute-start.4) | collective-permute-done | bytes 36896 | tf_op jit(solution)/shard_map/ppermute | solution.py:837
  44.2 0.0 collective-permute-done.3
  44.2 0.1 collective-permute-start.7
  44.3 1.2 %collective-permute-done.7.other_ref = f32[72,128]{1,0:T(8,128)S(1)} collective-permute-done((f32[72,128]{1,0:T(8,128)S(1)}, f32[72,128]{1,0:T(8,128)S(1)}, u32[]{:S(2)}, u32[]{:S(2)}) %collective-permute-start.7) | collective-permute-done | bytes 36896 | tf_op jit(solution)/shard_map/ppermute | solution.py:857
  45.5 7.7 %tokens.1 = (bf16[1024,128]{1,0:T(8,128)(2,1)S(1)}, f32[1024,128]{1,0:T(8,128)S(1)}, f32[72,128]{1,0:T(8,128)S(1)}, f32[72,128]{1,0:T(8,128)S(1)}, f32[128,128]{...) custom-call(s32[10]{0:T(128)S(1)} %pad_add_fusion.1.scal_ref, ...), custom_call_target="tpu_custom_call" | custom-call | flops 1610612736 | bytes 3145728 | tf_op jit(solution)/shard_map/tokens/pallas_call | solution.py:1077
  53.2 2.0 %collective-permute-start.8 = (f32[72,128]{1,0:T(8,128)S(1)}, f32[72,128]{1,0:T(8,128)S(1)}, u32[]{:S(2)}, u32[]{:S(2)}) collective-permute-start(f32[72,128]{1,0:T(8,128)S(1)} %get-tuple-element.130), channel_id=1, source_target_pairs={{0,16},{16,0},{1,17},{17,1},{2,18},{18,2},{3,19},{19,3},{4,20},{20... | collective-permute-start | bytes 110600 | tf_op jit(solution)/shard_map/ppermute | solution.py:857
  55.2 0.9 collective-permute-done.8
  56.0 0.1 collective-permute-start.11
  56.1 1.1 %collective-permute-start.10 = (f32[72,128]{1,0:T(8,128)S(1)}, f32[72,128]{1,0:T(8,128)S(1)}, u32[]{:S(2)}, u32[]{:S(2)}) collective-permute-start(f32[72,128]{1,0:T(8,128)S(1)} %add.86), channel_id=1, source_target_pairs={{0,2},{1,3},{2,0},{3,1},{4,6},{5,7},{6,4},{7,5},{8,10},{9,11},{10,... | collective-permute-start | bytes 110600 | tf_op jit(solution)/shard_map/ppermute | solution.py:837
  57.3 2.3 %collective-permute-start.9 = (f32[72,128]{1,0:T(8,128)S(1)}, f32[72,128]{1,0:T(8,128)S(1)}, u32[]{:S(2)}, u32[]{:S(2)}) collective-permute-start(f32[72,128]{1,0:T(8,128)S(1)} %add.86), channel_id=1, source_target_pairs={{0,1},{1,0},{2,3},{3,2},{4,5},{5,4},{6,7},{7,6},{8,9},{9,8},{10,11... | collective-permute-start | bytes 110600 | tf_op jit(solution)/shard_map/ppermute | solution.py:837
  59.5 1.1 %pack.1 = (f32[16,80,128]{2,1,0:T(8,128)S(1)}, bf16[16,80,128]{2,1,0:T(8,128)(2,1)S(1)}) custom-call(s32[10]{0:T(128)S(1)} %pad_add_fusion.1.scal_ref, f32[128,128]{1,0:T(8,128)S(1)} %get-tuple-element.137.g_query_ref, f32[144,128]{1,0:T(8,128)S(1)} %get-tuple-element.138.g_out_ref, f32[4,144,256]{2,1,0:T(8,128)S(1)} %get-tuple-element.139.g_up_ref, ...), custom_call_target="tpu_custom_call" | custom-call | flops 2147483648 | bytes 4194304 | tf_op jit(solution)/shard_map/pack/pallas_call | solution.py:1162
  60.7 0.4 collective-permute-done.11
  61.1 0.0 collective-permute-done.10
  61.1 0.4 collective-permute-done.9
  61.5 0.0 collective-permute-start.15
  61.5 0.5 collective-permute-start.17
  62.0 0.0 collective-permute-start.16
  62.0 1.8 %collective-permute-start.14 = (f32[72,128]{1,0:T(8,128)S(1)}, f32[72,128]{1,0:T(8,128)S(1)}, u32[]{:S(2)}, u32[]{:S(2)}) collective-permute-start(f32[72,128]{1,0:T(8,128)S(1)} %add_add_fusion.1), channel_id=1, source_target_pairs={{0,12},{1,13},{2,14},{3,15},{4,8},{5,9},{6,10},{7,11},{8,4},{9,5},... | collective-permute-start | bytes 110600 | tf_op jit(solution)/shard_map/ppermute | solution.py:837
  63.8 0.1 collective-permute-start.13
  63.9 0.0 collective-permute-done.15
  63.9 2.5 %collective-permute-start.12 = (f32[72,128]{1,0:T(8,128)S(1)}, f32[72,128]{1,0:T(8,128)S(1)}, u32[]{:S(2)}, u32[]{:S(2)}) collective-permute-start(f32[72,128]{1,0:T(8,128)S(1)} %add_add_fusion.1), channel_id=1, source_target_pairs={{0,4},{1,5},{2,6},{3,7},{4,0},{5,1},{6,2},{7,3},{8,12},{9,13},{10,... | collective-permute-start | bytes 110600 | tf_op jit(solution)/shard_map/ppermute | solution.py:837
  66.4 0.8 add_convert_fusion
  67.3 0.9 collective-permute-done.14
  68.1 0.0 collective-permute-done.16
  68.1 0.0 collective-permute-done.17
  68.1 3.5 %all-to-all-start.2 = ((bf16[16,80,128]{2,1,0:T(8,128)(2,1)}), bf16[16,80,128]{2,1,0:T(8,128)(2,1)S(1)}, u32[]{:S(2)}, u32[]{:S(2)}) async-start(bf16[16,80,128]{2,1,0:T(8,128)(2,1)} %add_convert_fusion), calls=%async_computation.2 | async-start | bytes 655360 | tf_op jit(solution)/shard_map/all_to_all | solution.py:1191
  71.7 0.0 collective-permute-done.13
  71.7 0.0 collective-permute-done.12
  71.7 8.1 %sample_backward.1 = bf16[16,32,128]{2,1,0:T(8,128)(2,1)} custom-call(s32[10]{0:T(128)S(1)} %pad_add_fusion.1.scal_ref, f32[72,128]{1,0:T(8,128)S(1)} %add_add_fusion.msg_ref, f32[1,3,4096]{2,1,0:T(4,128)S(1)} %copy.20.func_ref, bf16[128,4096]{1,0:T(8,128)(2,1)} %get-tuple-element.152.keys_hbm, bf16[128,4096]{1,0:T(8,128)(2,1)} %get-tuple-element.153.vals_hbm, ...), custom_call_target="tpu_custom_call" | custom-call | flops 20132659200 | bytes 6291456 | tf_op jit(solution)/shard_map/sample_backward/pallas_call | solution.py:1192
  79.9 2.6 %all-to-all-done.2 = bf16[16,80,128]{2,1,0:T(8,128)(2,1)S(1)} async-done(((bf16[16,80,128]{2,1,0:T(8,128)(2,1)}), bf16[16,80,128]{2,1,0:T(8,128)(2,1)S(1)}, u32[]{:S(2)}, u32[]{:S(2)}) %all-to-all-start.2) | async-done | bytes 327712 | tf_op jit(solution)/shard_map/all_to_all | solution.py:1191
  82.4 4.3 %all-to-all-start.3 = ((bf16[16,32,128]{2,1,0:T(8,128)(2,1)}), bf16[16,32,128]{2,1,0:T(8,128)(2,1)S(1)}, u32[]{:S(2)}, u32[]{:S(2)}) async-start(bf16[16,32,128]{2,1,0:T(8,128)(2,1)} %sample_backward.1), calls=%async_computation.3 | async-start | bytes 262144 | tf_op jit(solution)/shard_map/all_to_all | solution.py:1274
  86.8 0.1 convert_reduce_fusion
  86.8 0.1 collective-permute-start.18
  86.9 1.1 %maximum_select_fusion = f32[2048,128]{1,0:T(8,128)} fusion(f32[1024,128]{1,0:T(8,128)S(1)} %collective-permute-done.17, f32[1024,128]{1,0:T(8,128)S(1)} %get-tuple-element.164, pred[]{:T(512)S(6)} %eq.2), kind=kLoop, calls=%fused_computation | loop fusion | flops 786432 | bytes 2097153 | tf_op jit(solution)/shard_map/jit(_where)/select_n | solution.py:1262
  88.0 0.9 maximum_select_fusion.1
  89.0 0.7 multiply_subtract_fusion
  89.7 4.9 %all-to-all-done.3 = bf16[16,32,128]{2,1,0:T(8,128)(2,1)S(1)} async-done(((bf16[16,32,128]{2,1,0:T(8,128)(2,1)}), bf16[16,32,128]{2,1,0:T(8,128)(2,1)S(1)}, u32[]{:S(2)}, u32[]{:S(2)}) %all-to-all-start.3) | async-done | bytes 131104 | tf_op jit(solution)/shard_map/all_to_all | solution.py:1274
  94.6 0.7 multiply_subtract_fusion.1
  (33 shorter events, 0.2 us)
Async XLA Ops:
  2.1 8.5 %copy-start.3 = (f32[18568]{0:T(1024)S(1)}, f32[18568]{0:T(1024)}, u32[]{:S(2)}) copy-start(f32[18568]{0:T(1024)} %param.18) | copy-start | bytes 222820
  2.1 16.2 %all-to-all-start = ((bf16[16,32,128]{2,1,0:T(8,128)(2,1)}), bf16[16,32,128]{2,1,0:T(8,128)(2,1)S(1)}, u32[]{:S(2)}, u32[]{:S(2)}) async-start(bf16[16,32,128]{2,1,0:T(8,128)(2,1)} %broadcast_in_dim.6), calls=%async_computation | async-start | bytes 262144 | tf_op jit(solution)/shard_map/all_to_all | solution.py:899
  19.1 3.7 %copy-start.7 = (f32[1,3,4096]{2,0,1:T(1,128)S(1)}, f32[1,3,4096]{2,0,1:T(1,128)}, u32[]{:S(2)}) copy-start(f32[1,3,4096]{2,0,1:T(1,128)} %param.13) | copy-start | bytes 147460
  19.1 13.8 %all-to-all-start.1 = ((bf16[16,80,128]{2,1,0:T(8,128)(2,1)}), bf16[16,80,128]{2,1,0:T(8,128)(2,1)S(1)}, u32[]{:S(2)}, u32[]{:S(2)}) async-start(bf16[16,80,128]{2,1,0:T(8,128)(2,1)} %broadcast_in_dim.7), calls=%async_computation.1 | async-start | bytes 655360 | tf_op jit(solution)/shard_map/all_to_all | solution.py:902
  22.9 17.3 %copy-start.10 = (s32[1,4]{1,0:T(1,128)S(1)}, s32[1,4]{1,0:T(1,128)}, u32[]{:S(2)}) copy-start(s32[1,4]{1,0:T(1,128)} %count_hbm.1) | copy-start | bytes 52
  22.9 17.3 %copy-start.11 = (s32[4]{0:T(128)S(1)}, s32[4]{0:T(128)}, u32[]{:S(2)}) copy-start(s32[4]{0:T(128)} %param.14) | copy-start | bytes 52
  22.9 18.5 %copy-start = (f32[2048,128]{1,0:T(8,128)S(1)}, f32[2048,128]{1,0:T(8,128)}, u32[]{:S(2)}) copy-start(f32[2048,128]{1,0:T(8,128)} %cot_ref.1) | copy-start | bytes 3145732
  28.4 13.0 %copy-start.1 = (bf16[2048,128]{1,0:T(8,128)(2,1)S(1)}, bf16[2048,128]{1,0:T(8,128)(2,1)}, u32[]{:S(2)}) copy-start(bf16[2048,128]{1,0:T(8,128)(2,1)} %token_ref.1) | copy-start | bytes 1572868
  28.5 4.4 %collective-permute-start = (f32[72,128]{1,0:T(8,128)S(1)}, f32[72,128]{1,0:T(8,128)S(1)}, u32[]{:S(2)}, u32[]{:S(2)}) collective-permute-start(f32[72,128]{1,0:T(8,128)S(1)} %get-tuple-element.93), channel_id=1, source_target_pairs={{0,1},{1,0},{2,3},{3,2},{4,5},{5,4},{6,7},{7,6},{8,9},{9,8},{10,11... | collective-permute-start | bytes 110600 | tf_op jit(solution)/shard_map/ppermute | solution.py:837
  30.3 4.9 %collective-permute-start.2 = (f32[72,128]{1,0:T(8,128)S(1)}, f32[72,128]{1,0:T(8,128)S(1)}, u32[]{:S(2)}, u32[]{:S(2)}) collective-permute-start(f32[72,128]{1,0:T(8,128)S(1)} %get-tuple-element.93), channel_id=1, source_target_pairs={{0,3},{1,2},{2,1},{3,0},{4,7},{5,6},{6,5},{7,4},{8,11},{9,10},{10,... | collective-permute-start | bytes 110600 | tf_op jit(solution)/shard_map/ppermute | solution.py:837
  31.8 4.0 %collective-permute-start.1 = (f32[72,128]{1,0:T(8,128)S(1)}, f32[72,128]{1,0:T(8,128)S(1)}, u32[]{:S(2)}, u32[]{:S(2)}) collective-permute-start(f32[72,128]{1,0:T(8,128)S(1)} %get-tuple-element.93), channel_id=1, source_target_pairs={{0,2},{1,3},{2,0},{3,1},{4,6},{5,7},{6,4},{7,5},{8,10},{9,11},{10,... | collective-permute-start | bytes 110600 | tf_op jit(solution)/shard_map/ppermute | solution.py:837
  32.9 7.4 %collective-permute-start.6 = (bf16[16,80,128]{2,1,0:T(8,128)(2,1)S(1)}, bf16[16,80,128]{2,1,0:T(8,128)(2,1)S(1)}, u32[]{:S(2)}, u32[]{:S(2)}) collective-permute-start(bf16[16,80,128]{2,1,0:T(8,128)(2,1)S(1)} %all-to-all-done.1.own_ref), channel_id=1, source_target_pairs={{0,16},{16,0},{1,17},{17,1},{2,18},{18,2},{3,19},{19,3},{4,20},{20... | collective-permute-start | bytes 983048 | tf_op jit(solution)/shard_map/ppermute | solution.py:857
  35.8 6.9 %collective-permute-start.5 = (f32[72,128]{1,0:T(8,128)S(1)}, f32[72,128]{1,0:T(8,128)S(1)}, u32[]{:S(2)}, u32[]{:S(2)}) collective-permute-start(f32[72,128]{1,0:T(8,128)S(1)} %add_add_fusion.3), channel_id=1, source_target_pairs={{0,12},{1,13},{2,14},{3,15},{4,8},{5,9},{6,10},{7,11},{8,4},{9,5},... | collective-permute-start | bytes 110600 | tf_op jit(solution)/shard_map/ppermute | solution.py:837
  39.3 4.9 %collective-permute-start.4 = (f32[72,128]{1,0:T(8,128)S(1)}, f32[72,128]{1,0:T(8,128)S(1)}, u32[]{:S(2)}, u32[]{:S(2)}) collective-permute-start(f32[72,128]{1,0:T(8,128)S(1)} %add_add_fusion.3), channel_id=1, source_target_pairs={{0,8},{1,9},{2,10},{3,11},{4,12},{5,13},{6,14},{7,15},{8,0},{9,1},... | collective-permute-start | bytes 110600 | tf_op jit(solution)/shard_map/ppermute | solution.py:837
  39.3 4.9 %collective-permute-start.3 = (f32[72,128]{1,0:T(8,128)S(1)}, f32[72,128]{1,0:T(8,128)S(1)}, u32[]{:S(2)}, u32[]{:S(2)}) collective-permute-start(f32[72,128]{1,0:T(8,128)S(1)} %add_add_fusion.3), channel_id=1, source_target_pairs={{0,4},{1,5},{2,6},{3,7},{4,0},{5,1},{6,2},{7,3},{8,12},{9,13},{10,... | collective-permute-start | bytes 110600 | tf_op jit(solution)/shard_map/ppermute | solution.py:837
  44.2 1.3 %copy-start.2 = (s32[2048,4]{0,1:T(4,128)S(1)}, s32[2048,4]{0,1:T(4,128)}, u32[]{:S(2)}) copy-start(s32[2048,4]{0,1:T(4,128)} %param.16) | copy-start | bytes 98308
  44.2 1.3 %collective-permute-start.7 = (f32[72,128]{1,0:T(8,128)S(1)}, f32[72,128]{1,0:T(8,128)S(1)}, u32[]{:S(2)}, u32[]{:S(2)}) collective-permute-start(f32[72,128]{1,0:T(8,128)S(1)} %add_add_fusion.2.own_ref), channel_id=1, source_target_pairs={{0,16},{16,0},{1,17},{17,1},{2,18},{18,2},{3,19},{19,3},{4,20},{20... | collective-permute-start | bytes 110600 | tf_op jit(solution)/shard_map/ppermute | solution.py:857
  53.2 2.8 %collective-permute-start.8 = (f32[72,128]{1,0:T(8,128)S(1)}, f32[72,128]{1,0:T(8,128)S(1)}, u32[]{:S(2)}, u32[]{:S(2)}) collective-permute-start(f32[72,128]{1,0:T(8,128)S(1)} %get-tuple-element.130), channel_id=1, source_target_pairs={{0,16},{16,0},{1,17},{17,1},{2,18},{18,2},{3,19},{19,3},{4,20},{20... | collective-permute-start | bytes 110600 | tf_op jit(solution)/shard_map/ppermute | solution.py:857
  56.0 5.0 %collective-permute-start.11 = (f32[72,128]{1,0:T(8,128)S(1)}, f32[72,128]{1,0:T(8,128)S(1)}, u32[]{:S(2)}, u32[]{:S(2)}) collective-permute-start(f32[72,128]{1,0:T(8,128)S(1)} %add.86), channel_id=1, source_target_pairs={{0,3},{1,2},{2,1},{3,0},{4,7},{5,6},{6,5},{7,4},{8,11},{9,10},{10,... | collective-permute-start | bytes 110600 | tf_op jit(solution)/shard_map/ppermute | solution.py:837
  56.1 5.0 %collective-permute-start.10 = (f32[72,128]{1,0:T(8,128)S(1)}, f32[72,128]{1,0:T(8,128)S(1)}, u32[]{:S(2)}, u32[]{:S(2)}) collective-permute-start(f32[72,128]{1,0:T(8,128)S(1)} %add.86), channel_id=1, source_target_pairs={{0,2},{1,3},{2,0},{3,1},{4,6},{5,7},{6,4},{7,5},{8,10},{9,11},{10,... | collective-permute-start | bytes 110600 | tf_op jit(solution)/shard_map/ppermute | solution.py:837
  57.3 4.2 %collective-permute-start.9 = (f32[72,128]{1,0:T(8,128)S(1)}, f32[72,128]{1,0:T(8,128)S(1)}, u32[]{:S(2)}, u32[]{:S(2)}) collective-permute-start(f32[72,128]{1,0:T(8,128)S(1)} %add.86), channel_id=1, source_target_pairs={{0,1},{1,0},{2,3},{3,2},{4,5},{5,4},{6,7},{7,6},{8,9},{9,8},{10,11... | collective-permute-start | bytes 110600 | tf_op jit(solution)/shard_map/ppermute | solution.py:837
  61.5 2.5 %collective-permute-start.15 = (bf16[16,80,128]{2,1,0:T(8,128)(2,1)S(1)}, bf16[16,80,128]{2,1,0:T(8,128)(2,1)S(1)}, u32[]{:S(2)}, u32[]{:S(2)}) collective-permute-start(bf16[16,80,128]{2,1,0:T(8,128)(2,1)S(1)} %get-tuple-element.148), channel_id=1, source_target_pairs={{0,16},{16,0},{1,17},{17,1},{2,18},{18,2},{3,19},{19,3},{4,20},{20... | collective-permute-start | bytes 983048 | tf_op jit(solution)/shard_map/ppermute | solution.py:857
  61.5 6.7 %collective-permute-start.17 = (f32[1024,128]{1,0:T(8,128)S(1)}, f32[1024,128]{1,0:T(8,128)S(1)}, u32[]{:S(2)}, u32[]{:S(2)}) collective-permute-start(f32[1024,128]{1,0:T(8,128)S(1)} %get-tuple-element.164), channel_id=1, source_target_pairs={{0,16},{16,0},{1,17},{17,1},{2,18},{18,2},{3,19},{19,3},{4,20},{20... | collective-permute-start | bytes 1572872 | tf_op jit(solution)/shard_map/ppermute | solution.py:857
  62.0 6.2 %collective-permute-start.16 = (bf16[1024,128]{1,0:T(8,128)(2,1)S(1)}, bf16[1024,128]{1,0:T(8,128)(2,1)S(1)}, u32[]{:S(2)}, u32[]{:S(2)}) collective-permute-start(bf16[1024,128]{1,0:T(8,128)(2,1)S(1)} %get-tuple-element.162), channel_id=1, source_target_pairs={{0,16},{16,0},{1,17},{17,1},{2,18},{18,2},{3,19},{19,3},{4,20},{20... | collective-permute-start | bytes 786440 | tf_op jit(solution)/shard_map/ppermute | solution.py:857
  62.0 6.1 %collective-permute-start.14 = (f32[72,128]{1,0:T(8,128)S(1)}, f32[72,128]{1,0:T(8,128)S(1)}, u32[]{:S(2)}, u32[]{:S(2)}) collective-permute-start(f32[72,128]{1,0:T(8,128)S(1)} %add_add_fusion.1), channel_id=1, source_target_pairs={{0,12},{1,13},{2,14},{3,15},{4,8},{5,9},{6,10},{7,11},{8,4},{9,5},... | collective-permute-start | bytes 110600 | tf_op jit(solution)/shard_map/ppermute | solution.py:837
  63.8 7.9 %collective-permute-start.13 = (f32[72,128]{1,0:T(8,128)S(1)}, f32[72,128]{1,0:T(8,128)S(1)}, u32[]{:S(2)}, u32[]{:S(2)}) collective-permute-start(f32[72,128]{1,0:T(8,128)S(1)} %add_add_fusion.1), channel_id=1, source_target_pairs={{0,8},{1,9},{2,10},{3,11},{4,12},{5,13},{6,14},{7,15},{8,0},{9,1},... | collective-permute-start | bytes 110600 | tf_op jit(solution)/shard_map/ppermute | solution.py:837
  63.9 7.8 %collective-permute-start.12 = (f32[72,128]{1,0:T(8,128)S(1)}, f32[72,128]{1,0:T(8,128)S(1)}, u32[]{:S(2)}, u32[]{:S(2)}) collective-permute-start(f32[72,128]{1,0:T(8,128)S(1)} %add_add_fusion.1), channel_id=1, source_target_pairs={{0,4},{1,5},{2,6},{3,7},{4,0},{5,1},{6,2},{7,3},{8,12},{9,13},{10,... | collective-permute-start | bytes 110600 | tf_op jit(solution)/shard_map/ppermute | solution.py:837
  68.1 14.3 %all-to-all-start.2 = ((bf16[16,80,128]{2,1,0:T(8,128)(2,1)}), bf16[16,80,128]{2,1,0:T(8,128)(2,1)S(1)}, u32[]{:S(2)}, u32[]{:S(2)}) async-start(bf16[16,80,128]{2,1,0:T(8,128)(2,1)} %add_convert_fusion), calls=%async_computation.2 | async-start | bytes 655360 | tf_op jit(solution)/shard_map/all_to_all | solution.py:1191
  82.4 12.1 %all-to-all-start.3 = ((bf16[16,32,128]{2,1,0:T(8,128)(2,1)}), bf16[16,32,128]{2,1,0:T(8,128)(2,1)S(1)}, u32[]{:S(2)}, u32[]{:S(2)}) async-start(bf16[16,32,128]{2,1,0:T(8,128)(2,1)} %sample_backward.1), calls=%async_computation.3 | async-start | bytes 262144 | tf_op jit(solution)/shard_map/all_to_all | solution.py:1274
  86.8 2.1 %collective-permute-start.18 = (f32[10240]{0:T(1024)S(1)}, f32[10240]{0:T(1024)S(1)}, u32[]{:S(2)}, u32[]{:S(2)}) collective-permute-start(f32[10240]{0:T(1024)S(1)} %bitcast.10), channel_id=1, source_target_pairs={{0,16},{16,0},{1,17},{17,1},{2,18},{18,2},{3,19},{19,3},{4,20},{20... | collective-permute-start | bytes 122888 | tf_op jit(solution)/shard_map/ppermute | solution.py:857
  88.0 0.9 copy-start.4
  88.0 0.9 copy-start.5
  89.7 4.9 %copy-start.6 = (f32[1,3112]{1,0:T(1,128)S(1)}, f32[1,3112]{1,0:T(1,128)}, u32[]{:S(2)}) copy-start(f32[1,3112]{1,0:T(1,128)} %param.21) | copy-start | bytes 37348
  89.7 4.9 %copy-start.8 = (f32[1,3112]{1,0:T(1,128)S(1)}, f32[1,3112]{1,0:T(1,128)}, u32[]{:S(2)}) copy-start(f32[1,3112]{1,0:T(1,128)} %param.22) | copy-start | bytes 37348
  89.7 4.9 %copy-start.9 = (f32[1,3112]{1,0:T(1,128)S(1)}, f32[1,3112]{1,0:T(1,128)}, u32[]{:S(2)}) copy-start(f32[1,3112]{1,0:T(1,128)} %param.23) | copy-start | bytes 37348

commit v5 on v4

--- a/solution.py
+++ b/solution.py
@@ -741,17 +741,22 @@
         def build(item, carry):
             at = pl.multiple_of(item * HD, HD)
             block = spread_heads(msg_ref[pl.ds(at, HD), :], mask)
-            left_vals_ref[item] = block.astype(BF16)
+            high = block.astype(BF16)
+            left_vals_ref[item, :, :D] = high
+            left_vals_ref[item, :, D:] = (block - high.astype(F32)).astype(BF16)
             row = msg_ref[pl.ds(items * HD + item, 1), :]
             both = jnp.concatenate([block, row, jnp.zeros((D - 1, D), F32)], axis=0)
-            left_keys_ref[item] = jnp.transpose(both)[:, : D + 16].astype(BF16)
+            both = jnp.transpose(both)[:, : D + 16]
+            high = both.astype(BF16)
+            left_keys_ref[item, 0] = high
+            left_keys_ref[item, 1] = (both - high.astype(F32)).astype(BF16)
             return carry
 
         @pl.when(high <= low)
         def _():
             last = items - 1
-            left_vals_ref[last] = jnp.zeros((D, D), BF16)
-            left_keys_ref[last] = jnp.zeros((D, D + 16), BF16)
+            left_vals_ref[last] = jnp.zeros((D, 2 * D), BF16)
+            left_keys_ref[last] = jnp.zeros((2, D, D + 16), BF16)
 
         lax.fori_loop(low, high, build, 0)
 
@@ -769,8 +774,12 @@
 
         def visit(item, opening):
             row = item_row(starts, item, begin, tile)
-            fresh_keys = row * dot_nn(left_keys_ref[item], vals_ones)
-            fresh_vals = row * dot_nn(left_vals_ref[item], keys)
+            fresh_keys = row * (
+                dot_nn(left_keys_ref[item, 0], vals_ones) + dot_nn(left_keys_ref[item, 1], vals_ones)
+            )
+            fresh_vals = row * dot_nn(
+                left_vals_ref[item], jnp.concatenate([keys, keys], axis=0)
+            )
             keys_acc_ref[...] = fresh_keys if opening else keys_acc_ref[...] + fresh_keys
             vals_acc_ref[...] = fresh_vals if opening else vals_acc_ref[...] + fresh_vals
 
@@ -1212,8 +1221,8 @@
             scratch_shapes=[
                 pltpu.VMEM((2, D, slots), BF16),
                 pltpu.VMEM((vec_rows, LANES), F32),
-                pltpu.VMEM((items, D, D + 16), BF16),
-                pltpu.VMEM((items, D, D), BF16),
+                pltpu.VMEM((items, 2, D, D + 16), BF16),
+                pltpu.VMEM((items, D, 2 * D), BF16),
                 pltpu.VMEM((D, back_tile), F32),
                 pltpu.VMEM((D, back_tile), F32),
                 pltpu.VMEM((D, 2 * D), F32),

time: 96 us -> 96.8 us (level)
    ppermute x7, starting transfers between devices: 2.63 us -> 0.88 us  [swap_cores(): return lax.ppermute(values, 'branch', [(0, 1), (1, 0)])]
    ppermute x12, waiting for transfers between devices: 6.93 us -> 7.92 us  [sum_over_points(): lax.ppermute(values, 'pts', [(source, source ^ mask) for source in range(...]
  transfers between devices with their start and end apart: 23 -> 23, of which waited for: 12 -> 13; matrix products, arithmetic and copies ran while one was open for 4% -> 4% of each run, Pallas kernels for 18% -> 18%
where the time goes in v5:
time: 96.8 us; the launch traced here: 95.7 us
  starting transfers between devices  38 us (39%)
  Pallas kernels  25.1 us (26%)
  waiting for transfers between devices  24.9 us (26%)
  other arithmetic  5.28 us (5%)
  local copies, waits for them, and re-layouts  1.61 us (2%)
    ppermute x12, starting transfers between devices, sum_over_points(): lax.ppermute(values, 'pts', [(source, source ^ mask) for source in range(...  16.1 us
    all_to_all x1, starting transfers between devices, body(): lax.all_to_all(copies(branch_pad.reshape(height, LANES), count), 'pts', 0...  8.44 us
    pallas_call x1, Pallas kernels, body(): pl.pallas_call(functools.partial(sample_backward_kernel, (back_tile, item...  8.42 us
    ppermute x12, waiting for transfers between devices, sum_over_points(): lax.ppermute(values, 'pts', [(source, source ^ mask) for source in range(...  7.92 us
    all_to_all x1, waiting for transfers between devices, body(): lax.all_to_all(copies(branch_pad.reshape(height, LANES), count), 'pts', 0...  7.73 us
    pallas_call x1, Pallas kernels, body(): pl.pallas_call(functools.partial(token_kernel, (token_tile, items, chip_r...  7.7 us
    pallas_call x1, Pallas kernels, body(): pl.pallas_call(functools.partial(sample_forward_kernel, (tile, items, cou...  5.51 us
    all_to_all x1, starting transfers between devices, body(): branch_recv = lax.all_to_all(grads_send, 'pts', 0, 0)  4.96 us
  transfers between devices with their start and end apart: 23, of which 13 were waited for; matrix products, arithmetic and copies ran while one was open for 4% of the time, Pallas kernels for 18%

profile of v5, /device:TPU:0, one launch (start us, length us, event | category | flops | bytes accessed | tf_op | source)
XLA Modules:
  0.0 95.7 jit_solution(8935694988129495601)
XLA Ops:
  0.6 0.7 convert_element_type.22
  1.4 0.1 pad_reduce_fusion
  1.4 0.7 broadcast_in_dim.6
  2.1 8.4 %all-to-all-start = ((bf16[16,32,128]{2,1,0:T(8,128)(2,1)}), bf16[16,32,128]{2,1,0:T(8,128)(2,1)S(1)}, u32[]{:S(2)}, u32[]{:S(2)}) async-start(bf16[16,32,128]{2,1,0:T(8,128)(2,1)} %broadcast_in_dim.6), calls=%async_computation | async-start | bytes 262144 | tf_op jit(solution)/shard_map/all_to_all | solution.py:908
  10.6 7.7 %all-to-all-done.recv_ref = bf16[16,32,128]{2,1,0:T(8,128)(2,1)S(1)} async-done(((bf16[16,32,128]{2,1,0:T(8,128)(2,1)}), bf16[16,32,128]{2,1,0:T(8,128)(2,1)S(1)}, u32[]{:S(2)}, u32[]{:S(2)}) %all-to-all-start) | async-done | bytes 131104 | tf_op jit(solution)/shard_map/all_to_all | solution.py:908
  18.3 0.8 broadcast_in_dim.7
  19.1 3.7 %all-to-all-start.1 = ((bf16[16,80,128]{2,1,0:T(8,128)(2,1)}), bf16[16,80,128]{2,1,0:T(8,128)(2,1)S(1)}, u32[]{:S(2)}, u32[]{:S(2)}) async-start(bf16[16,80,128]{2,1,0:T(8,128)(2,1)} %broadcast_in_dim.7), calls=%async_computation.1 | async-start | bytes 655360 | tf_op jit(solution)/shard_map/all_to_all | solution.py:911
  22.8 0.1 pad_add_fusion.scal_ref
  22.9 5.5 %sample_forward.1 = (f32[72,128]{1,0:T(8,128)S(1)}, bf16[128,4096]{1,0:T(8,128)(2,1)}, bf16[128,4096]{1,0:T(8,128)(2,1)}, bf16[128,128]{1,0:T(8,128)(2,1)S(1)}, ...) custom-call(s32[2]{0:T(128)S(1)} %pad_add_fusion.scal_ref, ...), custom_call_target="tpu_custom_call" | custom-call | flops 671088640 | bytes 6291456 | tf_op jit(solution)/shard_map/sample_forward/pallas_call | solution.py:926
  28.4 0.0 copy-start.1
  28.5 1.9 %collective-permute-start = (f32[72,128]{1,0:T(8,128)S(1)}, f32[72,128]{1,0:T(8,128)S(1)}, u32[]{:S(2)}, u32[]{:S(2)}) collective-permute-start(f32[72,128]{1,0:T(8,128)S(1)} %get-tuple-element.93), channel_id=1, source_target_pairs={{0,1},{1,0},{2,3},{3,2},{4,5},{5,4},{6,7},{7,6},{8,9},{9,8},{10,11... | collective-permute-start | bytes 110600 | tf_op jit(solution)/shard_map/ppermute | solution.py:846
  30.3 1.5 %collective-permute-start.2 = (f32[72,128]{1,0:T(8,128)S(1)}, f32[72,128]{1,0:T(8,128)S(1)}, u32[]{:S(2)}, u32[]{:S(2)}) collective-permute-start(f32[72,128]{1,0:T(8,128)S(1)} %get-tuple-element.93), channel_id=1, source_target_pairs={{0,3},{1,2},{2,1},{3,0},{4,7},{5,6},{6,5},{7,4},{8,11},{9,10},{10,... | collective-permute-start | bytes 110600 | tf_op jit(solution)/shard_map/ppermute | solution.py:846
  31.8 0.3 collective-permute-start.1
  32.1 0.8 collective-permute-done
  32.9 0.0 all-to-all-done.1.own_ref
  32.9 0.0 collective-permute-start.6
  32.9 2.3 %collective-permute-done.2 = f32[72,128]{1,0:T(8,128)S(1)} collective-permute-done((f32[72,128]{1,0:T(8,128)S(1)}, f32[72,128]{1,0:T(8,128)S(1)}, u32[]{:S(2)}, u32[]{:S(2)}) %collective-permute-start.2) | collective-permute-done | bytes 36896 | tf_op jit(solution)/shard_map/ppermute | solution.py:846
  35.2 0.6 collective-permute-done.1
  35.8 3.6 %collective-permute-start.5 = (f32[72,128]{1,0:T(8,128)S(1)}, f32[72,128]{1,0:T(8,128)S(1)}, u32[]{:S(2)}, u32[]{:S(2)}) collective-permute-start(f32[72,128]{1,0:T(8,128)S(1)} %add_add_fusion.3), channel_id=1, source_target_pairs={{0,12},{1,13},{2,14},{3,15},{4,8},{5,9},{6,10},{7,11},{8,4},{9,5},... | collective-permute-start | bytes 110600 | tf_op jit(solution)/shard_map/ppermute | solution.py:846
  39.3 0.0 collective-permute-start.4
  39.3 0.9 collective-permute-start.3
  40.2 0.1 pad_add_fusion.1.scal_ref
  40.3 0.0 collective-permute-done.6.other_ref
  40.3 1.1 %weights.1 = (bf16[128,128]{1,0:T(8,128)(2,1)S(1)}, bf16[128,128]{1,0:T(8,128)(2,1)S(1)}, bf16[128,128]{1,0:T(8,128)(2,1)S(1)}, bf16[128,128]{1,0:T(8,128)(2,1)S...) custom-call(s32[10]{0:T(128)S(1)} %pad_add_fusion.1.scal_ref, ...), custom_call_target="tpu_custom_call" | custom-call | bytes 8388608 | tf_op jit(solution)/shard_map/weights/pallas_call | solution.py:989
  41.5 1.2 %queries.1 = (bf16[128,1024]{1,0:T(8,128)(2,1)S(1)}, f32[128,1024]{1,0:T(8,128)S(1)}, f32[128,1024]{1,0:T(8,128)S(1)}, f32[8,1024]{1,0:T(8,128)S(1)}, bf16[128,1...) custom-call(s32[10]{0:T(128)S(1)} %pad_add_fusion.1.scal_ref, bf16[2048,128]{1,0:T(8,128)(2,1)S(1)} %copy-done.1, ...), custom_call_target="tpu_custom_call" | custom-call | flops 33554432 | bytes 3145728 | tf_op jit(solution)/shard_map/queries/pallas_call | solution.py:1035
  42.7 0.0 collective-permute-done.5
  42.7 1.5 %collective-permute-done.4 = f32[72,128]{1,0:T(8,128)S(1)} collective-permute-done((f32[72,128]{1,0:T(8,128)S(1)}, f32[72,128]{1,0:T(8,128)S(1)}, u32[]{:S(2)}, u32[]{:S(2)}) %collective-permute-start.4) | collective-permute-done | bytes 36896 | tf_op jit(solution)/shard_map/ppermute | solution.py:846
  44.2 0.0 collective-permute-done.3
  44.2 0.1 collective-permute-start.7
  44.3 1.2 %collective-permute-done.7.other_ref = f32[72,128]{1,0:T(8,128)S(1)} collective-permute-done((f32[72,128]{1,0:T(8,128)S(1)}, f32[72,128]{1,0:T(8,128)S(1)}, u32[]{:S(2)}, u32[]{:S(2)}) %collective-permute-start.7) | collective-permute-done | bytes 36896 | tf_op jit(solution)/shard_map/ppermute | solution.py:866
  45.5 7.7 %tokens.1 = (bf16[1024,128]{1,0:T(8,128)(2,1)S(1)}, f32[1024,128]{1,0:T(8,128)S(1)}, f32[72,128]{1,0:T(8,128)S(1)}, f32[72,128]{1,0:T(8,128)S(1)}, f32[128,128]{...) custom-call(s32[10]{0:T(128)S(1)} %pad_add_fusion.1.scal_ref, ...), custom_call_target="tpu_custom_call" | custom-call | flops 1610612736 | bytes 3145728 | tf_op jit(solution)/shard_map/tokens/pallas_call | solution.py:1086
  53.2 0.2 collective-permute-start.8
  53.4 1.1 %collective-permute-done.8 = f32[72,128]{1,0:T(8,128)S(1)} collective-permute-done((f32[72,128]{1,0:T(8,128)S(1)}, f32[72,128]{1,0:T(8,128)S(1)}, u32[]{:S(2)}, u32[]{:S(2)}) %collective-permute-start.8) | collective-permute-done | bytes 36896 | tf_op jit(solution)/shard_map/ppermute | solution.py:866
  54.5 1.6 %collective-permute-start.11 = (f32[72,128]{1,0:T(8,128)S(1)}, f32[72,128]{1,0:T(8,128)S(1)}, u32[]{:S(2)}, u32[]{:S(2)}) collective-permute-start(f32[72,128]{1,0:T(8,128)S(1)} %add.86), channel_id=1, source_target_pairs={{0,3},{1,2},{2,1},{3,0},{4,7},{5,6},{6,5},{7,4},{8,11},{9,10},{10,... | collective-permute-start | bytes 110600 | tf_op jit(solution)/shard_map/ppermute | solution.py:846
  56.1 1.1 %collective-permute-start.10 = (f32[72,128]{1,0:T(8,128)S(1)}, f32[72,128]{1,0:T(8,128)S(1)}, u32[]{:S(2)}, u32[]{:S(2)}) collective-permute-start(f32[72,128]{1,0:T(8,128)S(1)} %add.86), channel_id=1, source_target_pairs={{0,2},{1,3},{2,0},{3,1},{4,6},{5,7},{6,4},{7,5},{8,10},{9,11},{10,... | collective-permute-start | bytes 110600 | tf_op jit(solution)/shard_map/ppermute | solution.py:846
  57.3 0.7 collective-permute-start.9
  58.0 1.1 %pack.1 = (f32[16,80,128]{2,1,0:T(8,128)S(1)}, bf16[16,80,128]{2,1,0:T(8,128)(2,1)S(1)}) custom-call(s32[10]{0:T(128)S(1)} %pad_add_fusion.1.scal_ref, f32[128,128]{1,0:T(8,128)S(1)} %get-tuple-element.137.g_query_ref, f32[144,128]{1,0:T(8,128)S(1)} %get-tuple-element.138.g_out_ref, f32[4,144,256]{2,1,0:T(8,128)S(1)} %get-tuple-element.139.g_up_ref, ...), custom_call_target="tpu_custom_call" | custom-call | flops 2147483648 | bytes 4194304 | tf_op jit(solution)/shard_map/pack/pallas_call | solution.py:1171
  59.1 0.3 collective-permute-done.11
  59.4 0.7 collective-permute-done.10
  60.1 1.1 %collective-permute-done.9 = f32[72,128]{1,0:T(8,128)S(1)} collective-permute-done((f32[72,128]{1,0:T(8,128)S(1)}, f32[72,128]{1,0:T(8,128)S(1)}, u32[]{:S(2)}, u32[]{:S(2)}) %collective-permute-start.9) | collective-permute-done | bytes 36896 | tf_op jit(solution)/shard_map/ppermute | solution.py:846
  61.2 0.0 collective-permute-start.15
  61.2 0.5 collective-permute-start.17
  61.7 0.0 collective-permute-start.16
  61.7 2.1 %collective-permute-start.14 = (f32[72,128]{1,0:T(8,128)S(1)}, f32[72,128]{1,0:T(8,128)S(1)}, u32[]{:S(2)}, u32[]{:S(2)}) collective-permute-start(f32[72,128]{1,0:T(8,128)S(1)} %add_add_fusion.1), channel_id=1, source_target_pairs={{0,12},{1,13},{2,14},{3,15},{4,8},{5,9},{6,10},{7,11},{8,4},{9,5},... | collective-permute-start | bytes 110600 | tf_op jit(solution)/shard_map/ppermute | solution.py:846
  63.8 0.1 collective-permute-start.13
  63.9 0.0 collective-permute-done.15
  63.9 2.3 %collective-permute-start.12 = (f32[72,128]{1,0:T(8,128)S(1)}, f32[72,128]{1,0:T(8,128)S(1)}, u32[]{:S(2)}, u32[]{:S(2)}) collective-permute-start(f32[72,128]{1,0:T(8,128)S(1)} %add_add_fusion.1), channel_id=1, source_target_pairs={{0,4},{1,5},{2,6},{3,7},{4,0},{5,1},{6,2},{7,3},{8,12},{9,13},{10,... | collective-permute-start | bytes 110600 | tf_op jit(solution)/shard_map/ppermute | solution.py:846
  66.2 0.8 add_convert_fusion
  67.0 0.7 collective-permute-done.14
  67.7 0.0 collective-permute-done.16
  67.7 0.0 collective-permute-done.17
  67.7 4.0 %all-to-all-start.2 = ((bf16[16,80,128]{2,1,0:T(8,128)(2,1)}), bf16[16,80,128]{2,1,0:T(8,128)(2,1)S(1)}, u32[]{:S(2)}, u32[]{:S(2)}) async-start(bf16[16,80,128]{2,1,0:T(8,128)(2,1)} %add_convert_fusion), calls=%async_computation.2 | async-start | bytes 655360 | tf_op jit(solution)/shard_map/all_to_all | solution.py:1200
  71.7 0.0 collective-permute-done.13
  71.7 0.0 collective-permute-done.12
  71.7 8.4 %sample_backward.1 = bf16[16,32,128]{2,1,0:T(8,128)(2,1)} custom-call(s32[10]{0:T(128)S(1)} %pad_add_fusion.1.scal_ref, f32[72,128]{1,0:T(8,128)S(1)} %add_add_fusion.msg_ref, f32[1,3,4096]{2,1,0:T(4,128)S(1)} %copy.20.func_ref, bf16[128,4096]{1,0:T(8,128)(2,1)} %get-tuple-element.152.keys_hbm, bf16[128,4096]{1,0:T(8,128)(2,1)} %get-tuple-element.153.vals_hbm, ...), custom_call_target="tpu_custom_call" | custom-call | flops 20132659200 | bytes 6291456 | tf_op jit(solution)/shard_map/sample_backward/pallas_call | solution.py:1201
  80.1 2.1 %all-to-all-done.2 = bf16[16,80,128]{2,1,0:T(8,128)(2,1)S(1)} async-done(((bf16[16,80,128]{2,1,0:T(8,128)(2,1)}), bf16[16,80,128]{2,1,0:T(8,128)(2,1)S(1)}, u32[]{:S(2)}, u32[]{:S(2)}) %all-to-all-start.2) | async-done | bytes 327712 | tf_op jit(solution)/shard_map/all_to_all | solution.py:1200
  82.2 5.0 %all-to-all-start.3 = ((bf16[16,32,128]{2,1,0:T(8,128)(2,1)}), bf16[16,32,128]{2,1,0:T(8,128)(2,1)S(1)}, u32[]{:S(2)}, u32[]{:S(2)}) async-start(bf16[16,32,128]{2,1,0:T(8,128)(2,1)} %sample_backward.1), calls=%async_computation.3 | async-start | bytes 262144 | tf_op jit(solution)/shard_map/all_to_all | solution.py:1283
  87.2 0.1 convert_reduce_fusion
  87.2 0.1 collective-permute-start.18
  87.3 1.1 %maximum_select_fusion = f32[2048,128]{1,0:T(8,128)} fusion(f32[1024,128]{1,0:T(8,128)S(1)} %collective-permute-done.17, f32[1024,128]{1,0:T(8,128)S(1)} %get-tuple-element.164, pred[]{:T(512)S(6)} %eq.2), kind=kLoop, calls=%fused_computation | loop fusion | flops 786432 | bytes 2097153 | tf_op jit(solution)/shard_map/jit(_where)/select_n | solution.py:1271
  88.4 0.9 maximum_select_fusion.1
  89.3 0.7 multiply_subtract_fusion
  90.1 4.9 %all-to-all-done.3 = bf16[16,32,128]{2,1,0:T(8,128)(2,1)S(1)} async-done(((bf16[16,32,128]{2,1,0:T(8,128)(2,1)}), bf16[16,32,128]{2,1,0:T(8,128)(2,1)S(1)}, u32[]{:S(2)}, u32[]{:S(2)}) %all-to-all-start.3) | async-done | bytes 131104 | tf_op jit(solution)/shard_map/all_to_all | solution.py:1283
  95.0 0.7 multiply_subtract_fusion.1
  (33 shorter events, 0.2 us)
Async XLA Ops:
  2.1 8.5 %copy-start.3 = (f32[18568]{0:T(1024)S(1)}, f32[18568]{0:T(1024)}, u32[]{:S(2)}) copy-start(f32[18568]{0:T(1024)} %param.18) | copy-start | bytes 222820
  2.1 16.2 %all-to-all-start = ((bf16[16,32,128]{2,1,0:T(8,128)(2,1)}), bf16[16,32,128]{2,1,0:T(8,128)(2,1)S(1)}, u32[]{:S(2)}, u32[]{:S(2)}) async-start(bf16[16,32,128]{2,1,0:T(8,128)(2,1)} %broadcast_in_dim.6), calls=%async_computation | async-start | bytes 262144 | tf_op jit(solution)/shard_map/all_to_all | solution.py:908
  19.1 3.7 %copy-start.7 = (f32[1,3,4096]{2,0,1:T(1,128)S(1)}, f32[1,3,4096]{2,0,1:T(1,128)}, u32[]{:S(2)}) copy-start(f32[1,3,4096]{2,0,1:T(1,128)} %param.13) | copy-start | bytes 147460
  19.1 13.8 %all-to-all-start.1 = ((bf16[16,80,128]{2,1,0:T(8,128)(2,1)}), bf16[16,80,128]{2,1,0:T(8,128)(2,1)S(1)}, u32[]{:S(2)}, u32[]{:S(2)}) async-start(bf16[16,80,128]{2,1,0:T(8,128)(2,1)} %broadcast_in_dim.7), calls=%async_computation.1 | async-start | bytes 655360 | tf_op jit(solution)/shard_map/all_to_all | solution.py:911
  22.9 17.3 %copy-start.10 = (s32[1,4]{1,0:T(1,128)S(1)}, s32[1,4]{1,0:T(1,128)}, u32[]{:S(2)}) copy-start(s32[1,4]{1,0:T(1,128)} %count_hbm.1) | copy-start | bytes 52
  22.9 17.3 %copy-start.11 = (s32[4]{0:T(128)S(1)}, s32[4]{0:T(128)}, u32[]{:S(2)}) copy-start(s32[4]{0:T(128)} %param.14) | copy-start | bytes 52
  22.9 18.5 %copy-start = (f32[2048,128]{1,0:T(8,128)S(1)}, f32[2048,128]{1,0:T(8,128)}, u32[]{:S(2)}) copy-start(f32[2048,128]{1,0:T(8,128)} %cot_ref.1) | copy-start | bytes 3145732
  28.4 13.0 %copy-start.1 = (bf16[2048,128]{1,0:T(8,128)(2,1)S(1)}, bf16[2048,128]{1,0:T(8,128)(2,1)}, u32[]{:S(2)}) copy-start(bf16[2048,128]{1,0:T(8,128)(2,1)} %token_ref.1) | copy-start | bytes 1572868
  28.5 4.4 %collective-permute-start = (f32[72,128]{1,0:T(8,128)S(1)}, f32[72,128]{1,0:T(8,128)S(1)}, u32[]{:S(2)}, u32[]{:S(2)}) collective-permute-start(f32[72,128]{1,0:T(8,128)S(1)} %get-tuple-element.93), channel_id=1, source_target_pairs={{0,1},{1,0},{2,3},{3,2},{4,5},{5,4},{6,7},{7,6},{8,9},{9,8},{10,11... | collective-permute-start | bytes 110600 | tf_op jit(solution)/shard_map/ppermute | solution.py:846
  30.3 4.9 %collective-permute-start.2 = (f32[72,128]{1,0:T(8,128)S(1)}, f32[72,128]{1,0:T(8,128)S(1)}, u32[]{:S(2)}, u32[]{:S(2)}) collective-permute-start(f32[72,128]{1,0:T(8,128)S(1)} %get-tuple-element.93), channel_id=1, source_target_pairs={{0,3},{1,2},{2,1},{3,0},{4,7},{5,6},{6,5},{7,4},{8,11},{9,10},{10,... | collective-permute-start | bytes 110600 | tf_op jit(solution)/shard_map/ppermute | solution.py:846
  31.8 4.0 %collective-permute-start.1 = (f32[72,128]{1,0:T(8,128)S(1)}, f32[72,128]{1,0:T(8,128)S(1)}, u32[]{:S(2)}, u32[]{:S(2)}) collective-permute-start(f32[72,128]{1,0:T(8,128)S(1)} %get-tuple-element.93), channel_id=1, source_target_pairs={{0,2},{1,3},{2,0},{3,1},{4,6},{5,7},{6,4},{7,5},{8,10},{9,11},{10,... | collective-permute-start | bytes 110600 | tf_op jit(solution)/shard_map/ppermute | solution.py:846
  32.9 7.4 %collective-permute-start.6 = (bf16[16,80,128]{2,1,0:T(8,128)(2,1)S(1)}, bf16[16,80,128]{2,1,0:T(8,128)(2,1)S(1)}, u32[]{:S(2)}, u32[]{:S(2)}) collective-permute-start(bf16[16,80,128]{2,1,0:T(8,128)(2,1)S(1)} %all-to-all-done.1.own_ref), channel_id=1, source_target_pairs={{0,16},{16,0},{1,17},{17,1},{2,18},{18,2},{3,19},{19,3},{4,20},{20... | collective-permute-start | bytes 983048 | tf_op jit(solution)/shard_map/ppermute | solution.py:866
  35.8 6.9 %collective-permute-start.5 = (f32[72,128]{1,0:T(8,128)S(1)}, f32[72,128]{1,0:T(8,128)S(1)}, u32[]{:S(2)}, u32[]{:S(2)}) collective-permute-start(f32[72,128]{1,0:T(8,128)S(1)} %add_add_fusion.3), channel_id=1, source_target_pairs={{0,12},{1,13},{2,14},{3,15},{4,8},{5,9},{6,10},{7,11},{8,4},{9,5},... | collective-permute-start | bytes 110600 | tf_op jit(solution)/shard_map/ppermute | solution.py:846
  39.3 4.9 %collective-permute-start.4 = (f32[72,128]{1,0:T(8,128)S(1)}, f32[72,128]{1,0:T(8,128)S(1)}, u32[]{:S(2)}, u32[]{:S(2)}) collective-permute-start(f32[72,128]{1,0:T(8,128)S(1)} %add_add_fusion.3), channel_id=1, source_target_pairs={{0,8},{1,9},{2,10},{3,11},{4,12},{5,13},{6,14},{7,15},{8,0},{9,1},... | collective-permute-start | bytes 110600 | tf_op jit(solution)/shard_map/ppermute | solution.py:846
  39.3 4.9 %collective-permute-start.3 = (f32[72,128]{1,0:T(8,128)S(1)}, f32[72,128]{1,0:T(8,128)S(1)}, u32[]{:S(2)}, u32[]{:S(2)}) collective-permute-start(f32[72,128]{1,0:T(8,128)S(1)} %add_add_fusion.3), channel_id=1, source_target_pairs={{0,4},{1,5},{2,6},{3,7},{4,0},{5,1},{6,2},{7,3},{8,12},{9,13},{10,... | collective-permute-start | bytes 110600 | tf_op jit(solution)/shard_map/ppermute | solution.py:846
  44.2 1.3 %copy-start.2 = (s32[2048,4]{0,1:T(4,128)S(1)}, s32[2048,4]{0,1:T(4,128)}, u32[]{:S(2)}) copy-start(s32[2048,4]{0,1:T(4,128)} %param.16) | copy-start | bytes 98308
  44.2 1.3 %collective-permute-start.7 = (f32[72,128]{1,0:T(8,128)S(1)}, f32[72,128]{1,0:T(8,128)S(1)}, u32[]{:S(2)}, u32[]{:S(2)}) collective-permute-start(f32[72,128]{1,0:T(8,128)S(1)} %add_add_fusion.2.own_ref), channel_id=1, source_target_pairs={{0,16},{16,0},{1,17},{17,1},{2,18},{18,2},{3,19},{19,3},{4,20},{20... | collective-permute-start | bytes 110600 | tf_op jit(solution)/shard_map/ppermute | solution.py:866
  53.2 1.3 %collective-permute-start.8 = (f32[72,128]{1,0:T(8,128)S(1)}, f32[72,128]{1,0:T(8,128)S(1)}, u32[]{:S(2)}, u32[]{:S(2)}) collective-permute-start(f32[72,128]{1,0:T(8,128)S(1)} %get-tuple-element.130), channel_id=1, source_target_pairs={{0,16},{16,0},{1,17},{17,1},{2,18},{18,2},{3,19},{19,3},{4,20},{20... | collective-permute-start | bytes 110600 | tf_op jit(solution)/shard_map/ppermute | solution.py:866
  54.5 4.9 %collective-permute-start.11 = (f32[72,128]{1,0:T(8,128)S(1)}, f32[72,128]{1,0:T(8,128)S(1)}, u32[]{:S(2)}, u32[]{:S(2)}) collective-permute-start(f32[72,128]{1,0:T(8,128)S(1)} %add.86), channel_id=1, source_target_pairs={{0,3},{1,2},{2,1},{3,0},{4,7},{5,6},{6,5},{7,4},{8,11},{9,10},{10,... | collective-permute-start | bytes 110600 | tf_op jit(solution)/shard_map/ppermute | solution.py:846
  56.1 4.0 %collective-permute-start.10 = (f32[72,128]{1,0:T(8,128)S(1)}, f32[72,128]{1,0:T(8,128)S(1)}, u32[]{:S(2)}, u32[]{:S(2)}) collective-permute-start(f32[72,128]{1,0:T(8,128)S(1)} %add.86), channel_id=1, source_target_pairs={{0,2},{1,3},{2,0},{3,1},{4,6},{5,7},{6,4},{7,5},{8,10},{9,11},{10,... | collective-permute-start | bytes 110600 | tf_op jit(solution)/shard_map/ppermute | solution.py:846
  57.3 4.0 %collective-permute-start.9 = (f32[72,128]{1,0:T(8,128)S(1)}, f32[72,128]{1,0:T(8,128)S(1)}, u32[]{:S(2)}, u32[]{:S(2)}) collective-permute-start(f32[72,128]{1,0:T(8,128)S(1)} %add.86), channel_id=1, source_target_pairs={{0,1},{1,0},{2,3},{3,2},{4,5},{5,4},{6,7},{7,6},{8,9},{9,8},{10,11... | collective-permute-start | bytes 110600 | tf_op jit(solution)/shard_map/ppermute | solution.py:846
  61.2 2.7 %collective-permute-start.15 = (bf16[16,80,128]{2,1,0:T(8,128)(2,1)S(1)}, bf16[16,80,128]{2,1,0:T(8,128)(2,1)S(1)}, u32[]{:S(2)}, u32[]{:S(2)}) collective-permute-start(bf16[16,80,128]{2,1,0:T(8,128)(2,1)S(1)} %get-tuple-element.148), channel_id=1, source_target_pairs={{0,16},{16,0},{1,17},{17,1},{2,18},{18,2},{3,19},{19,3},{4,20},{20... | collective-permute-start | bytes 983048 | tf_op jit(solution)/shard_map/ppermute | solution.py:866
  61.2 6.5 %collective-permute-start.17 = (f32[1024,128]{1,0:T(8,128)S(1)}, f32[1024,128]{1,0:T(8,128)S(1)}, u32[]{:S(2)}, u32[]{:S(2)}) collective-permute-start(f32[1024,128]{1,0:T(8,128)S(1)} %get-tuple-element.164), channel_id=1, source_target_pairs={{0,16},{16,0},{1,17},{17,1},{2,18},{18,2},{3,19},{19,3},{4,20},{20... | collective-permute-start | bytes 1572872 | tf_op jit(solution)/shard_map/ppermute | solution.py:866
  61.7 5.9 %collective-permute-start.16 = (bf16[1024,128]{1,0:T(8,128)(2,1)S(1)}, bf16[1024,128]{1,0:T(8,128)(2,1)S(1)}, u32[]{:S(2)}, u32[]{:S(2)}) collective-permute-start(bf16[1024,128]{1,0:T(8,128)(2,1)S(1)} %get-tuple-element.162), channel_id=1, source_target_pairs={{0,16},{16,0},{1,17},{17,1},{2,18},{18,2},{3,19},{19,3},{4,20},{20... | collective-permute-start | bytes 786440 | tf_op jit(solution)/shard_map/ppermute | solution.py:866
  61.7 5.9 %collective-permute-start.14 = (f32[72,128]{1,0:T(8,128)S(1)}, f32[72,128]{1,0:T(8,128)S(1)}, u32[]{:S(2)}, u32[]{:S(2)}) collective-permute-start(f32[72,128]{1,0:T(8,128)S(1)} %add_add_fusion.1), channel_id=1, source_target_pairs={{0,12},{1,13},{2,14},{3,15},{4,8},{5,9},{6,10},{7,11},{8,4},{9,5},... | collective-permute-start | bytes 110600 | tf_op jit(solution)/shard_map/ppermute | solution.py:846
  63.8 7.8 %collective-permute-start.13 = (f32[72,128]{1,0:T(8,128)S(1)}, f32[72,128]{1,0:T(8,128)S(1)}, u32[]{:S(2)}, u32[]{:S(2)}) collective-permute-start(f32[72,128]{1,0:T(8,128)S(1)} %add_add_fusion.1), channel_id=1, source_target_pairs={{0,8},{1,9},{2,10},{3,11},{4,12},{5,13},{6,14},{7,15},{8,0},{9,1},... | collective-permute-start | bytes 110600 | tf_op jit(solution)/shard_map/ppermute | solution.py:846
  63.9 7.8 %collective-permute-start.12 = (f32[72,128]{1,0:T(8,128)S(1)}, f32[72,128]{1,0:T(8,128)S(1)}, u32[]{:S(2)}, u32[]{:S(2)}) collective-permute-start(f32[72,128]{1,0:T(8,128)S(1)} %add_add_fusion.1), channel_id=1, source_target_pairs={{0,4},{1,5},{2,6},{3,7},{4,0},{5,1},{6,2},{7,3},{8,12},{9,13},{10,... | collective-permute-start | bytes 110600 | tf_op jit(solution)/shard_map/ppermute | solution.py:846
  67.7 14.5 %all-to-all-start.2 = ((bf16[16,80,128]{2,1,0:T(8,128)(2,1)}), bf16[16,80,128]{2,1,0:T(8,128)(2,1)S(1)}, u32[]{:S(2)}, u32[]{:S(2)}) async-start(bf16[16,80,128]{2,1,0:T(8,128)(2,1)} %add_convert_fusion), calls=%async_computation.2 | async-start | bytes 655360 | tf_op jit(solution)/shard_map/all_to_all | solution.py:1200
  82.2 12.8 %all-to-all-start.3 = ((bf16[16,32,128]{2,1,0:T(8,128)(2,1)}), bf16[16,32,128]{2,1,0:T(8,128)(2,1)S(1)}, u32[]{:S(2)}, u32[]{:S(2)}) async-start(bf16[16,32,128]{2,1,0:T(8,128)(2,1)} %sample_backward.1), calls=%async_computation.3 | async-start | bytes 262144 | tf_op jit(solution)/shard_map/all_to_all | solution.py:1283
  87.2 2.1 %collective-permute-start.18 = (f32[10240]{0:T(1024)S(1)}, f32[10240]{0:T(1024)S(1)}, u32[]{:S(2)}, u32[]{:S(2)}) collective-permute-start(f32[10240]{0:T(1024)S(1)} %bitcast.10), channel_id=1, source_target_pairs={{0,16},{16,0},{1,17},{17,1},{2,18},{18,2},{3,19},{19,3},{4,20},{20... | collective-permute-start | bytes 122888 | tf_op jit(solution)/shard_map/ppermute | solution.py:866
  88.4 0.9 copy-start.4
  88.4 0.9 copy-start.5
  90.1 4.9 %copy-start.6 = (f32[1,3112]{1,0:T(1,128)S(1)}, f32[1,3112]{1,0:T(1,128)}, u32[]{:S(2)}) copy-start(f32[1,3112]{1,0:T(1,128)} %param.21) | copy-start | bytes 37348
  90.1 4.9 %copy-start.8 = (f32[1,3112]{1,0:T(1,128)S(1)}, f32[1,3112]{1,0:T(1,128)}, u32[]{:S(2)}) copy-start(f32[1,3112]{1,0:T(1,128)} %param.22) | copy-start | bytes 37348
  90.1 4.9 %copy-start.9 = (f32[1,3112]{1,0:T(1,128)S(1)}, f32[1,3112]{1,0:T(1,128)}, u32[]{:S(2)}) copy-start(f32[1,3112]{1,0:T(1,128)} %param.23) | copy-start | bytes 37348

commit v6 on v5

--- a/solution.py
+++ b/solution.py
@@ -838,10 +838,12 @@
 
 
 def sum_over_points(values, count, besides, early):
+    groups = []
     bit = 1
-    number = 0
     while bit < count:
-        masks = [bit] if 2 * bit >= count else [bit, 2 * bit, 3 * bit]
+        groups.append([bit] if 2 * bit >= count else [bit, 2 * bit, 3 * bit])
+        bit *= 4
+    for number, masks in enumerate(reversed(groups)):
         pieces = [
             lax.ppermute(values, "pts", [(source, source ^ mask) for source in range(count)])
             for mask in masks
@@ -853,8 +855,6 @@
                 (pieces[some], besides[number](before))
             )
         values = functools.reduce(jnp.add, pieces, values)
-        bit *= 4
-        number += 1
     return values, besides
 
 

time: 96.8 us -> 97.3 us (level)
  waiting for transfers between devices: 24.9 us -> 27 us
  starting transfers between devices: 38 us -> 36.9 us
    ppermute x12, waiting for transfers between devices: 7.92 us -> 9.62 us  [sum_over_points(): lax.ppermute(values, 'pts', [(source, source ^ mask) for source in range(...]
where the time goes in v6:
time: 97.3 us; the launch traced here: 96.8 us
  starting transfers between devices  36.9 us (38%)
  waiting for transfers between devices  27 us (28%)
  Pallas kernels  25.1 us (26%)
  other arithmetic  5.28 us (5%)
  local copies, waits for them, and re-layouts  1.61 us (2%)
    ppermute x12, starting transfers between devices, sum_over_points(): lax.ppermute(values, 'pts', [(source, source ^ mask) for source in range(...  15.8 us
    ppermute x12, waiting for transfers between devices, sum_over_points(): lax.ppermute(values, 'pts', [(source, source ^ mask) for source in range(...  9.62 us
    all_to_all x1, starting transfers between devices, body(): lax.all_to_all(copies(branch_pad.reshape(height, LANES), count), 'pts', 0...  8.44 us
    pallas_call x1, Pallas kernels, body(): pl.pallas_call(functools.partial(sample_backward_kernel, (back_tile, item...  8.41 us
    all_to_all x1, waiting for transfers between devices, body(): lax.all_to_all(copies(branch_pad.reshape(height, LANES), count), 'pts', 0...  7.73 us
    pallas_call x1, Pallas kernels, body(): pl.pallas_call(functools.partial(token_kernel, (token_tile, items, chip_r...  7.7 us
    pallas_call x1, Pallas kernels, body(): pl.pallas_call(functools.partial(sample_forward_kernel, (tile, items, cou...  5.51 us
    all_to_all x1, waiting for transfers between devices, body(): branch_recv = lax.all_to_all(grads_send, 'pts', 0, 0)  4.88 us
  transfers between devices with their start and end apart: 23, of which 13 were waited for; matrix products, arithmetic and copies ran while one was open for 4% of the time, Pallas kernels for 18%

profile of v6, /device:TPU:0, one launch (start us, length us, event | category | flops | bytes accessed | tf_op | source)
XLA Modules:
  0.0 96.8 jit_solution(10980127923069110164)
XLA Ops:
  0.6 0.7 convert_element_type.22
  1.4 0.1 pad_reduce_fusion
  1.4 0.7 broadcast_in_dim.6
  2.1 8.4 %all-to-all-start = ((bf16[16,32,128]{2,1,0:T(8,128)(2,1)}), bf16[16,32,128]{2,1,0:T(8,128)(2,1)S(1)}, u32[]{:S(2)}, u32[]{:S(2)}) async-start(bf16[16,32,128]{2,1,0:T(8,128)(2,1)} %broadcast_in_dim.6), calls=%async_computation | async-start | bytes 262144 | tf_op jit(solution)/shard_map/all_to_all | solution.py:908
  10.6 7.7 %all-to-all-done.recv_ref = bf16[16,32,128]{2,1,0:T(8,128)(2,1)S(1)} async-done(((bf16[16,32,128]{2,1,0:T(8,128)(2,1)}), bf16[16,32,128]{2,1,0:T(8,128)(2,1)S(1)}, u32[]{:S(2)}, u32[]{:S(2)}) %all-to-all-start) | async-done | bytes 131104 | tf_op jit(solution)/shard_map/all_to_all | solution.py:908
  18.3 0.8 broadcast_in_dim.7
  19.1 3.7 %all-to-all-start.1 = ((bf16[16,80,128]{2,1,0:T(8,128)(2,1)}), bf16[16,80,128]{2,1,0:T(8,128)(2,1)S(1)}, u32[]{:S(2)}, u32[]{:S(2)}) async-start(bf16[16,80,128]{2,1,0:T(8,128)(2,1)} %broadcast_in_dim.7), calls=%async_computation.1 | async-start | bytes 655360 | tf_op jit(solution)/shard_map/all_to_all | solution.py:911
  22.8 0.1 pad_add_fusion.scal_ref
  22.9 5.5 %sample_forward.1 = (f32[72,128]{1,0:T(8,128)S(1)}, bf16[128,4096]{1,0:T(8,128)(2,1)}, bf16[128,4096]{1,0:T(8,128)(2,1)}, bf16[128,128]{1,0:T(8,128)(2,1)S(1)}, ...) custom-call(s32[2]{0:T(128)S(1)} %pad_add_fusion.scal_ref, ...), custom_call_target="tpu_custom_call" | custom-call | flops 671088640 | bytes 6291456 | tf_op jit(solution)/shard_map/sample_forward/pallas_call | solution.py:926
  28.4 0.0 copy-start.1
  28.5 1.9 %collective-permute-start = (f32[72,128]{1,0:T(8,128)S(1)}, f32[72,128]{1,0:T(8,128)S(1)}, u32[]{:S(2)}, u32[]{:S(2)}) collective-permute-start(f32[72,128]{1,0:T(8,128)S(1)} %get-tuple-element.93), channel_id=1, source_target_pairs={{0,4},{1,5},{2,6},{3,7},{4,0},{5,1},{6,2},{7,3},{8,12},{9,13},{10,... | collective-permute-start | bytes 110600 | tf_op jit(solution)/shard_map/ppermute | solution.py:848
  30.3 2.4 %collective-permute-start.2 = (f32[72,128]{1,0:T(8,128)S(1)}, f32[72,128]{1,0:T(8,128)S(1)}, u32[]{:S(2)}, u32[]{:S(2)}) collective-permute-start(f32[72,128]{1,0:T(8,128)S(1)} %get-tuple-element.93), channel_id=1, source_target_pairs={{0,12},{1,13},{2,14},{3,15},{4,8},{5,9},{6,10},{7,11},{8,4},{9,5},... | collective-permute-start | bytes 110600 | tf_op jit(solution)/shard_map/ppermute | solution.py:848
  32.7 0.0 collective-permute-start.1
  32.8 0.0 collective-permute-done
  32.8 0.1 all-to-all-done.1.own_ref
  32.9 0.0 collective-permute-start.6
  32.9 3.2 %collective-permute-done.2 = f32[72,128]{1,0:T(8,128)S(1)} collective-permute-done((f32[72,128]{1,0:T(8,128)S(1)}, f32[72,128]{1,0:T(8,128)S(1)}, u32[]{:S(2)}, u32[]{:S(2)}) %collective-permute-start.2) | collective-permute-done | bytes 36896 | tf_op jit(solution)/shard_map/ppermute | solution.py:848
  36.1 1.9 %collective-permute-done.1 = f32[72,128]{1,0:T(8,128)S(1)} collective-permute-done((f32[72,128]{1,0:T(8,128)S(1)}, f32[72,128]{1,0:T(8,128)S(1)}, u32[]{:S(2)}, u32[]{:S(2)}) %collective-permute-start.1) | collective-permute-done | bytes 36896 | tf_op jit(solution)/shard_map/ppermute | solution.py:848
  38.0 2.5 %collective-permute-start.5 = (f32[72,128]{1,0:T(8,128)S(1)}, f32[72,128]{1,0:T(8,128)S(1)}, u32[]{:S(2)}, u32[]{:S(2)}) collective-permute-start(f32[72,128]{1,0:T(8,128)S(1)} %add_add_fusion.3), channel_id=1, source_target_pairs={{0,3},{1,2},{2,1},{3,0},{4,7},{5,6},{6,5},{7,4},{8,11},{9,10},{10,... | collective-permute-start | bytes 110600 | tf_op jit(solution)/shard_map/ppermute | solution.py:848
  40.5 0.2 collective-permute-start.4
  40.6 0.9 collective-permute-start.3
  41.6 0.1 pad_add_fusion.1.scal_ref
  41.6 0.0 collective-permute-done.6.other_ref
  41.6 1.1 %weights.1 = (bf16[128,128]{1,0:T(8,128)(2,1)S(1)}, bf16[128,128]{1,0:T(8,128)(2,1)S(1)}, bf16[128,128]{1,0:T(8,128)(2,1)S(1)}, bf16[128,128]{1,0:T(8,128)(2,1)S...) custom-call(s32[10]{0:T(128)S(1)} %pad_add_fusion.1.scal_ref, ...), custom_call_target="tpu_custom_call" | custom-call | bytes 8388608 | tf_op jit(solution)/shard_map/weights/pallas_call | solution.py:989
  42.8 1.2 %queries.1 = (bf16[128,1024]{1,0:T(8,128)(2,1)S(1)}, f32[128,1024]{1,0:T(8,128)S(1)}, f32[128,1024]{1,0:T(8,128)S(1)}, f32[8,1024]{1,0:T(8,128)S(1)}, bf16[128,1...) custom-call(s32[10]{0:T(128)S(1)} %pad_add_fusion.1.scal_ref, bf16[2048,128]{1,0:T(8,128)(2,1)S(1)} %copy-done.1, ...), custom_call_target="tpu_custom_call" | custom-call | flops 33554432 | bytes 3145728 | tf_op jit(solution)/shard_map/queries/pallas_call | solution.py:1035
  44.0 0.0 collective-permute-done.5
  44.0 0.4 collective-permute-done.4
  44.4 0.2 collective-permute-done.3
  44.6 0.1 collective-permute-start.7
  44.7 1.2 %collective-permute-done.7.other_ref = f32[72,128]{1,0:T(8,128)S(1)} collective-permute-done((f32[72,128]{1,0:T(8,128)S(1)}, f32[72,128]{1,0:T(8,128)S(1)}, u32[]{:S(2)}, u32[]{:S(2)}) %collective-permute-start.7) | collective-permute-done | bytes 36896 | tf_op jit(solution)/shard_map/ppermute | solution.py:866
  45.9 7.7 %tokens.1 = (bf16[1024,128]{1,0:T(8,128)(2,1)S(1)}, f32[1024,128]{1,0:T(8,128)S(1)}, f32[72,128]{1,0:T(8,128)S(1)}, f32[72,128]{1,0:T(8,128)S(1)}, f32[128,128]{...) custom-call(s32[10]{0:T(128)S(1)} %pad_add_fusion.1.scal_ref, ...), custom_call_target="tpu_custom_call" | custom-call | flops 1610612736 | bytes 3145728 | tf_op jit(solution)/shard_map/tokens/pallas_call | solution.py:1086
  53.6 0.2 collective-permute-start.8
  53.8 1.0 %collective-permute-done.8 = f32[72,128]{1,0:T(8,128)S(1)} collective-permute-done((f32[72,128]{1,0:T(8,128)S(1)}, f32[72,128]{1,0:T(8,128)S(1)}, u32[]{:S(2)}, u32[]{:S(2)}) %collective-permute-start.8) | collective-permute-done | bytes 36896 | tf_op jit(solution)/shard_map/ppermute | solution.py:866
  54.9 3.7 %collective-permute-start.11 = (f32[72,128]{1,0:T(8,128)S(1)}, f32[72,128]{1,0:T(8,128)S(1)}, u32[]{:S(2)}, u32[]{:S(2)}) collective-permute-start(f32[72,128]{1,0:T(8,128)S(1)} %add.86), channel_id=1, source_target_pairs={{0,12},{1,13},{2,14},{3,15},{4,8},{5,9},{6,10},{7,11},{8,4},{9,5},... | collective-permute-start | bytes 110600 | tf_op jit(solution)/shard_map/ppermute | solution.py:848
  58.6 0.0 collective-permute-start.10
  58.6 0.6 collective-permute-start.9
  59.2 1.1 %pack.1 = (f32[16,80,128]{2,1,0:T(8,128)S(1)}, bf16[16,80,128]{2,1,0:T(8,128)(2,1)S(1)}) custom-call(s32[10]{0:T(128)S(1)} %pad_add_fusion.1.scal_ref, f32[128,128]{1,0:T(8,128)S(1)} %get-tuple-element.137.g_query_ref, f32[144,128]{1,0:T(8,128)S(1)} %get-tuple-element.138.g_out_ref, f32[4,144,256]{2,1,0:T(8,128)S(1)} %get-tuple-element.139.g_up_ref, ...), custom_call_target="tpu_custom_call" | custom-call | flops 2147483648 | bytes 4194304 | tf_op jit(solution)/shard_map/pack/pallas_call | solution.py:1171
  60.4 0.5 collective-permute-done.11
  60.9 2.5 %collective-permute-done.10 = f32[72,128]{1,0:T(8,128)S(1)} collective-permute-done((f32[72,128]{1,0:T(8,128)S(1)}, f32[72,128]{1,0:T(8,128)S(1)}, u32[]{:S(2)}, u32[]{:S(2)}) %collective-permute-start.10) | collective-permute-done | bytes 36896 | tf_op jit(solution)/shard_map/ppermute | solution.py:848
  63.5 0.0 collective-permute-done.9
  63.5 0.0 collective-permute-start.15
  63.5 0.5 collective-permute-start.17
  64.0 0.0 collective-permute-start.16
  64.0 0.4 collective-permute-start.14
  64.4 1.2 %collective-permute-start.13 = (f32[72,128]{1,0:T(8,128)S(1)}, f32[72,128]{1,0:T(8,128)S(1)}, u32[]{:S(2)}, u32[]{:S(2)}) collective-permute-start(f32[72,128]{1,0:T(8,128)S(1)} %add_add_fusion.1), channel_id=1, source_target_pairs={{0,2},{1,3},{2,0},{3,1},{4,6},{5,7},{6,4},{7,5},{8,10},{9,11},{10,... | collective-permute-start | bytes 110600 | tf_op jit(solution)/shard_map/ppermute | solution.py:848
  65.6 0.0 collective-permute-done.15
  65.6 2.0 %collective-permute-start.12 = (f32[72,128]{1,0:T(8,128)S(1)}, f32[72,128]{1,0:T(8,128)S(1)}, u32[]{:S(2)}, u32[]{:S(2)}) collective-permute-start(f32[72,128]{1,0:T(8,128)S(1)} %add_add_fusion.1), channel_id=1, source_target_pairs={{0,1},{1,0},{2,3},{3,2},{4,5},{5,4},{6,7},{7,6},{8,9},{9,8},{10,11... | collective-permute-start | bytes 110600 | tf_op jit(solution)/shard_map/ppermute | solution.py:848
  67.5 0.8 add_convert_fusion
  68.4 0.9 collective-permute-done.14
  69.2 0.0 collective-permute-done.16
  69.2 0.0 collective-permute-done.17
  69.2 3.5 %all-to-all-start.2 = ((bf16[16,80,128]{2,1,0:T(8,128)(2,1)}), bf16[16,80,128]{2,1,0:T(8,128)(2,1)S(1)}, u32[]{:S(2)}, u32[]{:S(2)}) async-start(bf16[16,80,128]{2,1,0:T(8,128)(2,1)} %add_convert_fusion), calls=%async_computation.2 | async-start | bytes 655360 | tf_op jit(solution)/shard_map/all_to_all | solution.py:1200
  72.8 0.0 collective-permute-done.13
  72.8 0.0 collective-permute-done.12
  72.8 8.4 %sample_backward.1 = bf16[16,32,128]{2,1,0:T(8,128)(2,1)} custom-call(s32[10]{0:T(128)S(1)} %pad_add_fusion.1.scal_ref, f32[72,128]{1,0:T(8,128)S(1)} %add_add_fusion.msg_ref, f32[1,3,4096]{2,1,0:T(4,128)S(1)} %copy.20.func_ref, bf16[128,4096]{1,0:T(8,128)(2,1)} %get-tuple-element.152.keys_hbm, bf16[128,4096]{1,0:T(8,128)(2,1)} %get-tuple-element.153.vals_hbm, ...), custom_call_target="tpu_custom_call" | custom-call | flops 20132659200 | bytes 6291456 | tf_op jit(solution)/shard_map/sample_backward/pallas_call | solution.py:1201
  81.3 2.4 %all-to-all-done.2 = bf16[16,80,128]{2,1,0:T(8,128)(2,1)S(1)} async-done(((bf16[16,80,128]{2,1,0:T(8,128)(2,1)}), bf16[16,80,128]{2,1,0:T(8,128)(2,1)S(1)}, u32[]{:S(2)}, u32[]{:S(2)}) %all-to-all-start.2) | async-done | bytes 327712 | tf_op jit(solution)/shard_map/all_to_all | solution.py:1200
  83.6 4.6 %all-to-all-start.3 = ((bf16[16,32,128]{2,1,0:T(8,128)(2,1)}), bf16[16,32,128]{2,1,0:T(8,128)(2,1)S(1)}, u32[]{:S(2)}, u32[]{:S(2)}) async-start(bf16[16,32,128]{2,1,0:T(8,128)(2,1)} %sample_backward.1), calls=%async_computation.3 | async-start | bytes 262144 | tf_op jit(solution)/shard_map/all_to_all | solution.py:1283
  88.2 0.1 convert_reduce_fusion
  88.3 0.1 collective-permute-start.18
  88.4 1.1 %maximum_select_fusion = f32[2048,128]{1,0:T(8,128)} fusion(f32[1024,128]{1,0:T(8,128)S(1)} %collective-permute-done.17, f32[1024,128]{1,0:T(8,128)S(1)} %get-tuple-element.164, pred[]{:T(512)S(6)} %eq.2), kind=kLoop, calls=%fused_computation | loop fusion | flops 786432 | bytes 2097153 | tf_op jit(solution)/shard_map/jit(_where)/select_n | solution.py:1271
  89.5 0.9 maximum_select_fusion.1
  90.4 0.7 multiply_subtract_fusion
  91.2 4.9 %all-to-all-done.3 = bf16[16,32,128]{2,1,0:T(8,128)(2,1)S(1)} async-done(((bf16[16,32,128]{2,1,0:T(8,128)(2,1)}), bf16[16,32,128]{2,1,0:T(8,128)(2,1)S(1)}, u32[]{:S(2)}, u32[]{:S(2)}) %all-to-all-start.3) | async-done | bytes 131104 | tf_op jit(solution)/shard_map/all_to_all | solution.py:1283
  96.1 0.7 multiply_subtract_fusion.1
  (33 shorter events, 0.2 us)
Async XLA Ops:
  2.1 8.5 %copy-start.3 = (f32[18568]{0:T(1024)S(1)}, f32[18568]{0:T(1024)}, u32[]{:S(2)}) copy-start(f32[18568]{0:T(1024)} %param.18) | copy-start | bytes 222820
  2.1 16.2 %all-to-all-start = ((bf16[16,32,128]{2,1,0:T(8,128)(2,1)}), bf16[16,32,128]{2,1,0:T(8,128)(2,1)S(1)}, u32[]{:S(2)}, u32[]{:S(2)}) async-start(bf16[16,32,128]{2,1,0:T(8,128)(2,1)} %broadcast_in_dim.6), calls=%async_computation | async-start | bytes 262144 | tf_op jit(solution)/shard_map/all_to_all | solution.py:908
  19.1 3.7 %copy-start.7 = (f32[1,3,4096]{2,0,1:T(1,128)S(1)}, f32[1,3,4096]{2,0,1:T(1,128)}, u32[]{:S(2)}) copy-start(f32[1,3,4096]{2,0,1:T(1,128)} %param.13) | copy-start | bytes 147460
  19.1 13.8 %all-to-all-start.1 = ((bf16[16,80,128]{2,1,0:T(8,128)(2,1)}), bf16[16,80,128]{2,1,0:T(8,128)(2,1)S(1)}, u32[]{:S(2)}, u32[]{:S(2)}) async-start(bf16[16,80,128]{2,1,0:T(8,128)(2,1)} %broadcast_in_dim.7), calls=%async_computation.1 | async-start | bytes 655360 | tf_op jit(solution)/shard_map/all_to_all | solution.py:911
  22.9 18.6 %copy-start.10 = (s32[1,4]{1,0:T(1,128)S(1)}, s32[1,4]{1,0:T(1,128)}, u32[]{:S(2)}) copy-start(s32[1,4]{1,0:T(1,128)} %count_hbm.1) | copy-start | bytes 52
  22.9 18.6 %copy-start.11 = (s32[4]{0:T(128)S(1)}, s32[4]{0:T(128)}, u32[]{:S(2)}) copy-start(s32[4]{0:T(128)} %param.14) | copy-start | bytes 52
  22.9 19.9 %copy-start = (f32[2048,128]{1,0:T(8,128)S(1)}, f32[2048,128]{1,0:T(8,128)}, u32[]{:S(2)}) copy-start(f32[2048,128]{1,0:T(8,128)} %cot_ref.1) | copy-start | bytes 3145732
  28.4 14.4 %copy-start.1 = (bf16[2048,128]{1,0:T(8,128)(2,1)S(1)}, bf16[2048,128]{1,0:T(8,128)(2,1)}, u32[]{:S(2)}) copy-start(bf16[2048,128]{1,0:T(8,128)(2,1)} %token_ref.1) | copy-start | bytes 1572868
  28.5 4.3 %collective-permute-start = (f32[72,128]{1,0:T(8,128)S(1)}, f32[72,128]{1,0:T(8,128)S(1)}, u32[]{:S(2)}, u32[]{:S(2)}) collective-permute-start(f32[72,128]{1,0:T(8,128)S(1)} %get-tuple-element.93), channel_id=1, source_target_pairs={{0,4},{1,5},{2,6},{3,7},{4,0},{5,1},{6,2},{7,3},{8,12},{9,13},{10,... | collective-permute-start | bytes 110600 | tf_op jit(solution)/shard_map/ppermute | solution.py:848
  30.3 5.8 %collective-permute-start.2 = (f32[72,128]{1,0:T(8,128)S(1)}, f32[72,128]{1,0:T(8,128)S(1)}, u32[]{:S(2)}, u32[]{:S(2)}) collective-permute-start(f32[72,128]{1,0:T(8,128)S(1)} %get-tuple-element.93), channel_id=1, source_target_pairs={{0,12},{1,13},{2,14},{3,15},{4,8},{5,9},{6,10},{7,11},{8,4},{9,5},... | collective-permute-start | bytes 110600 | tf_op jit(solution)/shard_map/ppermute | solution.py:848
  32.7 5.3 %collective-permute-start.1 = (f32[72,128]{1,0:T(8,128)S(1)}, f32[72,128]{1,0:T(8,128)S(1)}, u32[]{:S(2)}, u32[]{:S(2)}) collective-permute-start(f32[72,128]{1,0:T(8,128)S(1)} %get-tuple-element.93), channel_id=1, source_target_pairs={{0,8},{1,9},{2,10},{3,11},{4,12},{5,13},{6,14},{7,15},{8,0},{9,1},... | collective-permute-start | bytes 110600 | tf_op jit(solution)/shard_map/ppermute | solution.py:848
  32.9 8.7 %collective-permute-start.6 = (bf16[16,80,128]{2,1,0:T(8,128)(2,1)S(1)}, bf16[16,80,128]{2,1,0:T(8,128)(2,1)S(1)}, u32[]{:S(2)}, u32[]{:S(2)}) collective-permute-start(bf16[16,80,128]{2,1,0:T(8,128)(2,1)S(1)} %all-to-all-done.1.own_ref), channel_id=1, source_target_pairs={{0,16},{16,0},{1,17},{17,1},{2,18},{18,2},{3,19},{19,3},{4,20},{20... | collective-permute-start | bytes 983048 | tf_op jit(solution)/shard_map/ppermute | solution.py:866
  38.0 6.0 %collective-permute-start.5 = (f32[72,128]{1,0:T(8,128)S(1)}, f32[72,128]{1,0:T(8,128)S(1)}, u32[]{:S(2)}, u32[]{:S(2)}) collective-permute-start(f32[72,128]{1,0:T(8,128)S(1)} %add_add_fusion.3), channel_id=1, source_target_pairs={{0,3},{1,2},{2,1},{3,0},{4,7},{5,6},{6,5},{7,4},{8,11},{9,10},{10,... | collective-permute-start | bytes 110600 | tf_op jit(solution)/shard_map/ppermute | solution.py:848
  40.5 4.0 %collective-permute-start.4 = (f32[72,128]{1,0:T(8,128)S(1)}, f32[72,128]{1,0:T(8,128)S(1)}, u32[]{:S(2)}, u32[]{:S(2)}) collective-permute-start(f32[72,128]{1,0:T(8,128)S(1)} %add_add_fusion.3), channel_id=1, source_target_pairs={{0,2},{1,3},{2,0},{3,1},{4,6},{5,7},{6,4},{7,5},{8,10},{9,11},{10,... | collective-permute-start | bytes 110600 | tf_op jit(solution)/shard_map/ppermute | solution.py:848
  40.6 4.0 %collective-permute-start.3 = (f32[72,128]{1,0:T(8,128)S(1)}, f32[72,128]{1,0:T(8,128)S(1)}, u32[]{:S(2)}, u32[]{:S(2)}) collective-permute-start(f32[72,128]{1,0:T(8,128)S(1)} %add_add_fusion.3), channel_id=1, source_target_pairs={{0,1},{1,0},{2,3},{3,2},{4,5},{5,4},{6,7},{7,6},{8,9},{9,8},{10,11... | collective-permute-start | bytes 110600 | tf_op jit(solution)/shard_map/ppermute | solution.py:848
  44.6 1.3 %copy-start.2 = (s32[2048,4]{0,1:T(4,128)S(1)}, s32[2048,4]{0,1:T(4,128)}, u32[]{:S(2)}) copy-start(s32[2048,4]{0,1:T(4,128)} %param.16) | copy-start | bytes 98308
  44.6 1.3 %collective-permute-start.7 = (f32[72,128]{1,0:T(8,128)S(1)}, f32[72,128]{1,0:T(8,128)S(1)}, u32[]{:S(2)}, u32[]{:S(2)}) collective-permute-start(f32[72,128]{1,0:T(8,128)S(1)} %add_add_fusion.2.own_ref), channel_id=1, source_target_pairs={{0,16},{16,0},{1,17},{17,1},{2,18},{18,2},{3,19},{19,3},{4,20},{20... | collective-permute-start | bytes 110600 | tf_op jit(solution)/shard_map/ppermute | solution.py:866
  53.6 1.3 %collective-permute-start.8 = (f32[72,128]{1,0:T(8,128)S(1)}, f32[72,128]{1,0:T(8,128)S(1)}, u32[]{:S(2)}, u32[]{:S(2)}) collective-permute-start(f32[72,128]{1,0:T(8,128)S(1)} %get-tuple-element.130), channel_id=1, source_target_pairs={{0,16},{16,0},{1,17},{17,1},{2,18},{18,2},{3,19},{19,3},{4,20},{20... | collective-permute-start | bytes 110600 | tf_op jit(solution)/shard_map/ppermute | solution.py:866
  54.9 6.1 %collective-permute-start.11 = (f32[72,128]{1,0:T(8,128)S(1)}, f32[72,128]{1,0:T(8,128)S(1)}, u32[]{:S(2)}, u32[]{:S(2)}) collective-permute-start(f32[72,128]{1,0:T(8,128)S(1)} %add.86), channel_id=1, source_target_pairs={{0,12},{1,13},{2,14},{3,15},{4,8},{5,9},{6,10},{7,11},{8,4},{9,5},... | collective-permute-start | bytes 110600 | tf_op jit(solution)/shard_map/ppermute | solution.py:848
  58.6 4.9 %collective-permute-start.10 = (f32[72,128]{1,0:T(8,128)S(1)}, f32[72,128]{1,0:T(8,128)S(1)}, u32[]{:S(2)}, u32[]{:S(2)}) collective-permute-start(f32[72,128]{1,0:T(8,128)S(1)} %add.86), channel_id=1, source_target_pairs={{0,8},{1,9},{2,10},{3,11},{4,12},{5,13},{6,14},{7,15},{8,0},{9,1},... | collective-permute-start | bytes 110600 | tf_op jit(solution)/shard_map/ppermute | solution.py:848
  58.6 4.9 %collective-permute-start.9 = (f32[72,128]{1,0:T(8,128)S(1)}, f32[72,128]{1,0:T(8,128)S(1)}, u32[]{:S(2)}, u32[]{:S(2)}) collective-permute-start(f32[72,128]{1,0:T(8,128)S(1)} %add.86), channel_id=1, source_target_pairs={{0,4},{1,5},{2,6},{3,7},{4,0},{5,1},{6,2},{7,3},{8,12},{9,13},{10,... | collective-permute-start | bytes 110600 | tf_op jit(solution)/shard_map/ppermute | solution.py:848
  63.5 2.1 %collective-permute-start.15 = (bf16[16,80,128]{2,1,0:T(8,128)(2,1)S(1)}, bf16[16,80,128]{2,1,0:T(8,128)(2,1)S(1)}, u32[]{:S(2)}, u32[]{:S(2)}) collective-permute-start(bf16[16,80,128]{2,1,0:T(8,128)(2,1)S(1)} %get-tuple-element.148), channel_id=1, source_target_pairs={{0,16},{16,0},{1,17},{17,1},{2,18},{18,2},{3,19},{19,3},{4,20},{20... | collective-permute-start | bytes 983048 | tf_op jit(solution)/shard_map/ppermute | solution.py:866
  63.5 5.8 %collective-permute-start.17 = (f32[1024,128]{1,0:T(8,128)S(1)}, f32[1024,128]{1,0:T(8,128)S(1)}, u32[]{:S(2)}, u32[]{:S(2)}) collective-permute-start(f32[1024,128]{1,0:T(8,128)S(1)} %get-tuple-element.164), channel_id=1, source_target_pairs={{0,16},{16,0},{1,17},{17,1},{2,18},{18,2},{3,19},{19,3},{4,20},{20... | collective-permute-start | bytes 1572872 | tf_op jit(solution)/shard_map/ppermute | solution.py:866
  64.0 5.3 %collective-permute-start.16 = (bf16[1024,128]{1,0:T(8,128)(2,1)S(1)}, bf16[1024,128]{1,0:T(8,128)(2,1)S(1)}, u32[]{:S(2)}, u32[]{:S(2)}) collective-permute-start(bf16[1024,128]{1,0:T(8,128)(2,1)S(1)} %get-tuple-element.162), channel_id=1, source_target_pairs={{0,16},{16,0},{1,17},{17,1},{2,18},{18,2},{3,19},{19,3},{4,20},{20... | collective-permute-start | bytes 786440 | tf_op jit(solution)/shard_map/ppermute | solution.py:866
  64.0 5.2 %collective-permute-start.14 = (f32[72,128]{1,0:T(8,128)S(1)}, f32[72,128]{1,0:T(8,128)S(1)}, u32[]{:S(2)}, u32[]{:S(2)}) collective-permute-start(f32[72,128]{1,0:T(8,128)S(1)} %add_add_fusion.1), channel_id=1, source_target_pairs={{0,3},{1,2},{2,1},{3,0},{4,7},{5,6},{6,5},{7,4},{8,11},{9,10},{10,... | collective-permute-start | bytes 110600 | tf_op jit(solution)/shard_map/ppermute | solution.py:848
  64.4 8.4 %collective-permute-start.13 = (f32[72,128]{1,0:T(8,128)S(1)}, f32[72,128]{1,0:T(8,128)S(1)}, u32[]{:S(2)}, u32[]{:S(2)}) collective-permute-start(f32[72,128]{1,0:T(8,128)S(1)} %add_add_fusion.1), channel_id=1, source_target_pairs={{0,2},{1,3},{2,0},{3,1},{4,6},{5,7},{6,4},{7,5},{8,10},{9,11},{10,... | collective-permute-start | bytes 110600 | tf_op jit(solution)/shard_map/ppermute | solution.py:848
  65.6 7.2 %collective-permute-start.12 = (f32[72,128]{1,0:T(8,128)S(1)}, f32[72,128]{1,0:T(8,128)S(1)}, u32[]{:S(2)}, u32[]{:S(2)}) collective-permute-start(f32[72,128]{1,0:T(8,128)S(1)} %add_add_fusion.1), channel_id=1, source_target_pairs={{0,1},{1,0},{2,3},{3,2},{4,5},{5,4},{6,7},{7,6},{8,9},{9,8},{10,11... | collective-permute-start | bytes 110600 | tf_op jit(solution)/shard_map/ppermute | solution.py:848
  69.2 14.4 %all-to-all-start.2 = ((bf16[16,80,128]{2,1,0:T(8,128)(2,1)}), bf16[16,80,128]{2,1,0:T(8,128)(2,1)S(1)}, u32[]{:S(2)}, u32[]{:S(2)}) async-start(bf16[16,80,128]{2,1,0:T(8,128)(2,1)} %add_convert_fusion), calls=%async_computation.2 | async-start | bytes 655360 | tf_op jit(solution)/shard_map/all_to_all | solution.py:1200
  83.6 12.4 %all-to-all-start.3 = ((bf16[16,32,128]{2,1,0:T(8,128)(2,1)}), bf16[16,32,128]{2,1,0:T(8,128)(2,1)S(1)}, u32[]{:S(2)}, u32[]{:S(2)}) async-start(bf16[16,32,128]{2,1,0:T(8,128)(2,1)} %sample_backward.1), calls=%async_computation.3 | async-start | bytes 262144 | tf_op jit(solution)/shard_map/all_to_all | solution.py:1283
  88.3 2.1 %collective-permute-start.18 = (f32[10240]{0:T(1024)S(1)}, f32[10240]{0:T(1024)S(1)}, u32[]{:S(2)}, u32[]{:S(2)}) collective-permute-start(f32[10240]{0:T(1024)S(1)} %bitcast.10), channel_id=1, source_target_pairs={{0,16},{16,0},{1,17},{17,1},{2,18},{18,2},{3,19},{19,3},{4,20},{20... | collective-permute-start | bytes 122888 | tf_op jit(solution)/shard_map/ppermute | solution.py:866
  89.5 0.9 copy-start.4
  89.5 0.9 copy-start.5
  91.2 4.9 %copy-start.6 = (f32[1,3112]{1,0:T(1,128)S(1)}, f32[1,3112]{1,0:T(1,128)}, u32[]{:S(2)}) copy-start(f32[1,3112]{1,0:T(1,128)} %param.21) | copy-start | bytes 37348
  91.2 4.9 %copy-start.8 = (f32[1,3112]{1,0:T(1,128)S(1)}, f32[1,3112]{1,0:T(1,128)}, u32[]{:S(2)}) copy-start(f32[1,3112]{1,0:T(1,128)} %param.22) | copy-start | bytes 37348
  91.2 4.9 %copy-start.9 = (f32[1,3112]{1,0:T(1,128)S(1)}, f32[1,3112]{1,0:T(1,128)}, u32[]{:S(2)}) copy-start(f32[1,3112]{1,0:T(1,128)} %param.23) | copy-start | bytes 37348
